TPU v7x, 32 devices: a whole 2x2x4 slice. The times are simulated.
32 devices in a mesh: dop: 8 (over z, y), rng: 4 (over x, core).
Axes of the slice: x: 2, y: 2, z: 4, core: 2. Of those that a mesh axis runs over, the one named last changes fastest.
Arguments:
- raw_echo: float32 [2, 512, 512, 128], P(None, 'dop', 'rng'), may hold values from -6 to 6
- replica: float32 [2, 64], replicated, may hold values from -0.5 to 0.5
- beam_weights: bfloat16 [2, 512, 192], replicated, may hold values from -0.1875 to 0.1875
- pivots: int32 [128, 192], replicated, may hold values from 0 to 191, each once within a row
- owner_counts: int32 [8], replicated, may hold values from 1 to 32, 128 in all
- train_gates: int32 [128, 256], P(None, 'rng'), may hold values from 0 to 511, as said below
Outputs:
- factor: float32 [256, 384, 384], P('dop', 'rng')
Inputs may be any that keep to these rules, and one draw needn't show every extreme that they name: Owner o holds the run of owner_counts[o] consecutive Doppler bins that follows the bins of the owners below it; the counts sum to 128, and the largest is exactly 32 in every draw. `pivots`: each row is a permutation of 0 to 191. `train_gates`: in each row, columns r * 64 to (r + 1) * 64 - 1 hold distinct gates of range block r, that is of r * 128 to (r + 1) * 128 - 1.
All inputs are finite; a program needn't handle non-finite values.
Results may differ from a plain program's by a relative error of at most 0.005.
Values may be sent and summed in bfloat16 or wider, within the bound.
No kernel may reach another device: no remote copies, remote signals or barrier semaphores. Data moves between devices by JAX's collectives and lax.ppermute only.
A program may use at most 128 MiB of HBM per device.

v0:
```python
import math

import jax
import jax.numpy as jnp
from jax import lax
from jax.sharding import PartitionSpec as P

LOADING = 0.25


def shifted(array, axis, by):
    count = lax.axis_size(axis)
    pairs = [(i, i + by) for i in range(count) if 0 <= i + by < count]
    return lax.ppermute(array, axis, pairs)


def complex_block(real_part, imag_part):
    upper_row = jnp.stack([real_part, imag_part])
    lower_row = jnp.stack([-imag_part, real_part])
    return jnp.stack([upper_row, lower_row])


def doppler_table(pulse_count):
    pulse_index = jnp.arange(pulse_count, dtype=jnp.int32)
    phase_index = pulse_index[:, None] * pulse_index[None, :] % pulse_count
    angle_table = phase_index.astype(jnp.float32) * (2.0 * math.pi / pulse_count)
    norm_scale = 1.0 / math.sqrt(pulse_count)
    return complex_block(jnp.cos(angle_table) * norm_scale, jnp.sin(angle_table) * norm_scale)


def filter_rows(replica, block_rows):
    tap_count = replica.shape[1]
    span_rows = block_rows + tap_count - 1
    offsets = (
        jnp.arange(span_rows, dtype=jnp.int32)[None, :]
        - jnp.arange(block_rows, dtype=jnp.int32)[:, None]
    )
    matches = offsets[:, :, None] == jnp.arange(tap_count, dtype=jnp.int32)[None, None, :]
    picked = jnp.sum(jnp.where(matches[None], replica[:, None, None, :], 0.0), axis=3)
    return complex_block(picked[0], picked[1])


def factor_matrix(real_part, imag_part, pivot_row, count_rows):
    real_part = real_part / count_rows
    imag_part = imag_part / count_rows
    real_pivot = jnp.take(jnp.take(real_part, pivot_row, axis=0), pivot_row, axis=1)
    imag_pivot = jnp.take(jnp.take(imag_part, pivot_row, axis=0), pivot_row, axis=1)
    upper_half = jnp.concatenate([real_pivot, -imag_pivot], axis=1)
    lower_half = jnp.concatenate([imag_pivot, real_pivot], axis=1)
    matrix = jnp.concatenate([upper_half, lower_half], axis=0)
    matrix = matrix + LOADING * jnp.eye(matrix.shape[0], dtype=matrix.dtype)
    return jnp.linalg.cholesky(matrix).T


def form_beams(arrived, weights):
    incoming = arrived[0]
    beam_data = jnp.einsum("abcd,mbck->madk", weights, incoming, preferred_element_type=jnp.float32)
    return beam_data.astype(jnp.bfloat16).reshape(incoming.shape[0], -1, incoming.shape[3])


def gram_pieces(beam_data):
    half_rows = beam_data.shape[1] // 2
    product = jnp.einsum("mik,mjk->mij", beam_data, beam_data, preferred_element_type=jnp.float32)
    real_part = product[:, :half_rows, :half_rows] + product[:, half_rows:, half_rows:]
    imag_part = product[:, half_rows:, :half_rows] - product[:, :half_rows, half_rows:]
    return jnp.stack([real_part, imag_part], axis=1)


def factor_slots(pieces, pivot_rows, filled, count_rows):
    factors = jax.vmap(factor_matrix, in_axes=(0, 0, 0, None))(
        pieces[:, 0], pieces[:, 1], pivot_rows, count_rows
    )
    return jnp.where(filled[:, None, None], factors, 0.0)


def local(raw_echo, replica, beam_weights, pivots, owner_counts, train_gates):
    ch_local = raw_echo.shape[1]
    gate_rows = raw_echo.shape[2]
    pulse_count = raw_echo.shape[3]
    tap_count = replica.shape[1]
    owners = lax.axis_size("dop")
    most_slots = 2 * (pulse_count // owners)
    rim_rows = raw_echo[:, :, : tap_count - 1, :]
    next_rows = shifted(rim_rows.astype(jnp.bfloat16), "rng", -1).astype(rim_rows.dtype)
    extended = jnp.concatenate([raw_echo, next_rows], axis=2)
    block_rows = math.gcd(128, gate_rows)
    windows = jnp.stack([extended], axis=2)
    matched = jnp.einsum(
        "abji,bcnip->acnjp",
        filter_rows(replica, block_rows),
        windows,
        precision=lax.Precision.HIGHEST,
    )
    matched = matched.reshape(2, ch_local, gate_rows, pulse_count)
    spectrum = jnp.einsum(
        "abpk,bcgp->kacg", doppler_table(pulse_count), matched, precision=lax.Precision.HIGHEST
    ).astype(jnp.bfloat16)
    starts = jnp.cumsum(owner_counts, dtype=jnp.int32) - owner_counts
    slot_index = jnp.arange(most_slots, dtype=jnp.int32)
    local_gates = train_gates % gate_rows
    weights = complex_block(beam_weights[0], beam_weights[1])
    owner_hot = jnp.arange(owners, dtype=jnp.int32) == lax.axis_index("dop")
    my_start = jnp.sum(jnp.where(owner_hot, starts, 0), dtype=jnp.int32)
    my_count = jnp.sum(jnp.where(owner_hot, owner_counts, 0), dtype=jnp.int32)
    my_bins = jnp.minimum(my_start + slot_index, pulse_count - 1)
    my_full = slot_index < my_count
    my_pivots = jnp.take(pivots, my_bins, axis=0)
    count_rows = float(train_gates.shape[1] * lax.axis_size("rng"))
    slot_bins = jnp.minimum(starts[:, None] + slot_index[None, :], pulse_count - 1).reshape(-1)
    slot_full = (slot_index[None, :] < owner_counts[:, None]).reshape(-1)
    outgoing = jnp.where(
        slot_full[:, None, None, None],
        jnp.take(spectrum, slot_bins, axis=0),
        jnp.zeros((), jnp.bfloat16),
    )
    arrived = lax.all_to_all(
        outgoing.reshape(owners, most_slots, 2, ch_local, gate_rows),
        "dop",
        split_axis=0,
        concat_axis=3,
        tiled=True,
    )
    chosen = jnp.take(local_gates, my_bins, axis=0)
    picked = jnp.take_along_axis(arrived, chosen[None, :, None, None, :], axis=4)
    beam_data = form_beams(picked, weights)
    share_slots = most_slots // lax.axis_size("rng")
    lead_slot = lax.axis_index("rng") * share_slots
    mine = lax.psum_scatter(gram_pieces(beam_data), "rng", scatter_dimension=0, tiled=True)
    rows_done = factor_slots(
        mine,
        lax.dynamic_slice_in_dim(my_pivots, lead_slot, share_slots, 0),
        lax.dynamic_slice_in_dim(my_full, lead_slot, share_slots, 0),
        count_rows,
    )
    result = lax.all_to_all(rows_done, "rng", split_axis=1, concat_axis=0, tiled=True)
    return result


def solution(mesh):
    return jax.shard_map(
        local,
        mesh=mesh,
        in_specs=(P(None, "dop", "rng", None), P(), P(), P(), P(), P(None, "rng")),
        out_specs=P("dop", "rng", None),
        check_vma=False,
    )
```

profile of v0, /device:TPU:1, one launch (start us, length us, event | category | flops | bytes accessed | tf_op | source)
XLA Modules:
  0.0 1099.3 jit_solution(3344769109665122786)
XLA Ops:
  6.5 2.7 slice.120
  9.3 2.7 copy.160
  16.4 2.7 select_reduce_fusion
  19.2 20.8 %collective-permute-done = bf16[2,64,63,128]{3,1,2,0:T(8,128)(2,1)S(1)} collective-permute-done((bf16[2,64,63,128]{3,1,2,0:T(8,128)(2,1)}, bf16[2,64,63,128]{3,1,2,0:T(8,128)(2,1)S(1)}, u32[]{:S(2)}, u32[]{:S(2)}) %collective-permute-start) | collective-permute-done | bytes 2064416 | tf_op jit(solution)/shard_map/ppermute | solution.py:14
  41.2 24.0 %fusion = f32[64,128,2,128,1]{3,1,4,2,0:T(8,128)S(1)} fusion(f32[2,64,63,128]{3,2,0,1:T(8,128)S(1)} %copy.119, f32[1,2,128,191]{2,3,1,0:T(8,128)S(1)} %maximum_bitcast_fusion.9, f32[1,2,128,191]{2,3,1,0:T(8,128)S(1)} %bitcast.157, f32[2,64,128,128]{3,2,1,0:T(8,128)} %param.10), kind=kOutput, calls=%fused_computation.9 | convolution fusion | flops 9616572416 | bytes 21297152 | tf_op jit(solution)/shard_map/abji,bcnip->acnjp/dot_general | solution.py:88
  65.2 15.8 %fusion.8 = bf16[128,2,64,128]{0,3,1,2:T(8,128)(2,1)} fusion(f32[64,128,2,128,1]{3,1,4,2,0:T(8,128)S(1)} %fusion, f32[1,2,128,128]{3,2,1,0:T(8,128)S(1)} %get-tuple-element.26, f32[1,2,128,128]{3,2,1,0:T(8,128)S(1)} %get-tuple-element.25), kind=kOutput, calls=%fused_computation.27 | convolution fusion | flops 6444613632 | bytes 12845056 | tf_op jit(solution)/shard_map/abpk,bcgp->kacg/dot_general | solution.py:95
  81.1 6.5 copy.121
  87.6 10.8 gather_fusion.1
  98.4 7.4 select_select_fusion
  105.8 5.7 all-to-all-start
  114.4 161.8 %all-to-all-done = bf16[8,32,2,64,128]{4,3,2,1,0:T(8,128)(2,1)} async-done(((bf16[8,32,2,64,128]{4,3,2,1,0:T(8,128)(2,1)}), bf16[8,32,2,64,128]{4,3,2,1,0:T(8,128)(2,1)}, u32[]{:S(2)}, u32[]{:S(2)}) %all-to-all-start) | async-done | bytes 8388640 | tf_op jit(solution)/shard_map/all_to_all | solution.py:116
  276.2 9.6 copy.122
  285.8 21.4 %copy.123 = bf16[32,2,512,128]{2,1,3,0:T(2,128)(2,1)} copy(bf16[32,2,512,128]{3,2,1,0:T(8,128)(2,1)} %bitcast.150) | data formatting | bytes 16777216 | tf_op jit(solution)/shard_map/all_to_all | solution.py:116
  307.2 27.0 %gather_fusion.3 = bf16[2048,2,512]{2,1,0:T(2,128)(2,1)} fusion(bf16[32,2,512,128]{2,1,3,0:T(2,128)(2,1)} %copy.123, s32[2048]{0:T(1024)S(1)} %reshape.389), kind=kCustom, calls=%fused_computation.7 | custom fusion | bytes 8404992 | tf_op jit(solution)/shard_map/jit(take_along_axis)/gather | solution.py:124
  334.3 2.9 copy.124
  337.1 2.6 fusion.13
  339.8 2.2 copy.126
  343.9 4.6 fusion.52
  348.5 6.3 fusion.6
  354.8 10.7 pad_maximum_fusion
  365.6 10.5 copy.150
  376.1 11.0 reshape.446
  389.9 74.3 %reduce-scatter.4.cloned.1.call-done = f32[8,73728]{1,0:T(8,128)} async-done(((f32[32,73728]{1,0:T(8,128)}), f32[8,73728]{1,0:T(8,128)}) %reduce-scatter.4.cloned.1.call-update) | async-done | bytes 2359312
  464.3 4.8 reshape.447
  469.0 2.2 fusion.17
  471.3 18.0 %gather_fusion.6 = f32[1536,192]{1,0:T(8,128)} fusion(f32[8,192,192]{2,1,0:T(8,128)S(1)} %get-tuple-element.16, s32[1536]{0:T(1024)S(1)} %reshape.418), kind=kCustom, calls=%fused_computation.2.clone | custom fusion | bytes 2371584 | tf_op jit(solution)/shard_map/vmap(jit(_take))/gather | solution.py:47
  489.3 3.1 copy.128
  494.0 18.0 %gather_fusion.7 = f32[1536,192]{1,0:T(8,128)} fusion(f32[8,192,192]{1,2,0:T(8,128)S(1)} %broadcast_select_fusion, s32[1536]{0:T(1024)S(1)} %reshape.418), kind=kCustom, calls=%fused_computation.3.clone | custom fusion | bytes 2371584 | tf_op jit(solution)/shard_map/vmap(jit(_take))/gather | solution.py:47
  512.0 10.7 gather_fusion.4
  524.5 3.5 fusion.51
  527.9 18.0 %gather_fusion.5 = f32[1536,192]{1,0:T(8,128)} fusion(f32[8,192,192]{1,2,0:T(8,128)S(1)} %get-tuple-element.27, s32[1536]{0:T(1024)S(1)} %reshape.418), kind=kCustom, calls=%fused_computation.1.clone | custom fusion | bytes 2371584 | tf_op jit(solution)/shard_map/vmap(jit(_take))/gather | solution.py:46
  548.8 4.3 maximum_add_fusion
  553.1 6.2 copy.129
  559.2 4.8 fusion.7
  564.0 2.1 copy-done.2
  566.2 94.0 %custom-call.22 = f32[8,128,128]{2,1,0:T(8,128)S(1)} custom-call(f32[8,128,128]{2,1,0:T(8,128)S(1)} %cholesky.198), custom_call_target="Cholesky" | custom-call | tf_op jit(solution)/shard_map/vmap(jit(cholesky))/cholesky | solution.py:52
  660.2 2.6 cholesky.176
  662.8 78.6 %custom-call.23 = f32[8,1,128,128]{2,3,1,0:T(8,128)S(1)} custom-call(f32[8,1,128,128]{3,2,1,0:T(8,128)S(1)} %select_bitcast_fusion.5), custom_call_target="InvertDiagBlocksLowerTriangular" | custom-call | tf_op jit(solution)/shard_map/vmap(jit(cholesky))/cholesky | solution.py:52
  741.4 3.3 constant_dynamic-update-slice_fusion.2
  744.7 2.3 convolution_subtract_fusion
  747.0 94.0 %custom-call.24 = f32[8,128,128]{2,1,0:T(8,128)S(1)} custom-call(f32[8,128,128]{2,1,0:T(8,128)S(1)} %cholesky.202), custom_call_target="Cholesky" | custom-call | tf_op jit(solution)/shard_map/vmap(jit(cholesky))/cholesky | solution.py:52
  842.0 78.6 %custom-call.25 = f32[8,1,128,128]{2,3,1,0:T(8,128)S(1)} custom-call(f32[8,1,128,128]{3,2,1,0:T(8,128)S(1)} %get-tuple-element.19), custom_call_target="InvertDiagBlocksLowerTriangular" | custom-call | tf_op jit(solution)/shard_map/vmap(jit(cholesky))/cholesky | solution.py:52
  922.0 3.0 convolution_subtract_fusion.1
  925.1 94.1 %custom-call.26 = f32[8,128,128]{2,1,0:T(8,128)S(1)} custom-call(f32[8,128,128]{2,1,0:T(8,128)S(1)} %convolution_subtract_fusion.1), custom_call_target="Cholesky" | custom-call | tf_op jit(solution)/shard_map/vmap(jit(cholesky))/cholesky | solution.py:52
  1020.4 5.2 select_bitcast_fusion
  1025.6 6.1 copy.134
  1031.7 57.2 %all_to_all.36 = f32[8,384,384]{2,0,1:T(8,128)S(1)} all-to-all(f32[8,384,384]{2,0,1:T(8,128)} %copy.134), channel_id=1, replica_groups=mesh['dop'=8,'rng'=4] {'rng'}, dimensions={1} | all-to-all | bytes 9437184 | tf_op jit(solution)/shard_map/all_to_all | solution.py:135
  1089.0 3.0 copy.136
  (69 shorter events, 23.3 us)
Async XLA Ops:
  6.5 7.4 copy-start.6
  6.5 9.8 copy-start.7
  11.9 28.1 %collective-permute-start = (bf16[2,64,63,128]{3,1,2,0:T(8,128)(2,1)}, bf16[2,64,63,128]{3,1,2,0:T(8,128)(2,1)S(1)}, u32[]{:S(2)}, u32[]{:S(2)}) collective-permute-start(bf16[2,64,63,128]{3,1,2,0:T(8,128)(2,1)} %copy.160), channel_id=1, source_target_pairs={{1,0},{2,1},{3,2},{5,4},{6,5},{7,6},{9,8},{10,9},{11,10},{13,12},{... | collective-permute-start | bytes 6193160 | tf_op jit(solution)/shard_map/ppermute | solution.py:14
  105.8 5.7 copy-start.5
  105.8 8.5 copy-start.3
  105.8 170.4 %all-to-all-start = ((bf16[8,32,2,64,128]{4,3,2,1,0:T(8,128)(2,1)}), bf16[8,32,2,64,128]{4,3,2,1,0:T(8,128)(2,1)}, u32[]{:S(2)}, u32[]{:S(2)}) async-start(bf16[8,32,2,64,128]{4,3,2,1,0:T(8,128)(2,1)} %select_select_fusion), calls=%async_computation | async-start | bytes 16777216 | tf_op jit(solution)/shard_map/all_to_all | solution.py:116
  111.5 352.8 %reduce-scatter.4.cloned.1.call-start = ((), (), s32[]{:S(2)}) async-start(), calls=%async_computation.3 | async-start | bytes 11796480
  387.1 0.9 copy-start.4
  547.6 1.2 copy-start.1
  553.1 6.2 copy-start
  564.0 2.1 copy-start.2
Sparse Core Ops, SparseCore 0:
  387.2 77.0 reduce-scatter.3
where the time goes:
time: 1110 us; the launch traced here: 1100 us
  other arithmetic  497 us (45%)
  waiting for transfers between devices  257 us (23%)
  local copies, waits for them, and re-layouts  209 us (19%)
  matrix products  57.2 us (5%)
  blocking collectives  57.2 us (5%)
  between operations  14.3 us (1%)
    another operation x14, other arithmetic, factor_matrix(): return jnp.linalg.cholesky(matrix).T  442 us
    all_to_all x1, waiting for transfers between devices, local(): lax.all_to_all(outgoing.reshape(owners, most_slots, 2, ch_local, gate_row...  162 us
    unnamed x2, waiting for transfers between devices  74.4 us
    all_to_all x1, blocking collectives, local(): lax.all_to_all(rows_done, 'rng', split_axis=1, concat_axis=0, tiled=True)  57.2 us
    unnamed x22, local copies, waits for them, and re-layouts  33.2 us
    all_to_all x2, local copies, waits for them, and re-layouts, local(): lax.all_to_all(outgoing.reshape(owners, most_slots, 2, ch_local, gate_row...  31 us
    gather x3, local copies, waits for them, and re-layouts, local(): jnp.take_along_axis(arrived, chosen[None, :, None, None, :], axis=4)  29.9 us
    dot_general x1, matrix products, local(): jnp.einsum('abji,bcnip->acnjp', filter_rows(replica, block_rows), windows...  24 us
  transfers between devices with their start and end apart: 3, of which 3 were waited for; matrix products, arithmetic and copies ran while one was open for 1% of the time, Pallas kernels for 0%

commit v1 on v0

v1 whole, which is shorter than its diff:
```python
import functools
import math

import jax
import jax.numpy as jnp
from jax import lax
from jax.experimental import pallas as pl
from jax.experimental.pallas import tpu as pltpu
from jax.sharding import PartitionSpec as P

LOADING = 0.25
LANES = 128
PANEL = 16
BF16 = jnp.bfloat16
F32 = jnp.float32
PARAMS = pltpu.CompilerParams(vmem_limit_bytes=48 * 1024 * 1024)


def shifted(array, axis, by):
    count = lax.axis_size(axis)
    pairs = [(i, i + by) for i in range(count) if 0 <= i + by < count]
    return lax.ppermute(array, axis, pairs)


def complex_block(real_part, imag_part):
    upper_row = jnp.stack([real_part, imag_part])
    lower_row = jnp.stack([-imag_part, real_part])
    return jnp.stack([upper_row, lower_row])


def doppler_table(pulse_count):
    pulse_index = jnp.arange(pulse_count, dtype=jnp.int32)
    phase_index = pulse_index[:, None] * pulse_index[None, :] % pulse_count
    angle_table = phase_index.astype(jnp.float32) * (2.0 * math.pi / pulse_count)
    norm_scale = 1.0 / math.sqrt(pulse_count)
    return complex_block(jnp.cos(angle_table) * norm_scale, jnp.sin(angle_table) * norm_scale)


def filter_rows(replica, block_rows):
    tap_count = replica.shape[1]
    span_rows = block_rows + tap_count - 1
    offsets = (
        jnp.arange(span_rows, dtype=jnp.int32)[None, :]
        - jnp.arange(block_rows, dtype=jnp.int32)[:, None]
    )
    matches = offsets[:, :, None] == jnp.arange(tap_count, dtype=jnp.int32)[None, None, :]
    picked = jnp.sum(jnp.where(matches[None], replica[:, None, None, :], 0.0), axis=3)
    return complex_block(picked[0], picked[1])


def select_kernel(bins_ref, gates_ref, spectrum_ref, out_ref, *, pack, groups):
    owner = pl.program_id(0)
    gate_rows = spectrum_ref.shape[2]
    width = out_ref.shape[3]
    gate_index = lax.broadcasted_iota(jnp.int32, (gate_rows, width), 0)
    part_index = lax.broadcasted_iota(jnp.int32, (gate_rows, width), 1) // (width // pack)

    def one_group(group, carry):
        hit = gate_index == gates_ref[0, pl.ds(group, 1), :]
        total = jnp.zeros(out_ref.shape[2:], F32)
        for part in range(pack):
            bin_index = bins_ref[(owner * groups + group) * pack + part]
            chooser = jnp.where(hit & (part_index == part), 1.0, 0.0).astype(BF16)
            total += jnp.dot(spectrum_ref[bin_index], chooser, preferred_element_type=F32)
        out_ref[0, group] = total.astype(BF16)
        return carry

    lax.fori_loop(0, groups, one_group, 0)


def select_gates(spectrum, slot_bins, slot_gates, owners, pack):
    bins, rows, gate_rows = spectrum.shape
    groups = slot_bins.shape[0] // owners // pack
    width = slot_gates.shape[-1]
    return pl.pallas_call(
        functools.partial(select_kernel, pack=pack, groups=groups),
        out_shape=jax.ShapeDtypeStruct((owners, groups, rows, width), BF16),
        grid_spec=pltpu.PrefetchScalarGridSpec(
            num_scalar_prefetch=1,
            grid=(owners,),
            in_specs=[
                pl.BlockSpec((1, groups, width), lambda i, b: (i, 0, 0)),
                pl.BlockSpec((bins, rows, gate_rows), lambda i, b: (0, 0, 0)),
            ],
            out_specs=pl.BlockSpec((1, groups, rows, width), lambda i, b: (i, 0, 0, 0)),
        ),
        compiler_params=PARAMS,
        name="select_gates",
    )(slot_bins, slot_gates.reshape(owners, groups, width), spectrum)


def beam_kernel(weights_ref, arrived_ref, out_ref):
    sources, groups, rows, width = arrived_ref.shape
    packed = jnp.concatenate(
        [arrived_ref[:, g].reshape(sources * rows, width) for g in range(groups)], axis=1
    )
    beams = jnp.dot(weights_ref[...], packed, preferred_element_type=F32).astype(BF16)
    for g in range(groups):
        out_ref[g] = beams[:, g * width : (g + 1) * width]


def form_beams(arrived, weights):
    sources, groups, rows, width = arrived.shape
    step = 2 if groups % 2 == 0 else 1
    return pl.pallas_call(
        beam_kernel,
        out_shape=jax.ShapeDtypeStruct((groups, weights.shape[0], width), BF16),
        grid=(groups // step,),
        in_specs=[
            pl.BlockSpec(weights.shape, lambda i: (0, 0)),
            pl.BlockSpec((sources, step, rows, width), lambda i: (0, i, 0, 0)),
        ],
        out_specs=pl.BlockSpec((step, weights.shape[0], width), lambda i: (i, 0, 0)),
        compiler_params=PARAMS,
        name="form_beams",
    )(weights, arrived)


def split_terms(array):
    high = array.astype(BF16)
    return high, (array - high.astype(F32)).astype(BF16)


def cross_product(left, right):
    left_high, left_low = split_terms(left)
    right_high, right_low = split_terms(right)
    return lax.dot_general(
        jnp.concatenate([left_high, left_high, left_low], axis=0),
        jnp.concatenate([right_high, right_low, right_high], axis=0),
        (((0,), (0,)), ((), ())),
        preferred_element_type=F32,
    )


def loaded_covariance(beams, pivot_row, part, pack, count_rows):
    dof = pivot_row.shape[1]
    hot = lax.broadcasted_iota(jnp.int32, (dof, dof), 0) == pivot_row
    hot = jnp.where(hot, 1.0, 0.0).astype(BF16)
    picked = []
    for half in range(2):
        rows = jnp.concatenate([b[half * dof : (half + 1) * dof] for b in beams], axis=1)
        moved = lax.dot_general(hot, rows, (((0,), (0,)), ((), ())), preferred_element_type=F32)
        picked.append(moved)
    real_part, imag_part = picked
    upper = jnp.concatenate([real_part, imag_part], axis=1)
    lower = jnp.concatenate([imag_part, -real_part], axis=1)
    stacked = jnp.concatenate([upper, lower], axis=0)
    width = beams[0].shape[1]
    lane = lax.broadcasted_iota(jnp.int32, stacked.shape, 1)
    kept = jnp.where((lane % width) // (width // pack) == part, stacked, 0.0).astype(BF16)
    gram = lax.dot_general(
        kept, stacked.astype(BF16), (((1,), (1,)), ((), ())), preferred_element_type=F32
    )
    order = 2 * dof
    row = lax.broadcasted_iota(jnp.int32, (order, order), 0)
    col = lax.broadcasted_iota(jnp.int32, (order, order), 1)
    return gram / count_rows + jnp.where(row == col, LOADING, 0.0)


def eliminate(tiles):
    sub = lax.broadcasted_iota(jnp.int32, (8, LANES), 0)
    diagonal = [jnp.ones((8, LANES), F32) for _ in tiles]
    for t in range(PANEL):
        home, place = divmod(t, 8)
        column = jnp.broadcast_to(tiles[home][0][:, t : t + 1], (8, LANES))
        diagonal[home] = jnp.where(sub == place, column, diagonal[home])
        inverse = pl.reciprocal(column, approx=True)
        inverse = inverse * (2.0 - column * inverse)
        inverse = inverse[place : place + 1]
        scaled = [piece[place : place + 1] * inverse for piece in tiles[home]]
        for i in range(home, PANEL // 8):
            if i == home and place == 7:
                continue
            if i == home:
                factor = jnp.where(sub > place, column, 0.0)
            else:
                factor = jnp.broadcast_to(tiles[i][0][:, t : t + 1], (8, LANES))
            tiles[i] = [piece - factor * s for piece, s in zip(tiles[i], scaled)]
    scales = [lax.rsqrt(d) for d in diagonal]
    return [[piece * s for piece in row] for row, s in zip(tiles, scales)]


def factor_kernel(pivots_ref, beams_ref, out_ref, work, *, pack, count_rows):
    ranges, groups = beams_ref.shape[:2]
    slots, order, _ = work.shape

    for slot in range(slots):
        group, part = divmod(slot, pack)
        work[slot] = loaded_covariance(
            [beams_ref[r, group] for r in range(ranges)],
            pivots_ref[slot : slot + 1, :],
            part,
            pack,
            count_rows,
        )

    lane = lax.broadcasted_iota(jnp.int32, (PANEL, LANES), 1)
    for start in range(0, order, LANES):
        chunks = (order - start) // LANES

        def one_panel(p, carry, start=start, chunks=chunks):
            base = pl.multiple_of(start + p * PANEL, PANEL)
            back = p * PANEL
            for slot in range(slots):
                tiles = []
                for i in range(PANEL // 8):
                    piece = work[slot, pl.ds(pl.multiple_of(base + 8 * i, 8), 8), start:]
                    row = [piece[:, w * LANES : (w + 1) * LANES] for w in range(chunks)]
                    row[0] = pltpu.roll(row[0], (LANES - back) % LANES, 1)
                    tiles.append(row)
                tiles = eliminate(tiles)
                for row in tiles:
                    row[0] = pltpu.roll(row[0], back, 1)
                rows = [
                    jnp.concatenate([tiles[i][w] for i in range(PANEL // 8)], axis=0)
                    for w in range(chunks)
                ]
                panel = jnp.concatenate(rows, axis=1)
                work[slot, pl.ds(base, PANEL), start:] = panel
                below = jnp.where(lane >= back + PANEL, rows[0], 0.0)
                work[slot, start : start + LANES, start:] -= cross_product(below, panel)
            return carry

        lax.fori_loop(0, LANES // PANEL, one_panel, 0)
        if chunks > 1:
            after = start + LANES
            for slot in range(slots):
                ready = work[slot, start:after, after:]
                work[slot, after:, after:] -= cross_product(ready, ready)

    owners, _, share, _ = out_ref.shape
    for slot in range(slots):
        for r in range(owners):
            row = lax.broadcasted_iota(jnp.int32, (share, order), 0) + r * share
            col = lax.broadcasted_iota(jnp.int32, (share, order), 1)
            piece = work[slot, r * share : (r + 1) * share]
            out_ref[r, slot] = jnp.where(col >= row, piece, 0.0).astype(out_ref.dtype)


def factor_slots(beams, pivot_rows, pack, count_rows):
    ranges = beams.shape[0]
    slots, dof = pivot_rows.shape
    order = 2 * dof
    return pl.pallas_call(
        functools.partial(factor_kernel, pack=pack, count_rows=count_rows),
        out_shape=jax.ShapeDtypeStruct((ranges, slots, order // ranges, order), BF16),
        in_specs=[
            pl.BlockSpec(memory_space=pltpu.VMEM),
            pl.BlockSpec(memory_space=pltpu.VMEM),
        ],
        out_specs=pl.BlockSpec(memory_space=pltpu.VMEM),
        scratch_shapes=[pltpu.VMEM((slots, order, order), F32)],
        compiler_params=PARAMS,
        name="factor_slots",
    )(pivot_rows, beams)


def local(raw_echo, replica, beam_weights, pivots, owner_counts, train_gates):
    ch_local = raw_echo.shape[1]
    gate_rows = raw_echo.shape[2]
    pulse_count = raw_echo.shape[3]
    tap_count = replica.shape[1]
    train_local = train_gates.shape[1]
    owners = lax.axis_size("dop")
    ranges = lax.axis_size("rng")
    most_slots = 2 * (pulse_count // owners)
    share_slots = most_slots // ranges
    pack = max(1, min(LANES // train_local, share_slots))

    echo = raw_echo.astype(BF16)
    next_rows = shifted(echo[:, :, : tap_count - 1, :], "rng", -1)
    extended = jnp.concatenate([echo, next_rows], axis=2)
    matched = jnp.einsum(
        "abji,bcip->acjp",
        filter_rows(replica, gate_rows).astype(BF16),
        extended,
        preferred_element_type=F32,
    ).astype(BF16)
    spectrum = jnp.einsum(
        "abpk,bcgp->kacg",
        doppler_table(pulse_count).astype(BF16),
        matched,
        preferred_element_type=F32,
    ).astype(BF16)
    spectrum = spectrum.reshape(pulse_count, 2 * ch_local, gate_rows)

    starts = jnp.cumsum(owner_counts, dtype=jnp.int32) - owner_counts
    slot_index = jnp.arange(most_slots, dtype=jnp.int32)
    slot_bins = jnp.minimum(starts[:, None] + slot_index[None, :], pulse_count - 1).reshape(-1)
    slot_gates = jnp.take(train_gates % gate_rows, slot_bins, axis=0)
    slot_gates = slot_gates.reshape(-1, pack * train_local)
    outgoing = select_gates(spectrum, slot_bins, slot_gates, owners, pack)
    arrived = lax.all_to_all(outgoing, "dop", split_axis=0, concat_axis=0, tiled=True)

    dof = beam_weights.shape[2]
    weights = complex_block(beam_weights[0], beam_weights[1])
    weights = weights.reshape(2, 2, owners, ch_local, dof).transpose(0, 4, 2, 1, 3)
    weights = weights.reshape(2 * dof, -1)
    beams = form_beams(arrived, weights)
    beams = beams.reshape(ranges, -1, 2 * dof, beams.shape[-1])
    beams = lax.all_to_all(beams, "rng", split_axis=0, concat_axis=0, tiled=True)

    me = lax.axis_index("dop")
    my_start = lax.dynamic_index_in_dim(starts, me, 0, keepdims=False)
    my_count = lax.dynamic_index_in_dim(owner_counts, me, 0, keepdims=False)
    lead = lax.axis_index("rng") * share_slots
    share_bins = my_start + lead + jnp.arange(share_slots, dtype=jnp.int32)
    my_pivots = jnp.take(pivots, jnp.minimum(share_bins, pulse_count - 1), axis=0)
    count_rows = float(train_local * ranges)
    factors = factor_slots(beams, my_pivots, pack, count_rows)
    rows_done = lax.all_to_all(factors, "rng", split_axis=0, concat_axis=0, tiled=True)
    rows_done = rows_done.reshape(most_slots, *rows_done.shape[2:])
    filled = slot_index < my_count
    return jnp.where(filled[:, None, None], rows_done.astype(F32), 0.0)


def solution(mesh):
    return jax.shard_map(
        local,
        mesh=mesh,
        in_specs=(P(None, "dop", "rng", None), P(), P(), P(), P(), P(None, "rng")),
        out_specs=P("dop", "rng", None),
        check_vma=False,
    )
```

time: 1110 us -> 558 us (0.50)
  other arithmetic: 497 us -> 8.53 us
  Pallas kernels: 0 us -> 361 us
  local copies, waits for them, and re-layouts: 209 us -> 24.3 us
  waiting for transfers between devices: 257 us -> 135 us
  blocking collectives: 57.2 us -> 0 us
  matrix products: 57.2 us -> 9.16 us
  between operations: 14.3 us -> 0.96 us
    another operation x17 -> x6, other arithmetic: 459 us -> 0.86 us  [the longest x14 442 us: factor_matrix(): return jnp.linalg.cholesky(matrix).T]
    pallas_call x0 -> x3, Pallas kernels: none -> 361 us  [the longest x1 331 us: factor_slots(): pl.pallas_call(functools.partial(factor_kernel, pack=pack, count_rows=cou...]
    gather x13 -> x3, local copies, waits for them, and re-layouts: 112 us -> 1.37 us  [the longest x2 0.81 us: local(): slot_gates = jnp.take(train_gates % gate_rows, slot_bins, axis=0)]
    unnamed x2 -> x0, waiting for transfers between devices: 74.4 us -> none
    all_to_all x1 -> x0, blocking collectives: 57.2 us -> none  [local(): lax.all_to_all(rows_done, 'rng', split_axis=1, concat_axis=0, tiled=True)]
    all_to_all x1 -> x3, waiting for transfers between devices: 162 us -> 115 us  [the longest x1 72.1 us: local(): lax.all_to_all(outgoing, 'dop', split_axis=0, concat_axis=0, tiled=True)]
    dot_general x4 -> x1, matrix products: 47.1 us -> 9.16 us  [local(): jnp.einsum('abpk,bcgp->kacg', doppler_table(pulse_count).astype(BF16), ma...]
    all_to_all x3 -> x0, local copies, waits for them, and re-layouts: 34 us -> none  [the longest x2 31 us: local(): lax.all_to_all(outgoing.reshape(owners, most_slots, 2, ch_local, gate_row...]
  transfers between devices with their start and end apart: 3 -> 4, of which waited for: 3 -> 4; matrix products, arithmetic and copies ran while one was open for 1% -> 2% of each run, Pallas kernels for 0% -> 0%
where the time goes in v1:
time: 558 us; the launch traced here: 556 us
  Pallas kernels  361 us (65%)
  waiting for transfers between devices  135 us (24%)
  local copies, waits for them, and re-layouts  24.3 us (4%)
  starting transfers between devices  16.8 us (3%)
  matrix products  9.16 us (2%)
  other arithmetic  8.53 us (2%)
    pallas_call x1, Pallas kernels, factor_slots(): pl.pallas_call(functools.partial(factor_kernel, pack=pack, count_rows=cou...  331 us
    all_to_all x1, waiting for transfers between devices, local(): lax.all_to_all(outgoing, 'dop', split_axis=0, concat_axis=0, tiled=True)  72.1 us
    all_to_all x1, waiting for transfers between devices, local(): lax.all_to_all(factors, 'rng', split_axis=0, concat_axis=0, tiled=True)  26.4 us
    pallas_call x1, Pallas kernels, select_gates(): pl.pallas_call(functools.partial(select_kernel, pack=pack, groups=groups)...  23.3 us
    ppermute x1, waiting for transfers between devices, shifted(): return lax.ppermute(array, axis, pairs)  19.6 us
    all_to_all x1, waiting for transfers between devices, local(): lax.all_to_all(beams, 'rng', split_axis=0, concat_axis=0, tiled=True)  16.9 us
  transfers between devices with their start and end apart: 4, of which 4 were waited for; matrix products, arithmetic and copies ran while one was open for 2% of the time, Pallas kernels for 0%

profile of v1, /device:TPU:1, one launch (start us, length us, event | category | flops | bytes accessed | tf_op | source)
XLA Modules:
  0.0 556.0 jit_solution(3830090894503188710)
XLA Ops:
  0.0 4.4 copy.76
  4.4 0.0 copy-start.1
  4.4 0.0 copy-start.6
  4.4 0.3 slice.29
  4.7 1.3 copy.62
  6.0 2.1 collective-permute-start
  8.2 0.2 reduce-window.9
  8.4 0.8 iota_compare_fusion
  9.2 2.7 select_reduce_fusion
  11.9 0.1 add_minimum_fusion
  12.0 0.1 min.48
  12.1 0.1 min.45.bins_ref
  12.2 0.1 copy.58
  12.4 0.7 gather_fusion.1
  13.1 0.1 gather.12
  13.2 0.1 fusion.26
  13.3 0.1 copy.57
  13.4 0.2 broadcast_in_dim.68
  13.6 0.1 broadcast_in_dim.69
  13.7 0.3 fusion.23
  14.0 0.3 negate_convert_fusion
  14.4 19.6 %collective-permute-done = bf16[2,64,63,128]{3,1,2,0:T(8,128)(2,1)} collective-permute-done((bf16[2,64,63,128]{3,1,2,0:T(8,128)(2,1)S(1)}, bf16[2,64,63,128]{3,1,2,0:T(8,128)(2,1)}, u32[]{:S(2)}, u32[]{:S(2)}) %collective-permute-start) | collective-permute-done | bytes 2064416 | tf_op jit(solution)/shard_map/ppermute | solution.py:22
  34.0 2.9 copy.63
  36.9 9.2 %fusion.6 = bf16[128,2,64,128]{0,3,1,2:T(8,128)(2,1)} fusion(bf16[2,64,63,128]{3,2,0,1:T(8,128)(2,1)S(1)} %copy.63, bf16[2,64,128,128]{3,2,0,1:T(8,128)(2,1)} %copy-done.1, bf16[1,2,128,191]{2,3,1,0:T(8,128)(2,1)S(1)} %maximum_bitcast_fusion.14, bf16[1,2,128,191]{2,3,1,0:T(8,128)(2,1)S(1)} %convert_bitcast_fusion, ...), kind=kOutput, calls=%fused_computation.14 | convolution fusion | flops 2693330944 | bytes 10779648 | tf_op jit(solution)/shard_map/abpk,bcgp->kacg/dot_general | solution.py:279
  46.1 6.4 %copy.65 = bf16[128,2,64,128]{3,2,1,0:T(8,128)(2,1)} copy(bf16[128,2,64,128]{0,3,1,2:T(8,128)(2,1)} %fusion.6) | data formatting | bytes 8388608 | tf_op jit(solution)/shard_map/convert_element_type | solution.py:284
  52.5 23.3 %select_gates.1 = bf16[8,16,128,128]{3,2,1,0:T(8,128)(2,1)S(1)} custom-call(s32[256]{0:T(256)S(1)} %min.45.bins_ref, s32[8,16,128]{2,1,0:T(8,128)S(1)} %broadcast_select_fusion.gates_ref, bf16[128,128,128]{2,1,0:T(8,128)(2,1)} %bitcast.67), custom_call_target="tpu_custom_call" | custom-call | tf_op jit(solution)/shard_map/select_gates/pallas_call | solution.py:75
  75.8 0.0 copy-start
  75.9 2.0 copy-done
  77.9 5.7 %all-to-all-start = ((bf16[8,16,128,128]{3,2,1,0:T(8,128)(2,1)}), bf16[8,16,128,128]{3,2,1,0:T(8,128)(2,1)}, u32[]{:S(2)}, u32[]{:S(2)}) async-start(bf16[8,16,128,128]{3,2,1,0:T(8,128)(2,1)} %copy-done), calls=%async_computation | async-start | bytes 8388608 | tf_op jit(solution)/shard_map/all_to_all | solution.py:293
  83.6 0.2 copy.53
  83.8 0.1 pad_maximum_fusion
  83.9 0.2 maximum_bitcast_fusion.8
  84.1 2.2 copy.71
  86.3 1.1 reshape.253.weights_ref
  87.5 72.1 %all-to-all-done.arrived_ref = bf16[8,16,128,128]{3,2,1,0:T(8,128)(2,1)} async-done(((bf16[8,16,128,128]{3,2,1,0:T(8,128)(2,1)}), bf16[8,16,128,128]{3,2,1,0:T(8,128)(2,1)}, u32[]{:S(2)}, u32[]{:S(2)}) %all-to-all-start) | async-done | bytes 4194336 | tf_op jit(solution)/shard_map/all_to_all | solution.py:293
  159.6 7.3 %form_beams.1 = bf16[16,384,128]{2,1,0:T(8,128)(2,1)} custom-call(bf16[384,1024]{1,0:T(8,128)(2,1)S(1)} %reshape.253.weights_ref, bf16[8,16,128,128]{3,2,1,0:T(8,128)(2,1)} %all-to-all-done.arrived_ref), custom_call_target="tpu_custom_call" | custom-call | tf_op jit(solution)/shard_map/form_beams/pallas_call | solution.py:105
  166.9 4.2 all-to-all-start.1
  171.0 0.6 dynamic_slice.8
  171.7 0.1 copy.52
  172.5 0.6 gather_fusion
  173.0 0.1 broadcast_select_fusion.1.pivots_ref
  173.1 16.9 %all-to-all-done.1.beams_ref = bf16[4,4,384,128]{3,2,1,0:T(8,128)(2,1)S(1)} async-done(((bf16[4,4,384,128]{3,2,1,0:T(8,128)(2,1)}), bf16[4,4,384,128]{3,2,1,0:T(8,128)(2,1)S(1)}, u32[]{:S(2)}, u32[]{:S(2)}) %all-to-all-start.1) | async-done | bytes 1572896 | tf_op jit(solution)/shard_map/all_to_all | solution.py:301
  190.0 330.7 %factor_slots.1 = bf16[4,8,96,384]{3,2,1,0:T(8,128)(2,1)} custom-call(s32[8,192]{1,0:T(8,128)S(1)} %broadcast_select_fusion.1.pivots_ref, bf16[4,4,384,128]{3,2,1,0:T(8,128)(2,1)S(1)} %all-to-all-done.1.beams_ref), custom_call_target="tpu_custom_call" | custom-call | tf_op jit(solution)/shard_map/factor_slots/pallas_call | solution.py:244
  520.7 4.8 all-to-all-start.2
  525.4 0.6 dynamic_slice.7
  526.1 0.6 iota_compare_fusion.1
  526.7 26.4 %all-to-all-done.2 = bf16[4,8,96,384]{3,2,1,0:T(8,128)(2,1)S(1)} async-done(((bf16[4,8,96,384]{3,2,1,0:T(8,128)(2,1)}), bf16[4,8,96,384]{3,2,1,0:T(8,128)(2,1)S(1)}, u32[]{:S(2)}, u32[]{:S(2)}) %all-to-all-start.2) | async-done | bytes 2359328 | tf_op jit(solution)/shard_map/all_to_all | solution.py:311
  553.1 3.0 convert_select_fusion
  (26 shorter events, 0.2 us)
Async XLA Ops:
  4.4 3.8 copy-start.1
  4.4 3.8 copy-start.6
  4.4 4.8 copy-start.5
  4.7 7.5 %copy-start.4 = (s32[128,64]{0,1:T(8,128)S(1)}, s32[128,64]{0,1:T(8,128)}, u32[]{:S(2)}) copy-start(s32[128,64]{0,1:T(8,128)} %param.11) | copy-start | bytes 98308
  6.0 28.0 %collective-permute-start = (bf16[2,64,63,128]{3,1,2,0:T(8,128)(2,1)S(1)}, bf16[2,64,63,128]{3,1,2,0:T(8,128)(2,1)}, u32[]{:S(2)}, u32[]{:S(2)}) collective-permute-start(bf16[2,64,63,128]{3,1,2,0:T(8,128)(2,1)S(1)} %copy.62), channel_id=1, source_target_pairs={{1,0},{2,1},{3,2},{5,4},{6,5},{7,6},{9,8},{10,9},{11,10},{13,12},{... | collective-permute-start | bytes 6193160 | tf_op jit(solution)/shard_map/ppermute | solution.py:22
  75.8 2.0 copy-start
  77.9 5.7 %copy-start.2 = (bf16[2,512,192]{1,2,0:T(8,128)(2,1)S(1)}, bf16[2,512,192]{1,2,0:T(8,128)(2,1)}, u32[]{:S(2)}) copy-start(bf16[2,512,192]{1,2,0:T(8,128)(2,1)} %param.8) | copy-start | bytes 1179652
  77.9 81.7 %all-to-all-start = ((bf16[8,16,128,128]{3,2,1,0:T(8,128)(2,1)}), bf16[8,16,128,128]{3,2,1,0:T(8,128)(2,1)}, u32[]{:S(2)}, u32[]{:S(2)}) async-start(bf16[8,16,128,128]{3,2,1,0:T(8,128)(2,1)} %copy-done), calls=%async_computation | async-start | bytes 8388608 | tf_op jit(solution)/shard_map/all_to_all | solution.py:293
  87.4 84.3 %copy-start.3 = (s32[128,192]{0,1:T(8,128)S(1)}, s32[128,192]{0,1:T(8,128)}, u32[]{:S(2)}) copy-start(s32[128,192]{0,1:T(8,128)} %param.9) | copy-start | bytes 294916
  166.9 23.1 %all-to-all-start.1 = ((bf16[4,4,384,128]{3,2,1,0:T(8,128)(2,1)}), bf16[4,4,384,128]{3,2,1,0:T(8,128)(2,1)S(1)}, u32[]{:S(2)}, u32[]{:S(2)}) async-start(bf16[4,4,384,128]{3,2,1,0:T(8,128)(2,1)} %bitcast.25), calls=%async_computation.1 | async-start | bytes 3145728 | tf_op jit(solution)/shard_map/all_to_all | solution.py:301
  520.7 32.4 %all-to-all-start.2 = ((bf16[4,8,96,384]{3,2,1,0:T(8,128)(2,1)}), bf16[4,8,96,384]{3,2,1,0:T(8,128)(2,1)S(1)}, u32[]{:S(2)}, u32[]{:S(2)}) async-start(bf16[4,8,96,384]{3,2,1,0:T(8,128)(2,1)} %factor_slots.1), calls=%async_computation.2 | async-start | bytes 4718592 | tf_op jit(solution)/shard_map/all_to_all | solution.py:311

commit v2 on v1

--- a/solution.py
+++ b/solution.py
@@ -55,17 +55,22 @@
     gate_index = lax.broadcasted_iota(jnp.int32, (gate_rows, width), 0)
     part_index = lax.broadcasted_iota(jnp.int32, (gate_rows, width), 1) // (width // pack)
 
-    def one_group(group, carry):
-        hit = gate_index == gates_ref[0, pl.ds(group, 1), :]
-        total = jnp.zeros(out_ref.shape[2:], F32)
-        for part in range(pack):
-            bin_index = bins_ref[(owner * groups + group) * pack + part]
-            chooser = jnp.where(hit & (part_index == part), 1.0, 0.0).astype(BF16)
-            total += jnp.dot(spectrum_ref[bin_index], chooser, preferred_element_type=F32)
-        out_ref[0, group] = total.astype(BF16)
+    unroll = math.gcd(groups, 4)
+    masks = [part_index == part for part in range(pack)]
+
+    def some_groups(step, carry):
+        for inner in range(unroll):
+            group = step * unroll + inner
+            hit = gate_index == gates_ref[0, pl.ds(group, 1), :]
+            total = jnp.zeros(out_ref.shape[2:], F32)
+            for part in range(pack):
+                bin_index = bins_ref[(owner * groups + group) * pack + part]
+                chooser = jnp.where(hit & masks[part], 1.0, 0.0).astype(BF16)
+                total += jnp.dot(spectrum_ref[bin_index], chooser, preferred_element_type=F32)
+            out_ref[0, group] = total.astype(BF16)
         return carry
 
-    lax.fori_loop(0, groups, one_group, 0)
+    lax.fori_loop(0, groups // unroll, some_groups, 0)
 
 
 def select_gates(spectrum, slot_bins, slot_gates, owners, pack):
@@ -134,67 +139,79 @@
 
 def loaded_covariance(beams, pivot_row, part, pack, count_rows):
     dof = pivot_row.shape[1]
+    width = beams[0].shape[1] // pack
     hot = lax.broadcasted_iota(jnp.int32, (dof, dof), 0) == pivot_row
     hot = jnp.where(hot, 1.0, 0.0).astype(BF16)
-    picked = []
-    for half in range(2):
-        rows = jnp.concatenate([b[half * dof : (half + 1) * dof] for b in beams], axis=1)
-        moved = lax.dot_general(hot, rows, (((0,), (0,)), ((), ())), preferred_element_type=F32)
-        picked.append(moved)
-    real_part, imag_part = picked
-    upper = jnp.concatenate([real_part, imag_part], axis=1)
-    lower = jnp.concatenate([imag_part, -real_part], axis=1)
+    own = jnp.concatenate([b[:, part * width : (part + 1) * width] for b in beams], axis=1)
+    picked = [
+        lax.dot_general(
+            hot,
+            own[half * dof : (half + 1) * dof],
+            (((0,), (0,)), ((), ())),
+            preferred_element_type=F32,
+        )
+        for half in range(2)
+    ]
+    upper = jnp.concatenate([picked[0], picked[1]], axis=1).astype(BF16)
+    lower = jnp.concatenate([picked[1], -picked[0]], axis=1).astype(BF16)
     stacked = jnp.concatenate([upper, lower], axis=0)
-    width = beams[0].shape[1]
-    lane = lax.broadcasted_iota(jnp.int32, stacked.shape, 1)
-    kept = jnp.where((lane % width) // (width // pack) == part, stacked, 0.0).astype(BF16)
     gram = lax.dot_general(
-        kept, stacked.astype(BF16), (((1,), (1,)), ((), ())), preferred_element_type=F32
-    )
-    order = 2 * dof
-    row = lax.broadcasted_iota(jnp.int32, (order, order), 0)
-    col = lax.broadcasted_iota(jnp.int32, (order, order), 1)
-    return gram / count_rows + jnp.where(row == col, LOADING, 0.0)
-
-
-def eliminate(tiles):
-    sub = lax.broadcasted_iota(jnp.int32, (8, LANES), 0)
-    diagonal = [jnp.ones((8, LANES), F32) for _ in tiles]
-    for t in range(PANEL):
-        home, place = divmod(t, 8)
-        column = jnp.broadcast_to(tiles[home][0][:, t : t + 1], (8, LANES))
-        diagonal[home] = jnp.where(sub == place, column, diagonal[home])
-        inverse = pl.reciprocal(column, approx=True)
-        inverse = inverse * (2.0 - column * inverse)
-        inverse = inverse[place : place + 1]
-        scaled = [piece[place : place + 1] * inverse for piece in tiles[home]]
-        for i in range(home, PANEL // 8):
-            if i == home and place == 7:
-                continue
-            if i == home:
-                factor = jnp.where(sub > place, column, 0.0)
-            else:
-                factor = jnp.broadcast_to(tiles[i][0][:, t : t + 1], (8, LANES))
-            tiles[i] = [piece - factor * s for piece, s in zip(tiles[i], scaled)]
-    scales = [lax.rsqrt(d) for d in diagonal]
-    return [[piece * s for piece in row] for row, s in zip(tiles, scales)]
-
-
-def factor_kernel(pivots_ref, beams_ref, out_ref, work, *, pack, count_rows):
+        stacked, stacked, (((1,), (1,)), ((), ())), preferred_element_type=F32
+    )
+    return gram * (1.0 / count_rows)
+
+
+def lane_spread(piece, lane):
+    return jnp.broadcast_to(piece[:, lane : lane + 1], piece.shape)
+
+
+def eliminate(rows):
+    scales = []
+    for first in range(0, PANEL, 8):
+        span = range(first, first + 8)
+        small = {(i, j): lane_spread(rows[i][0], j) for i in span for j in span if j >= i}
+        for t in span:
+            pivot = small[t, t]
+            inverse = pl.reciprocal(pivot, approx=True)
+            inverse = inverse * (2.0 - pivot * inverse)
+            scales.append(lax.rsqrt(pivot))
+            for i in range(t + 1, first + 8):
+                factor = small[t, i] * inverse
+                for j in range(i, first + 8):
+                    small[i, j] = small[i, j] - factor * small[t, j]
+                rows[i] = [x - factor * y for x, y in zip(rows[i], rows[t])]
+        for t in span:
+            rows[t] = [x * scales[t] for x in rows[t]]
+        for i in range(first + 8, PANEL):
+            for t in span:
+                factor = lane_spread(rows[t][0], i)
+                rows[i] = [x - factor * y for x, y in zip(rows[i], rows[t])]
+    return rows
+
+
+def factor_kernel(pivots_ref, beams_ref, out_ref, panel_ref, *work, pack, count_rows):
     ranges, groups = beams_ref.shape[:2]
-    slots, order, _ = work.shape
-
+    slots = len(work)
+    order = work[0].shape[0]
+    height = panel_ref.shape[1] // PANEL
+
+    row = lax.broadcasted_iota(jnp.int32, (LANES, LANES), 0)
+    col = lax.broadcasted_iota(jnp.int32, (LANES, LANES), 1)
+    loading = jnp.where(row == col, LOADING, 0.0)
     for slot in range(slots):
         group, part = divmod(slot, pack)
-        work[slot] = loaded_covariance(
+        work[slot][...] = loaded_covariance(
             [beams_ref[r, group] for r in range(ranges)],
             pivots_ref[slot : slot + 1, :],
             part,
             pack,
             count_rows,
         )
+        for start in range(0, order, LANES):
+            work[slot][start : start + LANES, start : start + LANES] += loading
 
     lane = lax.broadcasted_iota(jnp.int32, (PANEL, LANES), 1)
+    eights = range(0, PANEL, 8)
     for start in range(0, order, LANES):
         chunks = (order - start) // LANES
 
@@ -202,38 +219,48 @@
             base = pl.multiple_of(start + p * PANEL, PANEL)
             back = p * PANEL
             for slot in range(slots):
-                tiles = []
-                for i in range(PANEL // 8):
-                    piece = work[slot, pl.ds(pl.multiple_of(base + 8 * i, 8), 8), start:]
-                    row = [piece[:, w * LANES : (w + 1) * LANES] for w in range(chunks)]
-                    row[0] = pltpu.roll(row[0], (LANES - back) % LANES, 1)
-                    tiles.append(row)
-                tiles = eliminate(tiles)
-                for row in tiles:
-                    row[0] = pltpu.roll(row[0], back, 1)
-                rows = [
-                    jnp.concatenate([tiles[i][w] for i in range(PANEL // 8)], axis=0)
-                    for w in range(chunks)
-                ]
-                panel = jnp.concatenate(rows, axis=1)
-                work[slot, pl.ds(base, PANEL), start:] = panel
-                below = jnp.where(lane >= back + PANEL, rows[0], 0.0)
-                work[slot, start : start + LANES, start:] -= cross_product(below, panel)
+                for i in eights:
+                    place = pl.ds(pl.multiple_of(base + i, 8), 8)
+                    for w in range(chunks):
+                        left = start + w * LANES
+                        piece = work[slot][place, left : left + LANES]
+                        panel_ref[w, pl.ds(i * height + slot, 8, stride=height), :] = piece
+            rows = []
+            for t in range(PANEL):
+                pieces = [panel_ref[w, t * height : (t + 1) * height, :] for w in range(chunks)]
+                pieces[0] = pltpu.roll(pieces[0], (LANES - back) % LANES, 1)
+                rows.append(pieces)
+            rows = eliminate(rows)
+            for t in range(PANEL):
+                rows[t][0] = pltpu.roll(rows[t][0], back, 1)
+                for w in range(chunks):
+                    panel_ref[w, t * height : (t + 1) * height, :] = rows[t][w]
+            for slot in range(slots):
+                parts = []
+                for w in range(chunks):
+                    pieces = [
+                        panel_ref[w, pl.ds(i * height + slot, 8, stride=height), :] for i in eights
+                    ]
+                    parts.append(jnp.concatenate(pieces, axis=0))
+                panel = jnp.concatenate(parts, axis=1)
+                work[slot][pl.ds(base, PANEL), start:] = panel
+                below = jnp.where(lane >= back + PANEL, parts[0], 0.0)
+                work[slot][start : start + LANES, start:] -= cross_product(below, panel)
             return carry
 
         lax.fori_loop(0, LANES // PANEL, one_panel, 0)
         if chunks > 1:
             after = start + LANES
             for slot in range(slots):
-                ready = work[slot, start:after, after:]
-                work[slot, after:, after:] -= cross_product(ready, ready)
+                ready = work[slot][start:after, after:]
+                work[slot][after:, after:] -= cross_product(ready, ready)
 
     owners, _, share, _ = out_ref.shape
     for slot in range(slots):
         for r in range(owners):
             row = lax.broadcasted_iota(jnp.int32, (share, order), 0) + r * share
             col = lax.broadcasted_iota(jnp.int32, (share, order), 1)
-            piece = work[slot, r * share : (r + 1) * share]
+            piece = work[slot][r * share : (r + 1) * share]
             out_ref[r, slot] = jnp.where(col >= row, piece, 0.0).astype(out_ref.dtype)
 
 
@@ -241,6 +268,7 @@
     ranges = beams.shape[0]
     slots, dof = pivot_rows.shape
     order = 2 * dof
+    height = -(-slots // 8) * 8
     return pl.pallas_call(
         functools.partial(factor_kernel, pack=pack, count_rows=count_rows),
         out_shape=jax.ShapeDtypeStruct((ranges, slots, order // ranges, order), BF16),
@@ -249,7 +277,8 @@
             pl.BlockSpec(memory_space=pltpu.VMEM),
         ],
         out_specs=pl.BlockSpec(memory_space=pltpu.VMEM),
-        scratch_shapes=[pltpu.VMEM((slots, order, order), F32)],
+        scratch_shapes=[pltpu.VMEM((order // LANES, PANEL * height, LANES), F32)]
+        + [pltpu.VMEM((order, order), F32) for _ in range(slots)],
         compiler_params=PARAMS,
         name="factor_slots",
     )(pivot_rows, beams)

time: 558 us -> 243 us (0.44)
  Pallas kernels: 361 us -> 46.6 us
    pallas_call x1, Pallas kernels: 331 us -> 29.3 us  [factor_slots(): pl.pallas_call(functools.partial(factor_kernel, pack=pack, count_rows=cou...]
    pallas_call x1, Pallas kernels: 23.3 us -> 9.97 us  [select_gates(): pl.pallas_call(functools.partial(select_kernel, pack=pack, groups=groups)...]
  transfers between devices with their start and end apart: 4 -> 4, of which waited for: 4 -> 4; matrix products, arithmetic and copies ran while one was open for 2% -> 5% of each run, Pallas kernels for 0% -> 0%
where the time goes in v2:
time: 243 us; the launch traced here: 241 us
  waiting for transfers between devices  135 us (56%)
  Pallas kernels  46.6 us (19%)
  local copies, waits for them, and re-layouts  24.3 us (10%)
  starting transfers between devices  16.8 us (7%)
  matrix products  9.16 us (4%)
  other arithmetic  8.53 us (4%)
    all_to_all x1, waiting for transfers between devices, local(): lax.all_to_all(outgoing, 'dop', split_axis=0, concat_axis=0, tiled=True)  72.1 us
    pallas_call x1, Pallas kernels, factor_slots(): pl.pallas_call(functools.partial(factor_kernel, pack=pack, count_rows=cou...  29.3 us
    all_to_all x1, waiting for transfers between devices, local(): lax.all_to_all(factors, 'rng', split_axis=0, concat_axis=0, tiled=True)  26.4 us
    ppermute x1, waiting for transfers between devices, shifted(): return lax.ppermute(array, axis, pairs)  19.6 us
    all_to_all x1, waiting for transfers between devices, local(): lax.all_to_all(beams, 'rng', split_axis=0, concat_axis=0, tiled=True)  16.9 us
    pallas_call x1, Pallas kernels, select_gates(): pl.pallas_call(functools.partial(select_kernel, pack=pack, groups=groups)...  9.97 us
    dot_general x1, matrix products, local(): jnp.einsum('abpk,bcgp->kacg', doppler_table(pulse_count).astype(BF16), ma...  9.16 us
    pallas_call x1, Pallas kernels, form_beams(): pl.pallas_call(beam_kernel, out_shape=jax.ShapeDtypeStruct((groups, weigh...  7.3 us
  transfers between devices with their start and end apart: 4, of which 4 were waited for; matrix products, arithmetic and copies ran while one was open for 5% of the time, Pallas kernels for 0%

profile of v2, /device:TPU:1, one launch (start us, length us, event | category | flops | bytes accessed | tf_op | source)
XLA Modules:
  0.0 241.3 jit_solution(9416949317210973526)
XLA Ops:
  0.0 4.4 %copy.76 = bf16[2,64,128,128]{3,2,0,1:T(8,128)(2,1)S(1)} copy(f32[2,64,128,128]{3,2,1,0:T(8,128)} %param.6) | data formatting | bytes 12582912 | tf_op args[0]
  4.4 0.0 copy-start.1
  4.4 0.0 copy-start.6
  4.4 0.0 copy-start.5
  4.4 0.3 slice.29
  4.7 1.3 copy.62
  6.0 2.1 collective-permute-start
  8.2 0.2 reduce-window.9
  8.4 0.8 iota_compare_fusion
  9.2 2.7 %select_reduce_fusion = f32[2,128,191]{1,2,0:T(8,128)S(1)} fusion(f32[2,64]{1,0:T(2,128)S(1)} %copy-done.5, pred[128,191,64]{0,2,1:T(8,128)(4,1)S(1)} %iota_compare_fusion), kind=kLoop, calls=%fused_computation.2 | loop fusion | flops 6209792 | bytes 1760768 | tf_op jit(solution)/shard_map/reduce_sum | solution.py:47
  11.9 0.1 add_minimum_fusion
  12.0 0.1 min.48
  12.1 0.1 min.45.bins_ref
  12.2 0.1 copy.58
  12.4 0.7 gather_fusion.1
  13.1 0.1 gather.12
  13.2 0.1 fusion.26
  13.2 0.1 copy.57
  13.4 0.2 broadcast_in_dim.68
  13.6 0.1 broadcast_in_dim.69
  13.7 0.3 fusion.23
  14.0 0.3 negate_convert_fusion
  14.4 19.6 %collective-permute-done = bf16[2,64,63,128]{3,1,2,0:T(8,128)(2,1)} collective-permute-done((bf16[2,64,63,128]{3,1,2,0:T(8,128)(2,1)S(1)}, bf16[2,64,63,128]{3,1,2,0:T(8,128)(2,1)}, u32[]{:S(2)}, u32[]{:S(2)}) %collective-permute-start) | collective-permute-done | bytes 2064416 | tf_op jit(solution)/shard_map/ppermute | solution.py:22
  34.0 2.9 %copy.63 = bf16[2,64,63,128]{3,2,0,1:T(8,128)(2,1)S(1)} copy(bf16[2,64,63,128]{3,1,2,0:T(8,128)(2,1)} %collective-permute-done) | data formatting | bytes 4128768 | tf_op jit(solution)/shard_map/ppermute | solution.py:22
  36.9 9.2 %fusion.6 = bf16[128,2,64,128]{0,3,1,2:T(8,128)(2,1)} fusion(bf16[2,64,63,128]{3,2,0,1:T(8,128)(2,1)S(1)} %copy.63, bf16[2,64,128,128]{3,2,0,1:T(8,128)(2,1)} %copy-done.1, bf16[1,2,128,191]{2,3,1,0:T(8,128)(2,1)S(1)} %maximum_bitcast_fusion.14, bf16[1,2,128,191]{2,3,1,0:T(8,128)(2,1)S(1)} %convert_bitcast_fusion, ...), kind=kOutput, calls=%fused_computation.14 | convolution fusion | flops 2693330944 | bytes 10779648 | tf_op jit(solution)/shard_map/abpk,bcgp->kacg/dot_general | solution.py:308
  46.1 6.4 %copy.65 = bf16[128,2,64,128]{3,2,1,0:T(8,128)(2,1)} copy(bf16[128,2,64,128]{0,3,1,2:T(8,128)(2,1)} %fusion.6) | data formatting | bytes 8388608 | tf_op jit(solution)/shard_map/convert_element_type | solution.py:313
  52.5 10.0 %select_gates.1 = bf16[8,16,128,128]{3,2,1,0:T(8,128)(2,1)S(1)} custom-call(s32[256]{0:T(256)S(1)} %min.45.bins_ref, s32[8,16,128]{2,1,0:T(8,128)S(1)} %broadcast_select_fusion.gates_ref, bf16[128,128,128]{2,1,0:T(8,128)(2,1)} %bitcast.67), custom_call_target="tpu_custom_call" | custom-call | tf_op jit(solution)/shard_map/select_gates/pallas_call | solution.py:80
  62.5 2.0 copy-done
  64.5 5.7 %all-to-all-start = ((bf16[8,16,128,128]{3,2,1,0:T(8,128)(2,1)}), bf16[8,16,128,128]{3,2,1,0:T(8,128)(2,1)}, u32[]{:S(2)}, u32[]{:S(2)}) async-start(bf16[8,16,128,128]{3,2,1,0:T(8,128)(2,1)} %copy-done), calls=%async_computation | async-start | bytes 8388608 | tf_op jit(solution)/shard_map/all_to_all | solution.py:322
  70.2 0.2 copy.53
  70.5 0.1 pad_maximum_fusion
  70.6 0.2 maximum_bitcast_fusion.8
  70.8 2.2 copy.71
  73.0 1.1 reshape.253.weights_ref
  74.1 72.1 %all-to-all-done.arrived_ref = bf16[8,16,128,128]{3,2,1,0:T(8,128)(2,1)} async-done(((bf16[8,16,128,128]{3,2,1,0:T(8,128)(2,1)}), bf16[8,16,128,128]{3,2,1,0:T(8,128)(2,1)}, u32[]{:S(2)}, u32[]{:S(2)}) %all-to-all-start) | async-done | bytes 4194336 | tf_op jit(solution)/shard_map/all_to_all | solution.py:322
  146.2 7.3 %form_beams.1 = bf16[16,384,128]{2,1,0:T(8,128)(2,1)} custom-call(bf16[384,1024]{1,0:T(8,128)(2,1)S(1)} %reshape.253.weights_ref, bf16[8,16,128,128]{3,2,1,0:T(8,128)(2,1)} %all-to-all-done.arrived_ref), custom_call_target="tpu_custom_call" | custom-call | tf_op jit(solution)/shard_map/form_beams/pallas_call | solution.py:110
  153.5 4.2 %all-to-all-start.1 = ((bf16[4,4,384,128]{3,2,1,0:T(8,128)(2,1)}), bf16[4,4,384,128]{3,2,1,0:T(8,128)(2,1)S(1)}, u32[]{:S(2)}, u32[]{:S(2)}) async-start(bf16[4,4,384,128]{3,2,1,0:T(8,128)(2,1)} %bitcast.25), calls=%async_computation.1 | async-start | bytes 3145728 | tf_op jit(solution)/shard_map/all_to_all | solution.py:330
  157.7 0.6 dynamic_slice.8
  158.4 0.1 copy.52
  159.1 0.6 gather_fusion
  159.7 0.1 broadcast_select_fusion.1.pivots_ref
  159.8 16.9 %all-to-all-done.1.beams_ref = bf16[4,4,384,128]{3,2,1,0:T(8,128)(2,1)S(1)} async-done(((bf16[4,4,384,128]{3,2,1,0:T(8,128)(2,1)}), bf16[4,4,384,128]{3,2,1,0:T(8,128)(2,1)S(1)}, u32[]{:S(2)}, u32[]{:S(2)}) %all-to-all-start.1) | async-done | bytes 1572896 | tf_op jit(solution)/shard_map/all_to_all | solution.py:330
  176.6 29.3 %factor_slots.1 = bf16[4,8,96,384]{3,2,1,0:T(8,128)(2,1)} custom-call(s32[8,192]{1,0:T(8,128)S(1)} %broadcast_select_fusion.1.pivots_ref, bf16[4,4,384,128]{3,2,1,0:T(8,128)(2,1)S(1)} %all-to-all-done.1.beams_ref), custom_call_target="tpu_custom_call" | custom-call | tf_op jit(solution)/shard_map/factor_slots/pallas_call | solution.py:272
  205.9 4.8 %all-to-all-start.2 = ((bf16[4,8,96,384]{3,2,1,0:T(8,128)(2,1)}), bf16[4,8,96,384]{3,2,1,0:T(8,128)(2,1)S(1)}, u32[]{:S(2)}, u32[]{:S(2)}) async-start(bf16[4,8,96,384]{3,2,1,0:T(8,128)(2,1)} %factor_slots.1), calls=%async_computation.2 | async-start | bytes 4718592 | tf_op jit(solution)/shard_map/all_to_all | solution.py:340
  210.7 0.6 dynamic_slice.7
  211.3 0.6 iota_compare_fusion.1
  212.0 26.4 %all-to-all-done.2 = bf16[4,8,96,384]{3,2,1,0:T(8,128)(2,1)S(1)} async-done(((bf16[4,8,96,384]{3,2,1,0:T(8,128)(2,1)}), bf16[4,8,96,384]{3,2,1,0:T(8,128)(2,1)S(1)}, u32[]{:S(2)}, u32[]{:S(2)}) %all-to-all-start.2) | async-done | bytes 2359328 | tf_op jit(solution)/shard_map/all_to_all | solution.py:340
  238.3 3.0 %convert_select_fusion = f32[32,96,384]{2,1,0:T(8,128)} fusion(bf16[4,8,96,384]{3,2,1,0:T(8,128)(2,1)S(1)} %all-to-all-done.2, pred[32]{0:T(512)(128)(4,1)S(1)} %iota_compare_fusion.1), kind=kLoop, calls=%fused_computation.11 | loop fusion | flops 2359296 | bytes 7077920 | tf_op jit(solution)/shard_map/jit(_where)/select_n | solution.py:343
  (26 shorter events, 0.2 us)
Async XLA Ops:
  4.4 3.8 %copy-start.1 = (bf16[2,64,128,128]{3,2,0,1:T(8,128)(2,1)}, bf16[2,64,128,128]{3,2,0,1:T(8,128)(2,1)S(1)}, u32[]{:S(2)}) copy-start(bf16[2,64,128,128]{3,2,0,1:T(8,128)(2,1)S(1)} %copy.76) | copy-start | bytes 12582916
  4.4 3.8 %copy-start.6 = (s32[8]{0:T(128)S(1)}, s32[8]{0:T(128)}, u32[]{:S(2)}) copy-start(s32[8]{0:T(128)} %param.10) | copy-start | bytes 100
  4.4 4.8 %copy-start.5 = (f32[2,64]{1,0:T(2,128)S(1)}, f32[2,64]{1,0:T(2,128)}, u32[]{:S(2)}) copy-start(f32[2,64]{1,0:T(2,128)} %param.7) | copy-start | bytes 1540
  4.7 7.5 %copy-start.4 = (s32[128,64]{0,1:T(8,128)S(1)}, s32[128,64]{0,1:T(8,128)}, u32[]{:S(2)}) copy-start(s32[128,64]{0,1:T(8,128)} %param.11) | copy-start | bytes 98308
  6.0 28.0 %collective-permute-start = (bf16[2,64,63,128]{3,1,2,0:T(8,128)(2,1)S(1)}, bf16[2,64,63,128]{3,1,2,0:T(8,128)(2,1)}, u32[]{:S(2)}, u32[]{:S(2)}) collective-permute-start(bf16[2,64,63,128]{3,1,2,0:T(8,128)(2,1)S(1)} %copy.62), channel_id=1, source_target_pairs={{1,0},{2,1},{3,2},{5,4},{6,5},{7,6},{9,8},{10,9},{11,10},{13,12},{... | collective-permute-start | bytes 6193160 | tf_op jit(solution)/shard_map/ppermute | solution.py:22
  62.5 2.0 copy-start
  64.5 5.7 %copy-start.2 = (bf16[2,512,192]{1,2,0:T(8,128)(2,1)S(1)}, bf16[2,512,192]{1,2,0:T(8,128)(2,1)}, u32[]{:S(2)}) copy-start(bf16[2,512,192]{1,2,0:T(8,128)(2,1)} %param.8) | copy-start | bytes 1179652
  64.5 81.7 %all-to-all-start = ((bf16[8,16,128,128]{3,2,1,0:T(8,128)(2,1)}), bf16[8,16,128,128]{3,2,1,0:T(8,128)(2,1)}, u32[]{:S(2)}, u32[]{:S(2)}) async-start(bf16[8,16,128,128]{3,2,1,0:T(8,128)(2,1)} %copy-done), calls=%async_computation | async-start | bytes 8388608 | tf_op jit(solution)/shard_map/all_to_all | solution.py:322
  74.1 84.3 %copy-start.3 = (s32[128,192]{0,1:T(8,128)S(1)}, s32[128,192]{0,1:T(8,128)}, u32[]{:S(2)}) copy-start(s32[128,192]{0,1:T(8,128)} %param.9) | copy-start | bytes 294916
  153.5 23.1 %all-to-all-start.1 = ((bf16[4,4,384,128]{3,2,1,0:T(8,128)(2,1)}), bf16[4,4,384,128]{3,2,1,0:T(8,128)(2,1)S(1)}, u32[]{:S(2)}, u32[]{:S(2)}) async-start(bf16[4,4,384,128]{3,2,1,0:T(8,128)(2,1)} %bitcast.25), calls=%async_computation.1 | async-start | bytes 3145728 | tf_op jit(solution)/shard_map/all_to_all | solution.py:330
  205.9 32.4 %all-to-all-start.2 = ((bf16[4,8,96,384]{3,2,1,0:T(8,128)(2,1)}), bf16[4,8,96,384]{3,2,1,0:T(8,128)(2,1)S(1)}, u32[]{:S(2)}, u32[]{:S(2)}) async-start(bf16[4,8,96,384]{3,2,1,0:T(8,128)(2,1)} %factor_slots.1), calls=%async_computation.2 | async-start | bytes 4718592 | tf_op jit(solution)/shard_map/all_to_all | solution.py:340

commit v3 on v2

--- a/solution.py
+++ b/solution.py
@@ -90,6 +90,11 @@
             out_specs=pl.BlockSpec((1, groups, rows, width), lambda i, b: (i, 0, 0, 0)),
         ),
         compiler_params=PARAMS,
+        cost_estimate=pl.CostEstimate(
+            flops=2 * slot_bins.shape[0] * rows * gate_rows * width,
+            bytes_accessed=spectrum.size * 2,
+            transcendentals=0,
+        ),
         name="select_gates",
     )(slot_bins, slot_gates.reshape(owners, groups, width), spectrum)
 
@@ -117,6 +122,11 @@
         ],
         out_specs=pl.BlockSpec((step, weights.shape[0], width), lambda i: (i, 0, 0)),
         compiler_params=PARAMS,
+        cost_estimate=pl.CostEstimate(
+            flops=2 * arrived.size * weights.shape[0],
+            bytes_accessed=arrived.size * 2,
+            transcendentals=0,
+        ),
         name="form_beams",
     )(weights, arrived)
 
@@ -280,8 +290,17 @@
         scratch_shapes=[pltpu.VMEM((order // LANES, PANEL * height, LANES), F32)]
         + [pltpu.VMEM((order, order), F32) for _ in range(slots)],
         compiler_params=PARAMS,
+        cost_estimate=pl.CostEstimate(
+            flops=order * 60_000_000, bytes_accessed=beams.size * 2, transcendentals=0
+        ),
         name="factor_slots",
     )(pivot_rows, beams)
+
+
+def slot_parts(share_slots, pack):
+    halves = 2 if share_slots % (2 * pack) == 0 else 1
+    count = share_slots // halves
+    return [(i * count, count) for i in range(halves)]
 
 
 def local(raw_echo, replica, beam_weights, pivots, owner_counts, train_gates):
@@ -314,32 +333,40 @@
     spectrum = spectrum.reshape(pulse_count, 2 * ch_local, gate_rows)
 
     starts = jnp.cumsum(owner_counts, dtype=jnp.int32) - owner_counts
-    slot_index = jnp.arange(most_slots, dtype=jnp.int32)
-    slot_bins = jnp.minimum(starts[:, None] + slot_index[None, :], pulse_count - 1).reshape(-1)
-    slot_gates = jnp.take(train_gates % gate_rows, slot_bins, axis=0)
-    slot_gates = slot_gates.reshape(-1, pack * train_local)
-    outgoing = select_gates(spectrum, slot_bins, slot_gates, owners, pack)
-    arrived = lax.all_to_all(outgoing, "dop", split_axis=0, concat_axis=0, tiled=True)
+    me = lax.axis_index("dop")
+    my_start = lax.dynamic_index_in_dim(starts, me, 0, keepdims=False)
+    my_count = lax.dynamic_index_in_dim(owner_counts, me, 0, keepdims=False)
+    my_lead = lax.axis_index("rng") * share_slots
+    local_gates = train_gates % gate_rows
+    count_rows = float(train_local * ranges)
 
     dof = beam_weights.shape[2]
     weights = complex_block(beam_weights[0], beam_weights[1])
     weights = weights.reshape(2, 2, owners, ch_local, dof).transpose(0, 4, 2, 1, 3)
     weights = weights.reshape(2 * dof, -1)
-    beams = form_beams(arrived, weights)
-    beams = beams.reshape(ranges, -1, 2 * dof, beams.shape[-1])
-    beams = lax.all_to_all(beams, "rng", split_axis=0, concat_axis=0, tiled=True)
-
-    me = lax.axis_index("dop")
-    my_start = lax.dynamic_index_in_dim(starts, me, 0, keepdims=False)
-    my_count = lax.dynamic_index_in_dim(owner_counts, me, 0, keepdims=False)
-    lead = lax.axis_index("rng") * share_slots
-    share_bins = my_start + lead + jnp.arange(share_slots, dtype=jnp.int32)
-    my_pivots = jnp.take(pivots, jnp.minimum(share_bins, pulse_count - 1), axis=0)
-    count_rows = float(train_local * ranges)
-    factors = factor_slots(beams, my_pivots, pack, count_rows)
-    rows_done = lax.all_to_all(factors, "rng", split_axis=0, concat_axis=0, tiled=True)
+
+    lead_slots = jnp.arange(ranges, dtype=jnp.int32) * share_slots
+    parts = slot_parts(share_slots, pack)
+    sent = []
+    for first, count in parts:
+        some = first + jnp.arange(count, dtype=jnp.int32)
+        slots = (lead_slots[:, None] + some[None, :]).reshape(-1)
+        bins = jnp.minimum(starts[:, None] + slots[None, :], pulse_count - 1).reshape(-1)
+        gates = jnp.take(local_gates, bins, axis=0).reshape(-1, pack * train_local)
+        outgoing = select_gates(spectrum, bins, gates, owners, pack)
+        sent.append(lax.all_to_all(outgoing, "dop", split_axis=0, concat_axis=0, tiled=True))
+    done = []
+    for (first, count), arrived in zip(parts, sent):
+        beams = form_beams(arrived, weights)
+        beams = beams.reshape(ranges, -1, 2 * dof, beams.shape[-1])
+        beams = lax.all_to_all(beams, "rng", split_axis=0, concat_axis=0, tiled=True)
+        bins = my_start + my_lead + first + jnp.arange(count, dtype=jnp.int32)
+        my_pivots = jnp.take(pivots, jnp.minimum(bins, pulse_count - 1), axis=0)
+        factors = factor_slots(beams, my_pivots, pack, count_rows)
+        done.append(lax.all_to_all(factors, "rng", split_axis=0, concat_axis=0, tiled=True))
+    rows_done = jnp.concatenate(done, axis=1)
     rows_done = rows_done.reshape(most_slots, *rows_done.shape[2:])
-    filled = slot_index < my_count
+    filled = jnp.arange(most_slots, dtype=jnp.int32) < my_count
     return jnp.where(filled[:, None, None], rows_done.astype(F32), 0.0)
 
 

time: 243 us -> 244 us (level)
  waiting for transfers between devices: 135 us -> 88.7 us
  Pallas kernels: 46.6 us -> 71 us
  starting transfers between devices: 16.8 us -> 27.4 us
  local copies, waits for them, and re-layouts: 24.3 us -> 34.4 us
    all_to_all x1 -> x2, waiting for transfers between devices: 72.1 us -> 49.1 us  [local(): lax.all_to_all(outgoing, 'dop', split_axis=0, concat_axis=0, tiled=True)]
    pallas_call x1 -> x2, Pallas kernels: 29.3 us -> 49.4 us  [factor_slots(): pl.pallas_call(functools.partial(factor_kernel, pack=pack, count_rows=cou...]
    all_to_all x1 -> x2, waiting for transfers between devices: 26.4 us -> 13.8 us  [local(): lax.all_to_all(factors, 'rng', split_axis=0, concat_axis=0, tiled=True)]
    all_to_all x1 -> x2, waiting for transfers between devices: 16.9 us -> 5.63 us  [local(): lax.all_to_all(beams, 'rng', split_axis=0, concat_axis=0, tiled=True)]
    reshape x2, local copies, waits for them, and re-layouts: 3.29 us -> 9.09 us  [local(): weights = weights.reshape(2 * dof, -1)]
    pallas_call x1 -> x2, Pallas kernels: 9.97 us -> 15.7 us  [select_gates(): pl.pallas_call(functools.partial(select_kernel, pack=pack, groups=groups)...]
    all_to_all x1 -> x2, starting transfers between devices: 5.69 us -> 10.1 us  [local(): lax.all_to_all(outgoing, 'dop', split_axis=0, concat_axis=0, tiled=True)]
    all_to_all x1 -> x2, starting transfers between devices: 4.19 us -> 8.03 us  [local(): lax.all_to_all(beams, 'rng', split_axis=0, concat_axis=0, tiled=True)]
  transfers between devices with their start and end apart: 4 -> 7, of which waited for: 4 -> 5; matrix products, arithmetic and copies ran while one was open for 5% -> 8% of each run, Pallas kernels for 0% -> 26%
where the time goes in v3:
time: 244 us; the launch traced here: 242 us
  waiting for transfers between devices  88.7 us (36%)
  Pallas kernels  71 us (29%)
  local copies, waits for them, and re-layouts  34.4 us (14%)
  starting transfers between devices  27.4 us (11%)
  other arithmetic  10.2 us (4%)
  matrix products  9.79 us (4%)
    pallas_call x2, Pallas kernels, factor_slots(): pl.pallas_call(functools.partial(factor_kernel, pack=pack, count_rows=cou...  49.4 us
    all_to_all x2, waiting for transfers between devices, local(): lax.all_to_all(outgoing, 'dop', split_axis=0, concat_axis=0, tiled=True)  49.1 us
    ppermute x1, waiting for transfers between devices, shifted(): return lax.ppermute(array, axis, pairs)  20.1 us
    pallas_call x2, Pallas kernels, select_gates(): pl.pallas_call(functools.partial(select_kernel, pack=pack, groups=groups)...  15.7 us
    all_to_all x2, waiting for transfers between devices, local(): lax.all_to_all(factors, 'rng', split_axis=0, concat_axis=0, tiled=True)  13.8 us
    all_to_all x2, starting transfers between devices, local(): lax.all_to_all(outgoing, 'dop', split_axis=0, concat_axis=0, tiled=True)  10.1 us
    dot_general x1, matrix products, local(): jnp.einsum('abpk,bcgp->kacg', doppler_table(pulse_count).astype(BF16), ma...  9.79 us
    reshape x2, local copies, waits for them, and re-layouts, local(): weights = weights.reshape(2 * dof, -1)  9.09 us
  transfers between devices with their start and end apart: 7, of which 5 were waited for; matrix products, arithmetic and copies ran while one was open for 8% of the time, Pallas kernels for 26%

profile of v3, /device:TPU:1, one launch (start us, length us, event | category | flops | bytes accessed | tf_op | source)
XLA Modules:
  0.0 242.4 jit_solution(11998028437835734049)
XLA Ops:
  0.0 4.4 %copy.68 = bf16[2,64,128,128]{3,2,0,1:T(8,128)(2,1)S(1)} copy(f32[2,64,128,128]{3,2,1,0:T(8,128)} %param.10) | data formatting | bytes 12582912 | tf_op args[0]
  4.4 2.0 copy-done.1
  6.4 0.3 slice.33
  6.7 2.7 %copy.52 = bf16[2,64,63,128]{3,1,2,0:T(8,128)(2,1)} copy(bf16[2,64,63,128]{3,2,0,1:T(8,128)(2,1)S(1)} %slice.33) | data formatting | bytes 4128768 | tf_op jit(solution)/shard_map/slice | solution.py:319
  9.3 2.1 collective-permute-start
  11.6 0.1 add.149
  11.7 0.2 reduce-window.9
  12.1 0.1 copy.48
  12.2 0.6 gather_fusion.3
  13.1 0.8 iota_compare_fusion
  13.9 2.8 %select_reduce_fusion = f32[2,128,191]{1,2,0:T(8,128)S(1)} fusion(f32[2,64]{1,0:T(2,128)S(1)} %copy-done.5, pred[128,191,64]{0,2,1:T(8,128)(4,1)S(1)} %iota_compare_fusion), kind=kLoop, calls=%fused_computation.4 | loop fusion | flops 6209792 | bytes 1760768 | tf_op jit(solution)/shard_map/reduce_sum | solution.py:47
  16.7 0.3 fusion.23
  17.0 0.3 negate_convert_fusion
  17.4 20.1 %collective-permute-done = bf16[2,64,63,128]{3,1,2,0:T(8,128)(2,1)} collective-permute-done((bf16[2,64,63,128]{3,1,2,0:T(8,128)(2,1)}, bf16[2,64,63,128]{3,1,2,0:T(8,128)(2,1)}, u32[]{:S(2)}, u32[]{:S(2)}) %collective-permute-start) | collective-permute-done | bytes 2064416 | tf_op jit(solution)/shard_map/ppermute | solution.py:22
  37.5 4.3 %copy.53 = bf16[2,64,63,128]{3,2,0,1:T(8,128)(2,1)} copy(bf16[2,64,63,128]{3,1,2,0:T(8,128)(2,1)} %collective-permute-done) | data formatting | bytes 4128768 | tf_op jit(solution)/shard_map/ppermute | solution.py:22
  41.8 9.8 %fusion.6 = bf16[128,2,64,128]{0,3,1,2:T(8,128)(2,1)} fusion(bf16[2,64,63,128]{3,2,0,1:T(8,128)(2,1)} %copy.53, bf16[2,64,128,128]{3,2,0,1:T(8,128)(2,1)} %copy-done.1, bf16[1,2,128,191]{2,3,1,0:T(8,128)(2,1)S(1)} %maximum_bitcast_fusion.14, bf16[1,2,128,191]{2,3,1,0:T(8,128)(2,1)S(1)} %convert_bitcast_fusion, ...), kind=kOutput, calls=%fused_computation.16 | convolution fusion | flops 2693330944 | bytes 10779648 | tf_op jit(solution)/shard_map/abpk,bcgp->kacg/dot_general | solution.py:327
  51.6 6.4 %copy.55 = bf16[128,2,64,128]{3,2,1,0:T(8,128)(2,1)} copy(bf16[128,2,64,128]{0,3,1,2:T(8,128)(2,1)} %fusion.6) | data formatting | bytes 8388608 | tf_op jit(solution)/shard_map/convert_element_type | solution.py:332
  58.0 7.8 %select_gates.3 = bf16[8,8,128,128]{3,2,1,0:T(8,128)(2,1)} custom-call(s32[128]{0:T(128)S(1)} %min.25.bins_ref, s32[8,8,128]{2,1,0:T(8,128)S(1)} %reshape_reshape.7.gates_ref, bf16[128,128,128]{2,1,0:T(8,128)(2,1)} %bitcast.66), custom_call_target="tpu_custom_call" | custom-call | flops 536870912 | bytes 4194304 | tf_op jit(solution)/shard_map/select_gates/pallas_call | solution.py:80
  65.8 5.6 %all-to-all-start.3 = ((bf16[8,8,128,128]{3,2,1,0:T(8,128)(2,1)}), bf16[8,8,128,128]{3,2,1,0:T(8,128)(2,1)S(1)}, u32[]{:S(2)}, u32[]{:S(2)}) async-start(bf16[8,8,128,128]{3,2,1,0:T(8,128)(2,1)} %select_gates.3), calls=%async_computation.3 | async-start | bytes 4194304 | tf_op jit(solution)/shard_map/all_to_all | solution.py:357
  71.5 0.6 gather_fusion.1
  72.3 7.8 %select_gates.2 = bf16[8,8,128,128]{3,2,1,0:T(8,128)(2,1)} custom-call(s32[128]{0:T(128)S(1)} %min.22.bins_ref, s32[8,8,128]{2,1,0:T(8,128)S(1)} %reshape_reshape.6.gates_ref, bf16[128,128,128]{2,1,0:T(8,128)(2,1)} %bitcast.67), custom_call_target="tpu_custom_call" | custom-call | flops 536870912 | bytes 4194304 | tf_op jit(solution)/shard_map/select_gates/pallas_call | solution.py:80
  80.2 21.7 %all-to-all-done.3.arrived_ref = bf16[8,8,128,128]{3,2,1,0:T(8,128)(2,1)S(1)} async-done(((bf16[8,8,128,128]{3,2,1,0:T(8,128)(2,1)}), bf16[8,8,128,128]{3,2,1,0:T(8,128)(2,1)S(1)}, u32[]{:S(2)}, u32[]{:S(2)}) %all-to-all-start.3) | async-done | bytes 2097184 | tf_op jit(solution)/shard_map/all_to_all | solution.py:357
  101.8 4.6 %all-to-all-start = ((bf16[8,8,128,128]{3,2,1,0:T(8,128)(2,1)}), bf16[8,8,128,128]{3,2,1,0:T(8,128)(2,1)}, u32[]{:S(2)}, u32[]{:S(2)}) async-start(bf16[8,8,128,128]{3,2,1,0:T(8,128)(2,1)} %select_gates.2), calls=%async_computation | async-start | bytes 4194304 | tf_op jit(solution)/shard_map/all_to_all | solution.py:357
  106.4 0.2 copy.44
  106.7 0.1 pad_maximum_fusion.1
  106.8 1.2 maximum_bitcast_fusion.8
  108.0 4.9 %copy.65 = bf16[2,192,8,2,64]{4,3,2,1,0:T(2,128)(2,1)} copy(bf16[2,192,8,2,64]{1,4,2,3,0:T(8,128)(2,1)} %maximum_bitcast_fusion.8) | data formatting | bytes 1572864 | tf_op jit(solution)/shard_map/reshape | solution.py:346
  112.9 4.2 %reshape.266.weights_ref = bf16[384,1024]{1,0:T(8,128)(2,1)S(1)} reshape(bf16[2,192,8,2,64]{4,3,2,1,0:T(2,128)(2,1)} %copy.65) | data formatting | bytes 1572864 | tf_op jit(solution)/shard_map/reshape | solution.py:346
  117.1 0.6 dynamic_slice.8
  117.7 0.1 copy.43
  118.5 0.6 gather_fusion.2
  119.0 0.6 gather_fusion
  119.6 1.7 form_beams.3
  121.3 0.9 copy-done
  122.2 27.5 %all-to-all-done.arrived_ref = bf16[8,8,128,128]{3,2,1,0:T(8,128)(2,1)} async-done(((bf16[8,8,128,128]{3,2,1,0:T(8,128)(2,1)}), bf16[8,8,128,128]{3,2,1,0:T(8,128)(2,1)}, u32[]{:S(2)}, u32[]{:S(2)}) %all-to-all-start) | async-done | bytes 2097184 | tf_op jit(solution)/shard_map/all_to_all | solution.py:357
  149.7 3.5 %all-to-all-start.4 = ((bf16[4,2,384,128]{3,2,1,0:T(8,128)(2,1)}), bf16[4,2,384,128]{3,2,1,0:T(8,128)(2,1)S(1)}, u32[]{:S(2)}, u32[]{:S(2)}) async-start(bf16[4,2,384,128]{3,2,1,0:T(8,128)(2,1)} %bitcast.65), calls=%async_computation.4 | async-start | bytes 1572864 | tf_op jit(solution)/shard_map/all_to_all | solution.py:362
  153.3 4.2 %form_beams.2 = bf16[8,384,128]{2,1,0:T(8,128)(2,1)} custom-call(bf16[384,1024]{1,0:T(8,128)(2,1)S(1)} %reshape.266.weights_ref, bf16[8,8,128,128]{3,2,1,0:T(8,128)(2,1)} %all-to-all-done.arrived_ref), custom_call_target="tpu_custom_call" | custom-call | flops 805306368 | bytes 2097152 | tf_op jit(solution)/shard_map/form_beams/pallas_call | solution.py:115
  157.6 5.6 %all-to-all-done.4.beams_ref = bf16[4,2,384,128]{3,2,1,0:T(8,128)(2,1)S(1)} async-done(((bf16[4,2,384,128]{3,2,1,0:T(8,128)(2,1)}), bf16[4,2,384,128]{3,2,1,0:T(8,128)(2,1)S(1)}, u32[]{:S(2)}, u32[]{:S(2)}) %all-to-all-start.4) | async-done | bytes 786464 | tf_op jit(solution)/shard_map/all_to_all | solution.py:362
  163.2 4.5 %all-to-all-start.1 = ((bf16[4,2,384,128]{3,2,1,0:T(8,128)(2,1)}), bf16[4,2,384,128]{3,2,1,0:T(8,128)(2,1)S(1)}, u32[]{:S(2)}, u32[]{:S(2)}) async-start(bf16[4,2,384,128]{3,2,1,0:T(8,128)(2,1)} %bitcast.23), calls=%async_computation.1 | async-start | bytes 1572864 | tf_op jit(solution)/shard_map/all_to_all | solution.py:362
  167.8 24.7 %factor_slots.3 = bf16[4,4,96,384]{3,2,1,0:T(8,128)(2,1)} custom-call(s32[4,192]{1,0:T(4,128)S(1)} %broadcast_select_fusion.2.pivots_ref, bf16[4,2,384,128]{3,2,1,0:T(8,128)(2,1)S(1)} %all-to-all-done.4.beams_ref), custom_call_target="tpu_custom_call" | custom-call | flops 23040000000 | bytes 786432 | tf_op jit(solution)/shard_map/factor_slots/pallas_call | solution.py:282
  192.4 3.5 %all-to-all-start.5 = ((bf16[4,4,96,384]{3,2,1,0:T(8,128)(2,1)}), bf16[4,4,96,384]{3,2,1,0:T(8,128)(2,1)S(1)}, u32[]{:S(2)}, u32[]{:S(2)}) async-start(bf16[4,4,96,384]{3,2,1,0:T(8,128)(2,1)} %factor_slots.3), calls=%async_computation.5 | async-start | bytes 2359296 | tf_op jit(solution)/shard_map/all_to_all | solution.py:366
  196.0 24.7 %factor_slots.2 = bf16[4,4,96,384]{3,2,1,0:T(8,128)(2,1)} custom-call(s32[4,192]{1,0:T(4,128)S(1)} %broadcast_select_fusion.3.pivots_ref, bf16[4,2,384,128]{3,2,1,0:T(8,128)(2,1)S(1)} %all-to-all-done.1.beams_ref), custom_call_target="tpu_custom_call" | custom-call | flops 23040000000 | bytes 786432 | tf_op jit(solution)/shard_map/factor_slots/pallas_call | solution.py:282
  220.7 3.5 %all-to-all-start.2 = ((bf16[4,4,96,384]{3,2,1,0:T(8,128)(2,1)}), bf16[4,4,96,384]{3,2,1,0:T(8,128)(2,1)S(1)}, u32[]{:S(2)}, u32[]{:S(2)}) async-start(bf16[4,4,96,384]{3,2,1,0:T(8,128)(2,1)} %factor_slots.2), calls=%async_computation.2 | async-start | bytes 2359296 | tf_op jit(solution)/shard_map/all_to_all | solution.py:366
  224.2 0.6 dynamic_slice.7
  224.8 0.6 iota_compare_fusion.1
  225.5 13.8 %all-to-all-done.2 = bf16[4,4,96,384]{3,2,1,0:T(8,128)(2,1)S(1)} async-done(((bf16[4,4,96,384]{3,2,1,0:T(8,128)(2,1)}), bf16[4,4,96,384]{3,2,1,0:T(8,128)(2,1)S(1)}, u32[]{:S(2)}, u32[]{:S(2)}) %all-to-all-start.2) | async-done | bytes 1179680 | tf_op jit(solution)/shard_map/all_to_all | solution.py:366
  239.2 0.3 pad_maximum_fusion
  239.5 3.0 %convert_select_fusion = f32[32,96,384]{2,1,0:T(8,128)} fusion(bf16[4,8,96,384]{3,2,1,0:T(8,128)(2,1)S(1)} %pad_maximum_fusion, pred[32]{0:T(512)(128)(4,1)S(1)} %iota_compare_fusion.1), kind=kLoop, calls=%fused_computation.13 | loop fusion | flops 2359296 | bytes 7077920 | tf_op jit(solution)/shard_map/jit(_where)/select_n | solution.py:370
  (48 shorter events, 1.1 us)
Async XLA Ops:
  4.4 2.0 copy-start.1
  6.4 5.3 %copy-start.6 = (s32[8]{0:T(128)S(1)}, s32[8]{0:T(128)}, u32[]{:S(2)}) copy-start(s32[8]{0:T(128)} %param.14) | copy-start | bytes 100
  6.4 5.7 %copy-start.4 = (s32[128,64]{0,1:T(8,128)S(1)}, s32[128,64]{0,1:T(8,128)}, u32[]{:S(2)}) copy-start(s32[128,64]{0,1:T(8,128)} %param.15) | copy-start | bytes 98308
  6.6 7.3 %copy-start.5 = (f32[2,64]{1,0:T(2,128)S(1)}, f32[2,64]{1,0:T(2,128)}, u32[]{:S(2)}) copy-start(f32[2,64]{1,0:T(2,128)} %param.11) | copy-start | bytes 1540
  9.3 28.2 %collective-permute-start = (bf16[2,64,63,128]{3,1,2,0:T(8,128)(2,1)}, bf16[2,64,63,128]{3,1,2,0:T(8,128)(2,1)}, u32[]{:S(2)}, u32[]{:S(2)}) collective-permute-start(bf16[2,64,63,128]{3,1,2,0:T(8,128)(2,1)} %copy.52), channel_id=1, source_target_pairs={{1,0},{2,1},{3,2},{5,4},{6,5},{7,6},{9,8},{10,9},{11,10},{13,12},{... | collective-permute-start | bytes 6193160 | tf_op jit(solution)/shard_map/ppermute | solution.py:22
  65.8 36.0 %all-to-all-start.3 = ((bf16[8,8,128,128]{3,2,1,0:T(8,128)(2,1)}), bf16[8,8,128,128]{3,2,1,0:T(8,128)(2,1)S(1)}, u32[]{:S(2)}, u32[]{:S(2)}) async-start(bf16[8,8,128,128]{3,2,1,0:T(8,128)(2,1)} %select_gates.3), calls=%async_computation.3 | async-start | bytes 4194304 | tf_op jit(solution)/shard_map/all_to_all | solution.py:357
  72.3 34.1 %copy-start.2 = (bf16[2,512,192]{1,2,0:T(8,128)(2,1)S(1)}, bf16[2,512,192]{1,2,0:T(8,128)(2,1)}, u32[]{:S(2)}) copy-start(bf16[2,512,192]{1,2,0:T(8,128)(2,1)} %param.12) | copy-start | bytes 1179652
  101.8 47.8 %all-to-all-start = ((bf16[8,8,128,128]{3,2,1,0:T(8,128)(2,1)}), bf16[8,8,128,128]{3,2,1,0:T(8,128)(2,1)}, u32[]{:S(2)}, u32[]{:S(2)}) async-start(bf16[8,8,128,128]{3,2,1,0:T(8,128)(2,1)} %select_gates.2), calls=%async_computation | async-start | bytes 4194304 | tf_op jit(solution)/shard_map/all_to_all | solution.py:357
  106.7 11.0 %copy-start.3 = (s32[128,192]{0,1:T(8,128)S(1)}, s32[128,192]{0,1:T(8,128)}, u32[]{:S(2)}) copy-start(s32[128,192]{0,1:T(8,128)} %param.13) | copy-start | bytes 294916
  121.3 0.9 copy-start
  149.7 13.5 %all-to-all-start.4 = ((bf16[4,2,384,128]{3,2,1,0:T(8,128)(2,1)}), bf16[4,2,384,128]{3,2,1,0:T(8,128)(2,1)S(1)}, u32[]{:S(2)}, u32[]{:S(2)}) async-start(bf16[4,2,384,128]{3,2,1,0:T(8,128)(2,1)} %bitcast.65), calls=%async_computation.4 | async-start | bytes 1572864 | tf_op jit(solution)/shard_map/all_to_all | solution.py:362
  163.2 29.2 %all-to-all-start.1 = ((bf16[4,2,384,128]{3,2,1,0:T(8,128)(2,1)}), bf16[4,2,384,128]{3,2,1,0:T(8,128)(2,1)S(1)}, u32[]{:S(2)}, u32[]{:S(2)}) async-start(bf16[4,2,384,128]{3,2,1,0:T(8,128)(2,1)} %bitcast.23), calls=%async_computation.1 | async-start | bytes 1572864 | tf_op jit(solution)/shard_map/all_to_all | solution.py:362
  192.4 28.3 %all-to-all-start.5 = ((bf16[4,4,96,384]{3,2,1,0:T(8,128)(2,1)}), bf16[4,4,96,384]{3,2,1,0:T(8,128)(2,1)S(1)}, u32[]{:S(2)}, u32[]{:S(2)}) async-start(bf16[4,4,96,384]{3,2,1,0:T(8,128)(2,1)} %factor_slots.3), calls=%async_computation.5 | async-start | bytes 2359296 | tf_op jit(solution)/shard_map/all_to_all | solution.py:366
  220.7 18.5 %all-to-all-start.2 = ((bf16[4,4,96,384]{3,2,1,0:T(8,128)(2,1)}), bf16[4,4,96,384]{3,2,1,0:T(8,128)(2,1)S(1)}, u32[]{:S(2)}, u32[]{:S(2)}) async-start(bf16[4,4,96,384]{3,2,1,0:T(8,128)(2,1)} %factor_slots.2), calls=%async_computation.2 | async-start | bytes 2359296 | tf_op jit(solution)/shard_map/all_to_all | solution.py:366

commit v4 on v3

--- a/solution.py
+++ b/solution.py
@@ -48,87 +48,172 @@
     return complex_block(picked[0], picked[1])
 
 
-def select_kernel(bins_ref, gates_ref, spectrum_ref, out_ref, *, pack, groups):
-    owner = pl.program_id(0)
-    gate_rows = spectrum_ref.shape[2]
-    width = out_ref.shape[3]
+def spectrum_kernel(rows_ref, table_ref, own_ref, next_ref, out_ref, turned):
+    step = pl.program_id(0)
+    _, channels, gate_rows, pulses = own_ref.shape
+    bins, height, _ = out_ref.shape
+    width = math.gcd(channels, 2)
+    for first in range(0, channels, width):
+        span = range(first, first + width)
+        samples = []
+        for part in range(2):
+            own = jnp.concatenate([own_ref[part, c] for c in span], axis=1).astype(BF16)
+            following = jnp.concatenate([next_ref[part, c] for c in span], axis=1)
+            samples += [own, following]
+        samples = jnp.concatenate(samples, axis=0)
+        matched = jnp.dot(rows_ref[...], samples, preferred_element_type=F32).astype(BF16)
+        stacked = jnp.concatenate(
+            [
+                jnp.concatenate(
+                    [
+                        matched[
+                            part * gate_rows : (part + 1) * gate_rows, i * pulses : (i + 1) * pulses
+                        ]
+                        for part in range(2)
+                    ],
+                    axis=1,
+                )
+                for i in range(width)
+            ],
+            axis=0,
+        )
+        spectra = lax.dot_general(
+            table_ref[...], stacked, (((1,), (1,)), ((), ())), preferred_element_type=F32
+        )
+        for part in range(2):
+            for i in range(width):
+                place = part * (height // 2) + step * channels + first + i
+                turned[pl.ds(place, bins, stride=height), :] = spectra[
+                    part * bins : (part + 1) * bins, i * gate_rows : (i + 1) * gate_rows
+                ]
+
+    @pl.when(step == pl.num_programs(0) - 1)
+    def _():
+        out_ref[...] = turned[...].astype(BF16).reshape(out_ref.shape)
+
+
+def form_spectrum(rows, table, raw_echo, next_rows, chunk, chunks):
+    _, ch_local, gate_rows, pulses = raw_echo.shape
+    channels = ch_local // chunks
+    step = math.gcd(channels, 4)
+    steps = channels // step
+    height = 2 * channels
+    bins = table.shape[0] // 2
+    return pl.pallas_call(
+        spectrum_kernel,
+        out_shape=jax.ShapeDtypeStruct((bins, height, gate_rows), BF16),
+        grid=(steps,),
+        in_specs=[
+            pl.BlockSpec(rows.shape, lambda i: (0, 0)),
+            pl.BlockSpec(table.shape, lambda i: (0, 0)),
+            pl.BlockSpec((2, step, gate_rows, pulses), lambda i: (0, chunk * steps + i, 0, 0)),
+            pl.BlockSpec((2, step) + next_rows.shape[2:], lambda i: (0, i, 0, 0)),
+        ],
+        out_specs=pl.BlockSpec((bins, height, gate_rows), lambda i: (0, 0, 0)),
+        scratch_shapes=[pltpu.VMEM((bins * height, gate_rows), F32)],
+        compiler_params=PARAMS,
+        cost_estimate=pl.CostEstimate(
+            flops=2 * rows.size * channels * pulses + 2 * table.size * channels * gate_rows,
+            bytes_accessed=8 * channels * gate_rows * pulses,
+            transcendentals=0,
+        ),
+        name="form_spectrum",
+    )(rows, table, raw_echo, next_rows)
+
+
+def select_kernel(bins_ref, gates_ref, *refs, pack):
+    *spectrum_refs, out_ref = refs
+    gate_rows = spectrum_refs[0].shape[2]
+    owners, groups, rows, width = out_ref.shape
     gate_index = lax.broadcasted_iota(jnp.int32, (gate_rows, width), 0)
     part_index = lax.broadcasted_iota(jnp.int32, (gate_rows, width), 1) // (width // pack)
-
     unroll = math.gcd(groups, 4)
     masks = [part_index == part for part in range(pack)]
 
     def some_groups(step, carry):
+        owner = step // (groups // unroll)
+        lead = step % (groups // unroll) * unroll
         for inner in range(unroll):
             group = step * unroll + inner
-            hit = gate_index == gates_ref[0, pl.ds(group, 1), :]
-            total = jnp.zeros(out_ref.shape[2:], F32)
+            hit = gate_index == gates_ref[pl.ds(group, 1), :]
+            total = jnp.zeros((rows, width), F32)
             for part in range(pack):
-                bin_index = bins_ref[(owner * groups + group) * pack + part]
+                bin_index = bins_ref[group * pack + part]
                 chooser = jnp.where(hit & masks[part], 1.0, 0.0).astype(BF16)
-                total += jnp.dot(spectrum_ref[bin_index], chooser, preferred_element_type=F32)
-            out_ref[0, group] = total.astype(BF16)
+                spectra = jnp.concatenate([ref[bin_index] for ref in spectrum_refs], axis=0)
+                total += jnp.dot(spectra, chooser, preferred_element_type=F32)
+            out_ref[owner, lead + inner] = total.astype(BF16)
         return carry
 
-    lax.fori_loop(0, groups // unroll, some_groups, 0)
-
-
-def select_gates(spectrum, slot_bins, slot_gates, owners, pack):
-    bins, rows, gate_rows = spectrum.shape
+    lax.fori_loop(0, owners * groups // unroll, some_groups, 0)
+
+
+def select_gates(spectra, slot_bins, slot_gates, owners, pack):
+    rows = sum(spectrum.shape[1] for spectrum in spectra)
+    gate_rows = spectra[0].shape[2]
     groups = slot_bins.shape[0] // owners // pack
     width = slot_gates.shape[-1]
     return pl.pallas_call(
-        functools.partial(select_kernel, pack=pack, groups=groups),
+        functools.partial(select_kernel, pack=pack),
         out_shape=jax.ShapeDtypeStruct((owners, groups, rows, width), BF16),
-        grid_spec=pltpu.PrefetchScalarGridSpec(
-            num_scalar_prefetch=1,
-            grid=(owners,),
-            in_specs=[
-                pl.BlockSpec((1, groups, width), lambda i, b: (i, 0, 0)),
-                pl.BlockSpec((bins, rows, gate_rows), lambda i, b: (0, 0, 0)),
-            ],
-            out_specs=pl.BlockSpec((1, groups, rows, width), lambda i, b: (i, 0, 0, 0)),
-        ),
+        in_specs=[pl.BlockSpec(memory_space=pltpu.SMEM)]
+        + [pl.BlockSpec(memory_space=pltpu.VMEM)] * (1 + len(spectra)),
+        out_specs=pl.BlockSpec(memory_space=pltpu.VMEM),
         compiler_params=PARAMS,
         cost_estimate=pl.CostEstimate(
             flops=2 * slot_bins.shape[0] * rows * gate_rows * width,
-            bytes_accessed=spectrum.size * 2,
+            bytes_accessed=owners * groups * rows * width * 2,
             transcendentals=0,
         ),
         name="select_gates",
-    )(slot_bins, slot_gates.reshape(owners, groups, width), spectrum)
-
-
-def beam_kernel(weights_ref, arrived_ref, out_ref):
+    )(slot_bins, slot_gates, *spectra)
+
+
+def beam_kernel(me_ref, weights_ref, arrived_ref, *out_refs):
     sources, groups, rows, width = arrived_ref.shape
-    packed = jnp.concatenate(
-        [arrived_ref[:, g].reshape(sources * rows, width) for g in range(groups)], axis=1
-    )
-    beams = jnp.dot(weights_ref[...], packed, preferred_element_type=F32).astype(BF16)
-    for g in range(groups):
-        out_ref[g] = beams[:, g * width : (g + 1) * width]
-
-
-def form_beams(arrived, weights):
-    sources, groups, rows, width = arrived.shape
-    step = 2 if groups % 2 == 0 else 1
+    ranges = len(out_refs)
+    share = groups // ranges
+    for shift, out_ref in enumerate(out_refs):
+        lead = lax.rem(me_ref[0] + shift, ranges) * share
+        packed = jnp.concatenate(
+            [arrived_ref[:, lead + g].reshape(sources * rows, width) for g in range(share)], axis=1
+        )
+        beams = lax.dot_general(
+            weights_ref[...], packed, (((0,), (0,)), ((), ())), preferred_element_type=F32
+        ).astype(BF16)
+        for g in range(share):
+            out_ref[g] = beams[:, g * width : (g + 1) * width]
+
+
+def form_beams(arrived, weights, me, ranges):
+    _, groups, _, width = arrived.shape
+    shape = (groups // ranges, weights.shape[1], width)
     return pl.pallas_call(
         beam_kernel,
-        out_shape=jax.ShapeDtypeStruct((groups, weights.shape[0], width), BF16),
-        grid=(groups // step,),
+        out_shape=[jax.ShapeDtypeStruct(shape, BF16)] * ranges,
         in_specs=[
-            pl.BlockSpec(weights.shape, lambda i: (0, 0)),
-            pl.BlockSpec((sources, step, rows, width), lambda i: (0, i, 0, 0)),
+            pl.BlockSpec(memory_space=pltpu.SMEM),
+            pl.BlockSpec(memory_space=pltpu.VMEM),
+            pl.BlockSpec(memory_space=pltpu.VMEM),
         ],
-        out_specs=pl.BlockSpec((step, weights.shape[0], width), lambda i: (i, 0, 0)),
+        out_specs=[pl.BlockSpec(memory_space=pltpu.VMEM)] * ranges,
         compiler_params=PARAMS,
         cost_estimate=pl.CostEstimate(
-            flops=2 * arrived.size * weights.shape[0],
+            flops=2 * arrived.size * weights.shape[1],
             bytes_accessed=arrived.size * 2,
             transcendentals=0,
         ),
         name="form_beams",
-    )(weights, arrived)
+    )(me, weights, arrived)
+
+
+def exchange(arrays, axis):
+    count = len(arrays)
+    moved = [arrays[0]]
+    for shift in range(1, count):
+        pairs = [(i, (i + shift) % count) for i in range(count)]
+        moved.append(lax.ppermute(arrays[shift], axis, pairs))
+    return moved
 
 
 def split_terms(array):
@@ -199,8 +284,9 @@
     return rows
 
 
-def factor_kernel(pivots_ref, beams_ref, out_ref, panel_ref, *work, pack, count_rows):
-    ranges, groups = beams_ref.shape[:2]
+def factor_kernel(me_ref, pivots_ref, *refs, ranges, pack, count_rows):
+    beams_refs, out_refs = refs[:ranges], refs[ranges : 2 * ranges]
+    panel_ref, *work = refs[2 * ranges :]
     slots = len(work)
     order = work[0].shape[0]
     height = panel_ref.shape[1] // PANEL
@@ -211,7 +297,7 @@
     for slot in range(slots):
         group, part = divmod(slot, pack)
         work[slot][...] = loaded_covariance(
-            [beams_ref[r, group] for r in range(ranges)],
+            [ref[group] for ref in beams_refs],
             pivots_ref[slot : slot + 1, :],
             part,
             pack,
@@ -265,36 +351,65 @@
                 ready = work[slot][start:after, after:]
                 work[slot][after:, after:] -= cross_product(ready, ready)
 
-    owners, _, share, _ = out_ref.shape
-    for slot in range(slots):
-        for r in range(owners):
-            row = lax.broadcasted_iota(jnp.int32, (share, order), 0) + r * share
-            col = lax.broadcasted_iota(jnp.int32, (share, order), 1)
-            piece = work[slot][r * share : (r + 1) * share]
-            out_ref[r, slot] = jnp.where(col >= row, piece, 0.0).astype(out_ref.dtype)
-
-
-def factor_slots(beams, pivot_rows, pack, count_rows):
-    ranges = beams.shape[0]
+    share = order // ranges
+    row = lax.broadcasted_iota(jnp.int32, (share, order), 0)
+    col = lax.broadcasted_iota(jnp.int32, (share, order), 1)
+    for shift, out_ref in enumerate(out_refs):
+        lead = pl.multiple_of(lax.rem(me_ref[0] + shift, ranges) * share, math.gcd(share, 16))
+        upper = col >= row + lead
+        for slot in range(slots):
+            piece = work[slot][pl.ds(lead, share), :]
+            out_ref[slot] = jnp.where(upper, piece, 0.0).astype(out_ref.dtype)
+
+
+def factor_slots(beams, pivot_rows, me, pack, count_rows):
+    ranges = len(beams)
     slots, dof = pivot_rows.shape
     order = 2 * dof
     height = -(-slots // 8) * 8
     return pl.pallas_call(
-        functools.partial(factor_kernel, pack=pack, count_rows=count_rows),
-        out_shape=jax.ShapeDtypeStruct((ranges, slots, order // ranges, order), BF16),
-        in_specs=[
-            pl.BlockSpec(memory_space=pltpu.VMEM),
-            pl.BlockSpec(memory_space=pltpu.VMEM),
-        ],
-        out_specs=pl.BlockSpec(memory_space=pltpu.VMEM),
+        functools.partial(factor_kernel, ranges=ranges, pack=pack, count_rows=count_rows),
+        out_shape=[jax.ShapeDtypeStruct((slots, order // ranges, order), BF16)] * ranges,
+        in_specs=[pl.BlockSpec(memory_space=pltpu.SMEM)]
+        + [pl.BlockSpec(memory_space=pltpu.VMEM)] * (1 + ranges),
+        out_specs=[pl.BlockSpec(memory_space=pltpu.VMEM)] * ranges,
         scratch_shapes=[pltpu.VMEM((order // LANES, PANEL * height, LANES), F32)]
         + [pltpu.VMEM((order, order), F32) for _ in range(slots)],
         compiler_params=PARAMS,
         cost_estimate=pl.CostEstimate(
-            flops=order * 60_000_000, bytes_accessed=beams.size * 2, transcendentals=0
+            flops=order * 60_000_000,
+            bytes_accessed=ranges * beams[0].size * 2,
+            transcendentals=0,
         ),
         name="factor_slots",
-    )(pivot_rows, beams)
+    )(me, pivot_rows, *beams)
+
+
+def place_kernel(place_ref, *refs, ranges, parts):
+    *in_refs, out_ref = refs
+    share_slots = out_ref.shape[0] // ranges
+    for shift in range(ranges):
+        lead = lax.rem(place_ref[0] + (ranges - shift), ranges) * share_slots
+        for index, (first, count) in enumerate(parts):
+            ref = in_refs[index * ranges + shift]
+            for i in range(count):
+                slot = lead + first + i
+                keep = jnp.broadcast_to(slot < place_ref[1], out_ref.shape[1:])
+                out_ref[slot] = jnp.where(keep, ref[i].astype(F32), 0.0)
+
+
+def place_rows(place, done, parts, most_slots):
+    ranges = len(done[0])
+    arrays = [array for part in done for array in part]
+    return pl.pallas_call(
+        functools.partial(place_kernel, ranges=ranges, parts=parts),
+        out_shape=jax.ShapeDtypeStruct((most_slots,) + arrays[0].shape[1:], F32),
+        in_specs=[pl.BlockSpec(memory_space=pltpu.SMEM)]
+        + [pl.BlockSpec(memory_space=pltpu.VMEM)] * len(arrays),
+        out_specs=pl.BlockSpec(memory_space=pltpu.VMEM),
+        compiler_params=PARAMS,
+        name="place_rows",
+    )(place, *arrays)
 
 
 def slot_parts(share_slots, pack):
@@ -315,35 +430,40 @@
     share_slots = most_slots // ranges
     pack = max(1, min(LANES // train_local, share_slots))
 
-    echo = raw_echo.astype(BF16)
-    next_rows = shifted(echo[:, :, : tap_count - 1, :], "rng", -1)
-    extended = jnp.concatenate([echo, next_rows], axis=2)
-    matched = jnp.einsum(
-        "abji,bcip->acjp",
-        filter_rows(replica, gate_rows).astype(BF16),
-        extended,
-        preferred_element_type=F32,
-    ).astype(BF16)
-    spectrum = jnp.einsum(
-        "abpk,bcgp->kacg",
-        doppler_table(pulse_count).astype(BF16),
-        matched,
-        preferred_element_type=F32,
-    ).astype(BF16)
-    spectrum = spectrum.reshape(pulse_count, 2 * ch_local, gate_rows)
+    chunks = max(1, min(4, ch_local // 16))
+    chunk_rows = ch_local // chunks
+    rim = -(-(tap_count - 1) // 16) * 16
+    filters = filter_rows(replica, gate_rows)
+    filters = jnp.pad(filters, ((0, 0), (0, 0), (0, 0), (0, rim - tap_count + 1)))
+    filters = filters.transpose(0, 2, 1, 3).reshape(2 * gate_rows, -1).astype(BF16)
+    table = doppler_table(pulse_count).transpose(0, 3, 1, 2)
+    table = table.reshape(2 * pulse_count, -1).astype(BF16)
+    following = [
+        shifted(raw_echo[:, c * chunk_rows : (c + 1) * chunk_rows, :rim, :].astype(BF16), "rng", -1)
+        for c in range(chunks)
+    ]
+    spectra = [
+        form_spectrum(filters, table, raw_echo, following[c], c, chunks) for c in range(chunks)
+    ]
 
     starts = jnp.cumsum(owner_counts, dtype=jnp.int32) - owner_counts
     me = lax.axis_index("dop")
     my_start = lax.dynamic_index_in_dim(starts, me, 0, keepdims=False)
     my_count = lax.dynamic_index_in_dim(owner_counts, me, 0, keepdims=False)
-    my_lead = lax.axis_index("rng") * share_slots
+    my_range = lax.axis_index("rng").astype(jnp.int32)
+    my_lead = my_range * share_slots
     local_gates = train_gates % gate_rows
     count_rows = float(train_local * ranges)
 
     dof = beam_weights.shape[2]
-    weights = complex_block(beam_weights[0], beam_weights[1])
-    weights = weights.reshape(2, 2, owners, ch_local, dof).transpose(0, 4, 2, 1, 3)
-    weights = weights.reshape(2 * dof, -1)
+    real_part, imag_part = beam_weights.reshape(2, owners, chunks, chunk_rows, dof)
+    weights = jnp.stack(
+        [
+            jnp.concatenate([real_part, -imag_part], axis=3),
+            jnp.concatenate([imag_part, real_part], axis=3),
+        ],
+        axis=2,
+    ).reshape(-1, 2 * dof)
 
     lead_slots = jnp.arange(ranges, dtype=jnp.int32) * share_slots
     parts = slot_parts(share_slots, pack)
@@ -353,21 +473,16 @@
         slots = (lead_slots[:, None] + some[None, :]).reshape(-1)
         bins = jnp.minimum(starts[:, None] + slots[None, :], pulse_count - 1).reshape(-1)
         gates = jnp.take(local_gates, bins, axis=0).reshape(-1, pack * train_local)
-        outgoing = select_gates(spectrum, bins, gates, owners, pack)
+        outgoing = select_gates(spectra, bins, gates, owners, pack)
         sent.append(lax.all_to_all(outgoing, "dop", split_axis=0, concat_axis=0, tiled=True))
     done = []
     for (first, count), arrived in zip(parts, sent):
-        beams = form_beams(arrived, weights)
-        beams = beams.reshape(ranges, -1, 2 * dof, beams.shape[-1])
-        beams = lax.all_to_all(beams, "rng", split_axis=0, concat_axis=0, tiled=True)
+        beams = exchange(form_beams(arrived, weights, my_range[None], ranges), "rng")
         bins = my_start + my_lead + first + jnp.arange(count, dtype=jnp.int32)
         my_pivots = jnp.take(pivots, jnp.minimum(bins, pulse_count - 1), axis=0)
-        factors = factor_slots(beams, my_pivots, pack, count_rows)
-        done.append(lax.all_to_all(factors, "rng", split_axis=0, concat_axis=0, tiled=True))
-    rows_done = jnp.concatenate(done, axis=1)
-    rows_done = rows_done.reshape(most_slots, *rows_done.shape[2:])
-    filled = jnp.arange(most_slots, dtype=jnp.int32) < my_count
-    return jnp.where(filled[:, None, None], rows_done.astype(F32), 0.0)
+        factors = factor_slots(beams, my_pivots, my_range[None], pack, count_rows)
+        done.append(exchange(factors, "rng"))
+    return place_rows(jnp.stack([my_range, my_count]), done, parts, most_slots)
 
 
 def solution(mesh):

time: 244 us -> 234 us (0.959)
  local copies, waits for them, and re-layouts: 34.4 us -> 12.9 us
  Pallas kernels: 71 us -> 87.9 us
  matrix products: 9.79 us -> 0 us
  starting transfers between devices: 27.4 us -> 35.2 us
  waiting for transfers between devices: 88.7 us -> 85.4 us
    all_to_all x2, waiting for transfers between devices: 49.1 us -> 73.5 us  [local(): lax.all_to_all(outgoing, 'dop', split_axis=0, concat_axis=0, tiled=True)]
    ppermute x1 -> x4, waiting for transfers between devices: 20.1 us -> 0.01 us  [shifted(): return lax.ppermute(array, axis, pairs)]
    all_to_all x4 -> x0, waiting for transfers between devices: 19.4 us -> none  [the longest x2 13.8 us: local(): lax.all_to_all(factors, 'rng', split_axis=0, concat_axis=0, tiled=True)]
    pallas_call x6 -> x11, Pallas kernels: 71 us -> 87.9 us  [the longest x2 48.4 us: factor_slots(): pl.pallas_call(functools.partial(factor_kernel, ranges=ranges, pack=pack,...]
    ppermute x0 -> x12, starting transfers between devices: none -> 16.7 us  [exchange(): moved.append(lax.ppermute(arrays[shift], axis, pairs))]
    all_to_all x4 -> x0, starting transfers between devices: 15.1 us -> none  [the longest x2 8.03 us: local(): lax.all_to_all(beams, 'rng', split_axis=0, concat_axis=0, tiled=True)]
    ppermute x0 -> x12, waiting for transfers between devices: none -> 11.9 us  [exchange(): moved.append(lax.ppermute(arrays[shift], axis, pairs))]
    dot_general x1 -> x0, matrix products: 9.79 us -> none  [local(): jnp.einsum('abpk,bcgp->kacg', doppler_table(pulse_count).astype(BF16), ma...]
  transfers between devices with their start and end apart: 7 -> 18, of which waited for: 5 -> 5; matrix products, arithmetic and copies ran while one was open for 8% -> 5% of each run, Pallas kernels for 26% -> 32%
where the time goes in v4:
time: 234 us; the launch traced here: 233 us
  Pallas kernels  87.9 us (38%)
  waiting for transfers between devices  85.4 us (36%)
  starting transfers between devices  35.2 us (15%)
  local copies, waits for them, and re-layouts  12.9 us (6%)
  other arithmetic  10.5 us (4%)
    all_to_all x2, waiting for transfers between devices, local(): lax.all_to_all(outgoing, 'dop', split_axis=0, concat_axis=0, tiled=True)  73.5 us
    pallas_call x2, Pallas kernels, factor_slots(): pl.pallas_call(functools.partial(factor_kernel, ranges=ranges, pack=pack,...  48.4 us
    pallas_call x4, Pallas kernels, form_spectrum(): pl.pallas_call(spectrum_kernel, out_shape=jax.ShapeDtypeStruct((bins, hei...  21.2 us
    ppermute x12, starting transfers between devices, exchange(): moved.append(lax.ppermute(arrays[shift], axis, pairs))  16.7 us
    ppermute x12, waiting for transfers between devices, exchange(): moved.append(lax.ppermute(arrays[shift], axis, pairs))  11.9 us
    pallas_call x2, Pallas kernels, select_gates(): pl.pallas_call(functools.partial(select_kernel, pack=pack), out_shape=jax...  10.9 us
    all_to_all x2, starting transfers between devices, local(): lax.all_to_all(outgoing, 'dop', split_axis=0, concat_axis=0, tiled=True)  10.8 us
    ppermute x4, starting transfers between devices, shifted(): return lax.ppermute(array, axis, pairs)  7.72 us
  transfers between devices with their start and end apart: 18, of which 5 were waited for; matrix products, arithmetic and copies ran while one was open for 5% of the time, Pallas kernels for 32%

profile of v4, /device:TPU:1, one launch (start us, length us, event | category | flops | bytes accessed | tf_op | source)
XLA Modules:
  0.0 233.0 jit_solution(6266449235107535886)
XLA Ops:
  0.0 4.4 %convert.40 = bf16[2,64,128,128]{3,2,1,0:T(8,128)(2,1)S(1)} convert(f32[2,64,128,128]{3,2,1,0:T(8,128)} %own_ref.7) | non-fusion elementwise | flops 2097152 | bytes 12582912 | tf_op jit(solution)/shard_map/convert.3
  4.4 1.2 fusion.13
  5.6 2.0 collective-permute-start.1
  7.6 1.9 collective-permute-start.2
  9.5 1.9 collective-permute-start.3
  11.4 1.9 collective-permute-start
  13.4 0.8 iota_compare_fusion
  14.2 2.7 %select_reduce_fusion = f32[2,128,191]{1,2,0:T(8,128)S(1)} fusion(f32[2,64]{1,0:T(2,128)S(1)} %copy-done.10, pred[128,191,64]{0,2,1:T(8,128)(4,1)S(1)} %iota_compare_fusion), kind=kLoop, calls=%fused_computation.4 | loop fusion | flops 6209792 | bytes 1760768 | tf_op jit(solution)/shard_map/reduce_sum | solution.py:47
  18.9 0.6 gather_fusion.3
  19.7 5.3 %form_spectrum.5.refs_1_ = bf16[128,32,128]{2,1,0:T(8,128)(2,1)S(1)} custom-call(bf16[256,384]{1,0:T(8,128)(2,1)S(1)} %reshape.252.rows_ref, bf16[256,256]{1,0:T(8,128)(2,1)S(1)} %bitcast.29, f32[2,64,128,128]{3,2,1,0:T(8,128)} %own_ref.7, bf16[2,16,64,128]{3,2,1,0:T(8,128)(2,1)S(1)} %collective-permute-done.1.next_ref), custom_call_target="tpu_custom_call" | custom-call | flops 671088640 | bytes 2097152 | tf_op jit(solution)/shard_map/form_spectrum/pallas_call | solution.py:102
  25.0 5.3 %form_spectrum.6.refs_2_ = bf16[128,32,128]{2,1,0:T(8,128)(2,1)S(1)} custom-call(bf16[256,384]{1,0:T(8,128)(2,1)S(1)} %reshape.252.rows_ref, bf16[256,256]{1,0:T(8,128)(2,1)S(1)} %bitcast.30, f32[2,64,128,128]{3,2,1,0:T(8,128)} %own_ref.7, bf16[2,16,64,128]{3,2,1,0:T(8,128)(2,1)S(1)} %collective-permute-done.2.next_ref), custom_call_target="tpu_custom_call" | custom-call | flops 671088640 | bytes 2097152 | tf_op jit(solution)/shard_map/form_spectrum/pallas_call | solution.py:102
  30.4 0.8 copy-done.2
  31.2 1.0 copy-done.3
  32.2 5.3 %form_spectrum.7.refs_3_ = bf16[128,32,128]{2,1,0:T(8,128)(2,1)S(1)} custom-call(bf16[256,384]{1,0:T(8,128)(2,1)S(1)} %reshape.252.rows_ref, bf16[256,256]{1,0:T(8,128)(2,1)S(1)} %bitcast.31, f32[2,64,128,128]{3,2,1,0:T(8,128)} %own_ref.7, bf16[2,16,64,128]{3,2,1,0:T(8,128)(2,1)S(1)} %copy-done.3), custom_call_target="tpu_custom_call" | custom-call | flops 671088640 | bytes 2097152 | tf_op jit(solution)/shard_map/form_spectrum/pallas_call | solution.py:102
  37.5 5.3 %form_spectrum.4.refs_0_ = bf16[128,32,128]{2,1,0:T(8,128)(2,1)S(1)} custom-call(bf16[256,384]{1,0:T(8,128)(2,1)S(1)} %reshape.252.rows_ref, bf16[256,256]{1,0:T(8,128)(2,1)S(1)} %bitcast.32, f32[2,64,128,128]{3,2,1,0:T(8,128)} %own_ref.7, bf16[2,16,64,128]{3,2,1,0:T(8,128)(2,1)} %collective-permute-done.next_ref), custom_call_target="tpu_custom_call" | custom-call | flops 671088640 | bytes 2097152 | tf_op jit(solution)/shard_map/form_spectrum/pallas_call | solution.py:102
  42.9 5.4 %select_gates.3 = bf16[8,8,128,128]{3,2,1,0:T(8,128)(2,1)} custom-call(s32[128]{0:T(128)S(1)} %min.25.bins_ref, s32[64,128]{1,0:T(8,128)S(1)} %reshape.207.gates_ref, bf16[128,32,128]{2,1,0:T(8,128)(2,1)S(1)} %form_spectrum.4.refs_0_, bf16[128,32,128]{2,1,0:T(8,128)(2,1)S(1)} %form_spectrum.5.refs_1_, bf16[128,32,128]{2,1,0:T(8,128)(2,1)S(1)} %form_spectrum.6.refs_2_, ...), custom_call_target="tpu_custom_call" | custom-call | flops 536870912 | bytes 2097152 | tf_op jit(solution)/shard_map/select_gates/pallas_call | solution.py:156
  48.3 1.0 copy-done
  49.3 7.0 %all-to-all-start.1 = ((bf16[8,8,128,128]{3,2,1,0:T(8,128)(2,1)}), bf16[8,8,128,128]{3,2,1,0:T(8,128)(2,1)}, u32[]{:S(2)}, u32[]{:S(2)}) async-start(bf16[8,8,128,128]{3,2,1,0:T(8,128)(2,1)} %select_gates.3), calls=%async_computation.1 | async-start | bytes 4194304 | tf_op jit(solution)/shard_map/all_to_all | solution.py:477
  56.4 0.6 gather_fusion.1
  57.2 1.2 copy-done.1
  58.5 5.4 %select_gates.2 = bf16[8,8,128,128]{3,2,1,0:T(8,128)(2,1)} custom-call(s32[128]{0:T(128)S(1)} %min.22.bins_ref, s32[64,128]{1,0:T(8,128)S(1)} %reshape.206.gates_ref, bf16[128,32,128]{2,1,0:T(8,128)(2,1)S(1)} %copy-done.1, bf16[128,32,128]{2,1,0:T(8,128)(2,1)S(1)} %form_spectrum.5.refs_1_, bf16[128,32,128]{2,1,0:T(8,128)(2,1)S(1)} %form_spectrum.6.refs_2_, ...), custom_call_target="tpu_custom_call" | custom-call | flops 536870912 | bytes 2097152 | tf_op jit(solution)/shard_map/select_gates/pallas_call | solution.py:156
  63.9 39.7 %all-to-all-done.1.arrived_ref = bf16[8,8,128,128]{3,2,1,0:T(8,128)(2,1)} async-done(((bf16[8,8,128,128]{3,2,1,0:T(8,128)(2,1)}), bf16[8,8,128,128]{3,2,1,0:T(8,128)(2,1)}, u32[]{:S(2)}, u32[]{:S(2)}) %all-to-all-start.1) | async-done | bytes 2097184 | tf_op jit(solution)/shard_map/all_to_all | solution.py:477
  103.6 3.8 %all-to-all-start = ((bf16[8,8,128,128]{3,2,1,0:T(8,128)(2,1)}), bf16[8,8,128,128]{3,2,1,0:T(8,128)(2,1)S(1)}, u32[]{:S(2)}, u32[]{:S(2)}) async-start(bf16[8,8,128,128]{3,2,1,0:T(8,128)(2,1)} %select_gates.2), calls=%async_computation | async-start | bytes 4194304 | tf_op jit(solution)/shard_map/all_to_all | solution.py:477
  108.3 0.7 dynamic_slice.8
  108.9 1.0 copy.55
  110.7 0.6 gather_fusion.2
  111.2 0.6 gather_fusion
  111.9 3.3 %form_beams.3 = (bf16[2,384,128]{2,1,0:T(8,128)(2,1)S(1)}, bf16[2,384,128]{2,1,0:T(8,128)(2,1)}, bf16[2,384,128]{2,1,0:T(8,128)(2,1)}, bf16[2,384,128]{2,1,0:T(8,128)(2,1)S(1)}) custom-call(s32[1]{0:T(128)} %bitcast.me_ref, bf16[1024,384]{1,0:T(8,128)(2,1)S(1)} %bitcast.33, bf16[8,8,128,128]{3,2,1,0:T(8,128)(2,1)} %all-to-all-done.1.arrived_ref), custom_call_target="tpu_custom_call" | custom-call | flops 805306368 | bytes 2097152 | tf_op jit(solution)/shard_map/form_beams/pallas_call | solution.py:191
  115.2 0.7 copy-done.4
  115.9 4.9 %collective-permute-start.10 = (bf16[2,384,128]{2,1,0:T(8,128)(2,1)}, bf16[2,384,128]{2,1,0:T(8,128)(2,1)S(1)}, u32[]{:S(2)}, u32[]{:S(2)}) collective-permute-start(bf16[2,384,128]{2,1,0:T(8,128)(2,1)} %get-tuple-element.32), channel_id=1, source_target_pairs={{0,1},{1,2},{2,3},{3,0},{4,5},{5,6},{6,7},{7,4},{8,9},{9,10},{10,1... | collective-permute-start | bytes 589832 | tf_op jit(solution)/shard_map/ppermute | solution.py:215
  120.8 0.5 collective-permute-start.12
  121.4 33.8 %all-to-all-done.arrived_ref = bf16[8,8,128,128]{3,2,1,0:T(8,128)(2,1)S(1)} async-done(((bf16[8,8,128,128]{3,2,1,0:T(8,128)(2,1)}), bf16[8,8,128,128]{3,2,1,0:T(8,128)(2,1)S(1)}, u32[]{:S(2)}, u32[]{:S(2)}) %all-to-all-start) | async-done | bytes 2097184 | tf_op jit(solution)/shard_map/all_to_all | solution.py:477
  155.2 1.0 form_beams.2
  156.2 5.7 %collective-permute-start.4 = (bf16[2,384,128]{2,1,0:T(8,128)(2,1)S(1)}, bf16[2,384,128]{2,1,0:T(8,128)(2,1)S(1)}, u32[]{:S(2)}, u32[]{:S(2)}) collective-permute-start(bf16[2,384,128]{2,1,0:T(8,128)(2,1)S(1)} %get-tuple-element.24), channel_id=1, source_target_pairs={{0,1},{1,2},{2,3},{3,0},{4,5},{5,6},{6,7},{7,4},{8,9},{9,10},{10,1... | collective-permute-start | bytes 589832 | tf_op jit(solution)/shard_map/ppermute | solution.py:215
  161.9 0.5 collective-permute-start.6
  162.4 0.9 copy-done.5
  163.3 24.7 %factor_slots.3 = (bf16[4,96,384]{2,1,0:T(8,128)(2,1)S(1)}, bf16[4,96,384]{2,1,0:T(8,128)(2,1)S(1)}, bf16[4,96,384]{2,1,0:T(8,128)(2,1)S(1)}, bf16[4,96,384]{2,1,0:T(8,128)(2,1)S(1)}) custom-call(s32[1]{0:T(128)} %bitcast.me_ref, s32[4,192]{1,0:T(4,128)S(1)} %broadcast_select_fusion.2.pivots_ref, bf16[2,384,128]{2,1,0:T(8,128)(2,1)S(1)} %copy-done.5, ...), custom_call_target="tpu_custom_call" | custom-call | flops 23040000000 | bytes 786432 | tf_op jit(solution)/shard_map/factor_slots/pallas_call | solution.py:370
  188.0 1.4 collective-permute-start.13
  189.3 1.4 collective-permute-start.14
  190.8 23.7 %factor_slots.2 = (bf16[4,96,384]{2,1,0:T(8,128)(2,1)S(1)}, bf16[4,96,384]{2,1,0:T(8,128)(2,1)S(1)}, bf16[4,96,384]{2,1,0:T(8,128)(2,1)S(1)}, bf16[4,96,384]{2,1,0:T(8,128)(2,1)S(1)}) custom-call(s32[1]{0:T(128)} %bitcast.me_ref, s32[4,192]{1,0:T(4,128)S(1)} %broadcast_select_fusion.3.pivots_ref, bf16[2,384,128]{2,1,0:T(8,128)(2,1)S(1)} %get-tuple-element.23.refs_0_, ...), custom_call_target="tpu_custom_call" | custom-call | flops 23040000000 | bytes 786432 | tf_op jit(solution)/shard_map/factor_slots/pallas_call | solution.py:370
  214.5 1.8 collective-permute-start.7
  216.4 0.4 collective-permute-start.9
  216.8 0.6 dynamic_slice.7
  217.4 0.7 pad_add_fusion.place_ref
  218.1 4.4 %collective-permute-done.7.refs_1_ = bf16[4,96,384]{2,1,0:T(8,128)(2,1)S(1)} collective-permute-done((bf16[4,96,384]{2,1,0:T(8,128)(2,1)S(1)}, bf16[4,96,384]{2,1,0:T(8,128)(2,1)S(1)}, u32[]{:S(2)}, u32[]{:S(2)}) %collective-permute-start.7) | collective-permute-done | bytes 294944 | tf_op jit(solution)/shard_map/ppermute | solution.py:215
  222.5 6.8 %collective-permute-done.8.refs_2_ = bf16[4,96,384]{2,1,0:T(8,128)(2,1)S(1)} collective-permute-done((bf16[4,96,384]{2,1,0:T(8,128)(2,1)S(1)}, bf16[4,96,384]{2,1,0:T(8,128)(2,1)S(1)}, u32[]{:S(2)}, u32[]{:S(2)}) %collective-permute-start.8) | collective-permute-done | bytes 294944 | tf_op jit(solution)/shard_map/ppermute | solution.py:215
  229.4 0.6 collective-permute-done.9.refs_3_
  230.0 3.0 %place_rows.1 = f32[32,96,384]{2,1,0:T(8,128)} custom-call(s32[2]{0:T(128)S(1)} %pad_add_fusion.place_ref, bf16[4,96,384]{2,1,0:T(8,128)(2,1)S(1)} %get-tuple-element.27.refs_0_, bf16[4,96,384]{2,1,0:T(8,128)(2,1)S(1)} %collective-permute-done.7.refs_1_, bf16[4,96,384]{2,1,0:T(8,128)(2,1)S(1)} %collective-permute-done.8.refs_2_, ...), custom_call_target="tpu_custom_call" | custom-call | tf_op jit(solution)/shard_map/place_rows/pallas_call | solution.py:404
  (86 shorter events, 3.5 us)
Async XLA Ops:
  4.4 9.8 %copy-start.10 = (f32[2,64]{1,0:T(2,128)S(1)}, f32[2,64]{1,0:T(2,128)}, u32[]{:S(2)}) copy-start(f32[2,64]{1,0:T(2,128)} %param.11) | copy-start | bytes 1540
  4.4 13.4 %copy-start.11 = (s32[8]{0:T(128)S(1)}, s32[8]{0:T(128)}, u32[]{:S(2)}) copy-start(s32[8]{0:T(128)} %param.14) | copy-start | bytes 100
  4.4 13.7 %copy-start.9 = (s32[128,64]{0,1:T(8,128)S(1)}, s32[128,64]{0,1:T(8,128)}, u32[]{:S(2)}) copy-start(s32[128,64]{0,1:T(8,128)} %param.15) | copy-start | bytes 98308
  5.6 14.1 %collective-permute-start.1 = (bf16[2,16,64,128]{3,2,1,0:T(8,128)(2,1)S(1)}, bf16[2,16,64,128]{3,2,1,0:T(8,128)(2,1)S(1)}, u32[]{:S(2)}, u32[]{:S(2)}) collective-permute-start(bf16[2,16,64,128]{3,2,1,0:T(8,128)(2,1)S(1)} %get-tuple-element.41), channel_id=1, source_target_pairs={{1,0},{2,1},{3,2},{5,4},{6,5},{7,6},{9,8},{10,9},{11,10},{13,12},{... | collective-permute-start | bytes 1572872 | tf_op jit(solution)/shard_map/ppermute | solution.py:22
  7.6 17.5 %collective-permute-start.2 = (bf16[2,16,64,128]{3,2,1,0:T(8,128)(2,1)}, bf16[2,16,64,128]{3,2,1,0:T(8,128)(2,1)S(1)}, u32[]{:S(2)}, u32[]{:S(2)}) collective-permute-start(bf16[2,16,64,128]{3,2,1,0:T(8,128)(2,1)} %get-tuple-element.40), channel_id=1, source_target_pairs={{1,0},{2,1},{3,2},{5,4},{6,5},{7,6},{9,8},{10,9},{11,10},{13,12},{... | collective-permute-start | bytes 1572872 | tf_op jit(solution)/shard_map/ppermute | solution.py:22
  9.5 20.9 %collective-permute-start.3 = (bf16[2,16,64,128]{3,2,1,0:T(8,128)(2,1)}, bf16[2,16,64,128]{3,2,1,0:T(8,128)(2,1)S(1)}, u32[]{:S(2)}, u32[]{:S(2)}) collective-permute-start(bf16[2,16,64,128]{3,2,1,0:T(8,128)(2,1)} %get-tuple-element.39), channel_id=1, source_target_pairs={{1,0},{2,1},{3,2},{5,4},{6,5},{7,6},{9,8},{10,9},{11,10},{13,12},{... | collective-permute-start | bytes 1572872 | tf_op jit(solution)/shard_map/ppermute | solution.py:22
  11.4 26.1 %collective-permute-start = (bf16[2,16,64,128]{3,2,1,0:T(8,128)(2,1)}, bf16[2,16,64,128]{3,2,1,0:T(8,128)(2,1)}, u32[]{:S(2)}, u32[]{:S(2)}) collective-permute-start(bf16[2,16,64,128]{3,2,1,0:T(8,128)(2,1)} %get-tuple-element.42), channel_id=1, source_target_pairs={{1,0},{2,1},{3,2},{5,4},{6,5},{7,6},{9,8},{10,9},{11,10},{13,12},{... | collective-permute-start | bytes 1572872 | tf_op jit(solution)/shard_map/ppermute | solution.py:22
  18.3 6.8 %copy-start.6 = (s32[128,64]{1,0:T(8,128)}, s32[128,64]{1,0:T(8,128)S(1)}, u32[]{:S(2)}) copy-start(s32[128,64]{1,0:T(8,128)S(1)} %add_select_fusion.1) | copy-start | bytes 98308
  30.4 0.8 copy-start.2
  31.2 1.0 copy-start.3
  42.9 13.5 %copy-start.7 = (s32[128,64]{1,0:T(8,128)S(1)}, s32[128,64]{1,0:T(8,128)}, u32[]{:S(2)}) copy-start(s32[128,64]{1,0:T(8,128)} %copy-done.6) | copy-start | bytes 98308
  48.3 1.0 copy-start
  49.3 54.3 %all-to-all-start.1 = ((bf16[8,8,128,128]{3,2,1,0:T(8,128)(2,1)}), bf16[8,8,128,128]{3,2,1,0:T(8,128)(2,1)}, u32[]{:S(2)}, u32[]{:S(2)}) async-start(bf16[8,8,128,128]{3,2,1,0:T(8,128)(2,1)} %select_gates.3), calls=%async_computation.1 | async-start | bytes 4194304 | tf_op jit(solution)/shard_map/all_to_all | solution.py:477
  57.2 1.2 copy-start.1
  63.9 43.5 %copy-start.8 = (bf16[2,512,192]{1,2,0:T(8,128)(2,1)S(1)}, bf16[2,512,192]{1,2,0:T(8,128)(2,1)}, u32[]{:S(2)}) copy-start(bf16[2,512,192]{1,2,0:T(8,128)(2,1)} %param.12) | copy-start | bytes 1179652
  103.6 51.6 %all-to-all-start = ((bf16[8,8,128,128]{3,2,1,0:T(8,128)(2,1)}), bf16[8,8,128,128]{3,2,1,0:T(8,128)(2,1)S(1)}, u32[]{:S(2)}, u32[]{:S(2)}) async-start(bf16[8,8,128,128]{3,2,1,0:T(8,128)(2,1)} %select_gates.2), calls=%async_computation | async-start | bytes 4194304 | tf_op jit(solution)/shard_map/all_to_all | solution.py:477
  115.2 0.7 copy-start.4
  115.9 46.0 %collective-permute-start.10 = (bf16[2,384,128]{2,1,0:T(8,128)(2,1)}, bf16[2,384,128]{2,1,0:T(8,128)(2,1)S(1)}, u32[]{:S(2)}, u32[]{:S(2)}) collective-permute-start(bf16[2,384,128]{2,1,0:T(8,128)(2,1)} %get-tuple-element.32), channel_id=1, source_target_pairs={{0,1},{1,2},{2,3},{3,0},{4,5},{5,6},{6,7},{7,4},{8,9},{9,10},{10,1... | collective-permute-start | bytes 589832 | tf_op jit(solution)/shard_map/ppermute | solution.py:215
  120.8 41.6 %collective-permute-start.11 = (bf16[2,384,128]{2,1,0:T(8,128)(2,1)}, bf16[2,384,128]{2,1,0:T(8,128)(2,1)S(1)}, u32[]{:S(2)}, u32[]{:S(2)}) collective-permute-start(bf16[2,384,128]{2,1,0:T(8,128)(2,1)} %get-tuple-element.33), channel_id=1, source_target_pairs={{0,2},{1,3},{2,0},{3,1},{4,6},{5,7},{6,4},{7,5},{8,10},{9,11},{10,... | collective-permute-start | bytes 589832 | tf_op jit(solution)/shard_map/ppermute | solution.py:215
  120.8 41.6 %collective-permute-start.12 = (bf16[2,384,128]{2,1,0:T(8,128)(2,1)S(1)}, bf16[2,384,128]{2,1,0:T(8,128)(2,1)}, u32[]{:S(2)}, u32[]{:S(2)}) collective-permute-start(bf16[2,384,128]{2,1,0:T(8,128)(2,1)S(1)} %get-tuple-element.34), channel_id=1, source_target_pairs={{0,3},{1,0},{2,1},{3,2},{4,7},{5,4},{6,5},{7,6},{8,11},{9,8},{10,9... | collective-permute-start | bytes 589832 | tf_op jit(solution)/shard_map/ppermute | solution.py:215
  156.2 34.6 %collective-permute-start.4 = (bf16[2,384,128]{2,1,0:T(8,128)(2,1)S(1)}, bf16[2,384,128]{2,1,0:T(8,128)(2,1)S(1)}, u32[]{:S(2)}, u32[]{:S(2)}) collective-permute-start(bf16[2,384,128]{2,1,0:T(8,128)(2,1)S(1)} %get-tuple-element.24), channel_id=1, source_target_pairs={{0,1},{1,2},{2,3},{3,0},{4,5},{5,6},{6,7},{7,4},{8,9},{9,10},{10,1... | collective-permute-start | bytes 589832 | tf_op jit(solution)/shard_map/ppermute | solution.py:215
  161.9 28.9 %collective-permute-start.5 = (bf16[2,384,128]{2,1,0:T(8,128)(2,1)S(1)}, bf16[2,384,128]{2,1,0:T(8,128)(2,1)S(1)}, u32[]{:S(2)}, u32[]{:S(2)}) collective-permute-start(bf16[2,384,128]{2,1,0:T(8,128)(2,1)S(1)} %get-tuple-element.25), channel_id=1, source_target_pairs={{0,2},{1,3},{2,0},{3,1},{4,6},{5,7},{6,4},{7,5},{8,10},{9,11},{10,... | collective-permute-start | bytes 589832 | tf_op jit(solution)/shard_map/ppermute | solution.py:215
  161.9 28.9 %collective-permute-start.6 = (bf16[2,384,128]{2,1,0:T(8,128)(2,1)S(1)}, bf16[2,384,128]{2,1,0:T(8,128)(2,1)S(1)}, u32[]{:S(2)}, u32[]{:S(2)}) collective-permute-start(bf16[2,384,128]{2,1,0:T(8,128)(2,1)S(1)} %get-tuple-element.26), channel_id=1, source_target_pairs={{0,3},{1,0},{2,1},{3,2},{4,7},{5,4},{6,5},{7,6},{8,11},{9,8},{10,9... | collective-permute-start | bytes 589832 | tf_op jit(solution)/shard_map/ppermute | solution.py:215
  162.4 0.9 copy-start.5
  188.0 28.4 %collective-permute-start.13 = (bf16[4,96,384]{2,1,0:T(8,128)(2,1)S(1)}, bf16[4,96,384]{2,1,0:T(8,128)(2,1)S(1)}, u32[]{:S(2)}, u32[]{:S(2)}) collective-permute-start(bf16[4,96,384]{2,1,0:T(8,128)(2,1)S(1)} %get-tuple-element.36), channel_id=1, source_target_pairs={{0,1},{1,2},{2,3},{3,0},{4,5},{5,6},{6,7},{7,4},{8,9},{9,10},{10,1... | collective-permute-start | bytes 884744 | tf_op jit(solution)/shard_map/ppermute | solution.py:215
  189.3 28.8 %collective-permute-start.14 = (bf16[4,96,384]{2,1,0:T(8,128)(2,1)S(1)}, bf16[4,96,384]{2,1,0:T(8,128)(2,1)S(1)}, u32[]{:S(2)}, u32[]{:S(2)}) collective-permute-start(bf16[4,96,384]{2,1,0:T(8,128)(2,1)S(1)} %get-tuple-element.37), channel_id=1, source_target_pairs={{0,2},{1,3},{2,0},{3,1},{4,6},{5,7},{6,4},{7,5},{8,10},{9,11},{10,... | collective-permute-start | bytes 884744 | tf_op jit(solution)/shard_map/ppermute | solution.py:215
  190.8 27.3 %collective-permute-start.15 = (bf16[4,96,384]{2,1,0:T(8,128)(2,1)S(1)}, bf16[4,96,384]{2,1,0:T(8,128)(2,1)S(1)}, u32[]{:S(2)}, u32[]{:S(2)}) collective-permute-start(bf16[4,96,384]{2,1,0:T(8,128)(2,1)S(1)} %get-tuple-element.38), channel_id=1, source_target_pairs={{0,3},{1,0},{2,1},{3,2},{4,7},{5,4},{6,5},{7,6},{8,11},{9,8},{10,9... | collective-permute-start | bytes 884744 | tf_op jit(solution)/shard_map/ppermute | solution.py:215
  214.5 8.0 %collective-permute-start.7 = (bf16[4,96,384]{2,1,0:T(8,128)(2,1)S(1)}, bf16[4,96,384]{2,1,0:T(8,128)(2,1)S(1)}, u32[]{:S(2)}, u32[]{:S(2)}) collective-permute-start(bf16[4,96,384]{2,1,0:T(8,128)(2,1)S(1)} %get-tuple-element.28), channel_id=1, source_target_pairs={{0,1},{1,2},{2,3},{3,0},{4,5},{5,6},{6,7},{7,4},{8,9},{9,10},{10,1... | collective-permute-start | bytes 884744 | tf_op jit(solution)/shard_map/ppermute | solution.py:215
  216.3 13.0 %collective-permute-start.8 = (bf16[4,96,384]{2,1,0:T(8,128)(2,1)S(1)}, bf16[4,96,384]{2,1,0:T(8,128)(2,1)S(1)}, u32[]{:S(2)}, u32[]{:S(2)}) collective-permute-start(bf16[4,96,384]{2,1,0:T(8,128)(2,1)S(1)} %get-tuple-element.29), channel_id=1, source_target_pairs={{0,2},{1,3},{2,0},{3,1},{4,6},{5,7},{6,4},{7,5},{8,10},{9,11},{10,... | collective-permute-start | bytes 884744 | tf_op jit(solution)/shard_map/ppermute | solution.py:215
  216.4 13.6 %collective-permute-start.9 = (bf16[4,96,384]{2,1,0:T(8,128)(2,1)S(1)}, bf16[4,96,384]{2,1,0:T(8,128)(2,1)S(1)}, u32[]{:S(2)}, u32[]{:S(2)}) collective-permute-start(bf16[4,96,384]{2,1,0:T(8,128)(2,1)S(1)} %get-tuple-element.30), channel_id=1, source_target_pairs={{0,3},{1,0},{2,1},{3,2},{4,7},{5,4},{6,5},{7,6},{8,11},{9,8},{10,9... | collective-permute-start | bytes 884744 | tf_op jit(solution)/shard_map/ppermute | solution.py:215

commit v5 on v4

--- a/solution.py
+++ b/solution.py
@@ -36,56 +36,89 @@
     return complex_block(jnp.cos(angle_table) * norm_scale, jnp.sin(angle_table) * norm_scale)
 
 
-def filter_rows(replica, block_rows):
+def filter_kernel(replica_ref, out_ref):
+    gate_rows, span = out_ref.shape[0] // 2, replica_ref.shape[1]
+    banded = [
+        pltpu.roll(
+            jnp.broadcast_to(replica_ref[part : part + 1, :], (gate_rows, span)),
+            0,
+            1,
+            stride=1,
+            stride_axis=0,
+        )
+        for part in range(2)
+    ]
+    out_ref[:gate_rows, :span] = banded[0].astype(BF16)
+    out_ref[:gate_rows, span:] = banded[1].astype(BF16)
+    out_ref[gate_rows:, :span] = (-banded[1]).astype(BF16)
+    out_ref[gate_rows:, span:] = banded[0].astype(BF16)
+
+
+def filter_rows(replica, gate_rows):
     tap_count = replica.shape[1]
-    span_rows = block_rows + tap_count - 1
-    offsets = (
-        jnp.arange(span_rows, dtype=jnp.int32)[None, :]
-        - jnp.arange(block_rows, dtype=jnp.int32)[:, None]
-    )
-    matches = offsets[:, :, None] == jnp.arange(tap_count, dtype=jnp.int32)[None, None, :]
-    picked = jnp.sum(jnp.where(matches[None], replica[:, None, None, :], 0.0), axis=3)
-    return complex_block(picked[0], picked[1])
+    span = -(-(gate_rows + tap_count) // LANES) * LANES
+    return pl.pallas_call(
+        filter_kernel,
+        out_shape=jax.ShapeDtypeStruct((2 * gate_rows, 2 * span), BF16),
+        in_specs=[pl.BlockSpec(memory_space=pltpu.VMEM)],
+        out_specs=pl.BlockSpec(memory_space=pltpu.VMEM),
+        compiler_params=PARAMS,
+        name="filter_rows",
+    )(jnp.pad(replica, ((0, 0), (0, span - tap_count))))
+
+
+def rim_kernel(echo_ref, out_ref):
+    out_ref[...] = echo_ref[...].astype(BF16)
+
+
+def rim_rows(raw_echo, rim, chunk, chunks):
+    _, ch_local, _, pulses = raw_echo.shape
+    shape = (2, ch_local // chunks, rim, pulses)
+    return pl.pallas_call(
+        rim_kernel,
+        out_shape=jax.ShapeDtypeStruct(shape, BF16),
+        grid=(1,),
+        in_specs=[pl.BlockSpec(shape, lambda i: (0, chunk, 0, 0))],
+        out_specs=pl.BlockSpec(shape, lambda i: (0, 0, 0, 0)),
+        compiler_params=PARAMS,
+        name="rim_rows",
+    )(raw_echo)
 
 
 def spectrum_kernel(rows_ref, table_ref, own_ref, next_ref, out_ref, turned):
     step = pl.program_id(0)
     _, channels, gate_rows, pulses = own_ref.shape
     bins, height, _ = out_ref.shape
-    width = math.gcd(channels, 2)
-    for first in range(0, channels, width):
-        span = range(first, first + width)
-        samples = []
-        for part in range(2):
-            own = jnp.concatenate([own_ref[part, c] for c in span], axis=1).astype(BF16)
-            following = jnp.concatenate([next_ref[part, c] for c in span], axis=1)
-            samples += [own, following]
-        samples = jnp.concatenate(samples, axis=0)
-        matched = jnp.dot(rows_ref[...], samples, preferred_element_type=F32).astype(BF16)
-        stacked = jnp.concatenate(
-            [
-                jnp.concatenate(
-                    [
-                        matched[
-                            part * gate_rows : (part + 1) * gate_rows, i * pulses : (i + 1) * pulses
-                        ]
-                        for part in range(2)
-                    ],
-                    axis=1,
-                )
-                for i in range(width)
-            ],
-            axis=0,
-        )
-        spectra = lax.dot_general(
-            table_ref[...], stacked, (((1,), (1,)), ((), ())), preferred_element_type=F32
-        )
-        for part in range(2):
-            for i in range(width):
-                place = part * (height // 2) + step * channels + first + i
-                turned[pl.ds(place, bins, stride=height), :] = spectra[
-                    part * bins : (part + 1) * bins, i * gate_rows : (i + 1) * gate_rows
-                ]
+    rim = next_ref.shape[2]
+    span = rows_ref.shape[1] // 2
+    each = range(channels)
+    samples = []
+    for part in range(2):
+        samples += [
+            jnp.concatenate([own_ref[part, c] for c in each], axis=1).astype(BF16),
+            jnp.concatenate([next_ref[part, c] for c in each], axis=1),
+        ]
+        if span > gate_rows + rim:
+            samples.append(jnp.zeros((span - gate_rows - rim, channels * pulses), BF16))
+    samples = jnp.concatenate(samples, axis=0)
+    matched = jnp.dot(rows_ref[...], samples, preferred_element_type=F32).astype(BF16)
+    halves = [matched[:gate_rows], matched[gate_rows:]]
+    stacked = jnp.concatenate(
+        [
+            jnp.concatenate([half[:, c * pulses : (c + 1) * pulses] for half in halves], axis=1)
+            for c in each
+        ],
+        axis=0,
+    )
+    spectra = lax.dot_general(
+        table_ref[...], stacked, (((1,), (1,)), ((), ())), preferred_element_type=F32
+    )
+    for part in range(2):
+        for c in each:
+            place = part * (height // 2) + step * channels + c
+            turned[pl.ds(place, bins, stride=height), :] = spectra[
+                part * bins : (part + 1) * bins, c * gate_rows : (c + 1) * gate_rows
+            ]
 
     @pl.when(step == pl.num_programs(0) - 1)
     def _():
@@ -95,7 +128,7 @@
 def form_spectrum(rows, table, raw_echo, next_rows, chunk, chunks):
     _, ch_local, gate_rows, pulses = raw_echo.shape
     channels = ch_local // chunks
-    step = math.gcd(channels, 4)
+    step = math.gcd(channels, 8)
     steps = channels // step
     height = 2 * channels
     bins = table.shape[0] // 2
@@ -169,9 +202,9 @@
     )(slot_bins, slot_gates, *spectra)
 
 
-def beam_kernel(me_ref, weights_ref, arrived_ref, *out_refs):
+def beam_kernel(me_ref, weights_ref, arrived_ref, *refs, ranges):
+    out_refs = refs[-ranges:]
     sources, groups, rows, width = arrived_ref.shape
-    ranges = len(out_refs)
     share = groups // ranges
     for shift, out_ref in enumerate(out_refs):
         lead = lax.rem(me_ref[0] + shift, ranges) * share
@@ -185,17 +218,18 @@
             out_ref[g] = beams[:, g * width : (g + 1) * width]
 
 
-def form_beams(arrived, weights, me, ranges):
+def form_beams(arrived, weights, me, ranges, earlier):
     _, groups, _, width = arrived.shape
     shape = (groups // ranges, weights.shape[1], width)
     return pl.pallas_call(
-        beam_kernel,
+        functools.partial(beam_kernel, ranges=ranges),
         out_shape=[jax.ShapeDtypeStruct(shape, BF16)] * ranges,
         in_specs=[
             pl.BlockSpec(memory_space=pltpu.SMEM),
             pl.BlockSpec(memory_space=pltpu.VMEM),
             pl.BlockSpec(memory_space=pltpu.VMEM),
-        ],
+        ]
+        + [pl.BlockSpec(memory_space=pl.ANY)] * len(earlier),
         out_specs=[pl.BlockSpec(memory_space=pltpu.VMEM)] * ranges,
         compiler_params=PARAMS,
         cost_estimate=pl.CostEstimate(
@@ -204,7 +238,7 @@
             transcendentals=0,
         ),
         name="form_beams",
-    )(me, weights, arrived)
+    )(me, weights, arrived, *earlier)
 
 
 def exchange(arrays, axis):
@@ -260,21 +294,33 @@
     return jnp.broadcast_to(piece[:, lane : lane + 1], piece.shape)
 
 
+def refined_reciprocal(value):
+    guess = pl.reciprocal(value, approx=True)
+    return guess * (2.0 - value * guess)
+
+
 def eliminate(rows):
     scales = []
     for first in range(0, PANEL, 8):
         span = range(first, first + 8)
         small = {(i, j): lane_spread(rows[i][0], j) for i in span for j in span if j >= i}
-        for t in span:
-            pivot = small[t, t]
-            inverse = pl.reciprocal(pivot, approx=True)
-            inverse = inverse * (2.0 - pivot * inverse)
-            scales.append(lax.rsqrt(pivot))
-            for i in range(t + 1, first + 8):
-                factor = small[t, i] * inverse
+        for t in range(first, first + 8, 2):
+            u = t + 1
+            inverse = refined_reciprocal(small[t, t])
+            cross = small[t, t] * small[u, u] - small[t, u] * small[t, u]
+            second = refined_reciprocal(cross) * small[t, t]
+            scales += [lax.rsqrt(small[t, t]), lax.rsqrt(cross * inverse)]
+            factor = small[t, u] * inverse
+            for j in range(u + 1, first + 8):
+                small[u, j] = small[u, j] - factor * small[t, j]
+            rows[u] = [x - factor * y for x, y in zip(rows[u], rows[t])]
+            for i in range(u + 1, first + 8):
+                one, two = small[t, i] * inverse, small[u, i] * second
                 for j in range(i, first + 8):
-                    small[i, j] = small[i, j] - factor * small[t, j]
-                rows[i] = [x - factor * y for x, y in zip(rows[i], rows[t])]
+                    small[i, j] = small[i, j] - one * small[t, j] - two * small[u, j]
+                rows[i] = [
+                    x - one * y - two * z for x, y, z in zip(rows[i], rows[t], rows[u])
+                ]
         for t in span:
             rows[t] = [x * scales[t] for x in rows[t]]
         for i in range(first + 8, PANEL):
@@ -434,14 +480,9 @@
     chunk_rows = ch_local // chunks
     rim = -(-(tap_count - 1) // 16) * 16
     filters = filter_rows(replica, gate_rows)
-    filters = jnp.pad(filters, ((0, 0), (0, 0), (0, 0), (0, rim - tap_count + 1)))
-    filters = filters.transpose(0, 2, 1, 3).reshape(2 * gate_rows, -1).astype(BF16)
     table = doppler_table(pulse_count).transpose(0, 3, 1, 2)
     table = table.reshape(2 * pulse_count, -1).astype(BF16)
-    following = [
-        shifted(raw_echo[:, c * chunk_rows : (c + 1) * chunk_rows, :rim, :].astype(BF16), "rng", -1)
-        for c in range(chunks)
-    ]
+    following = [shifted(rim_rows(raw_echo, rim, c, chunks), "rng", -1) for c in range(chunks)]
     spectra = [
         form_spectrum(filters, table, raw_echo, following[c], c, chunks) for c in range(chunks)
     ]
@@ -475,12 +516,13 @@
         gates = jnp.take(local_gates, bins, axis=0).reshape(-1, pack * train_local)
         outgoing = select_gates(spectra, bins, gates, owners, pack)
         sent.append(lax.all_to_all(outgoing, "dop", split_axis=0, concat_axis=0, tiled=True))
-    done = []
+    done, earlier = [], []
     for (first, count), arrived in zip(parts, sent):
-        beams = exchange(form_beams(arrived, weights, my_range[None], ranges), "rng")
+        beams = exchange(form_beams(arrived, weights, my_range[None], ranges, earlier), "rng")
         bins = my_start + my_lead + first + jnp.arange(count, dtype=jnp.int32)
         my_pivots = jnp.take(pivots, jnp.minimum(bins, pulse_count - 1), axis=0)
         factors = factor_slots(beams, my_pivots, my_range[None], pack, count_rows)
+        earlier = factors[:1]
         done.append(exchange(factors, "rng"))
     return place_rows(jnp.stack([my_range, my_count]), done, parts, most_slots)
 

time: 234 us -> 204 us (0.87)
  waiting for transfers between devices: 85.4 us -> 71.2 us
  other arithmetic: 10.5 us -> 2.53 us
  Pallas kernels: 87.9 us -> 82.3 us
  local copies, waits for them, and re-layouts: 12.9 us -> 10.3 us
    all_to_all x2, waiting for transfers between devices: 73.5 us -> 44.1 us  [local(): lax.all_to_all(outgoing, 'dop', split_axis=0, concat_axis=0, tiled=True)]
    ppermute x12, waiting for transfers between devices: 11.9 us -> 27.1 us  [exchange(): moved.append(lax.ppermute(arrays[shift], axis, pairs))]
    pallas_call x4, Pallas kernels: 21.2 us -> 14.5 us  [form_spectrum(): pl.pallas_call(spectrum_kernel, out_shape=jax.ShapeDtypeStruct((bins, hei...]
    pallas_call x2 -> x7, Pallas kernels: 4.3 us -> 10.5 us  [the longest x4 6.72 us: rim_rows(): pl.pallas_call(rim_kernel, out_shape=jax.ShapeDtypeStruct(shape, BF16), g...]
    pallas_call x2, Pallas kernels: 48.4 us -> 43.4 us  [factor_slots(): pl.pallas_call(functools.partial(factor_kernel, ranges=ranges, pack=pack,...]
    another operation x6 -> x3, other arithmetic: 5.11 us -> 0.73 us
    reduce_sum x1 -> x0, other arithmetic: 2.66 us -> none  [filter_rows(): jnp.sum(jnp.where(matches[None], replica[:, None, None, :], 0.0), axis=3)]
    unnamed x29 -> x31, local copies, waits for them, and re-layouts: 7.01 us -> 5.96 us
  transfers between devices with their start and end apart: 18 -> 18, of which waited for: 5 -> 11; matrix products, arithmetic and copies ran while one was open for 5% -> 4% of each run, Pallas kernels for 32% -> 33%
where the time goes in v5:
time: 204 us; the launch traced here: 203 us
  Pallas kernels  82.3 us (40%)
  waiting for transfers between devices  71.2 us (35%)
  starting transfers between devices  35.3 us (17%)
  local copies, waits for them, and re-layouts  10.3 us (5%)
  other arithmetic  2.53 us (1%)
    all_to_all x2, waiting for transfers between devices, local(): lax.all_to_all(outgoing, 'dop', split_axis=0, concat_axis=0, tiled=True)  44.1 us
    pallas_call x2, Pallas kernels, factor_slots(): pl.pallas_call(functools.partial(factor_kernel, ranges=ranges, pack=pack,...  43.4 us
    ppermute x12, waiting for transfers between devices, exchange(): moved.append(lax.ppermute(arrays[shift], axis, pairs))  27.1 us
    ppermute x12, starting transfers between devices, exchange(): moved.append(lax.ppermute(arrays[shift], axis, pairs))  16.8 us
    pallas_call x4, Pallas kernels, form_spectrum(): pl.pallas_call(spectrum_kernel, out_shape=jax.ShapeDtypeStruct((bins, hei...  14.5 us
    pallas_call x2, Pallas kernels, select_gates(): pl.pallas_call(functools.partial(select_kernel, pack=pack), out_shape=jax...  10.9 us
    all_to_all x2, starting transfers between devices, local(): lax.all_to_all(outgoing, 'dop', split_axis=0, concat_axis=0, tiled=True)  10.6 us
    ppermute x4, starting transfers between devices, shifted(): return lax.ppermute(array, axis, pairs)  7.97 us
  transfers between devices with their start and end apart: 18, of which 11 were waited for; matrix products, arithmetic and copies ran while one was open for 4% of the time, Pallas kernels for 33%

profile of v5, /device:TPU:1, one launch (start us, length us, event | category | flops | bytes accessed | tf_op | source)
XLA Modules:
  0.0 202.7 jit_solution(948919935547144816)
XLA Ops:
  0.0 1.3 rim_rows.4
  1.3 2.0 collective-permute-start
  3.3 1.3 rim_rows.5
  4.6 1.9 collective-permute-start.1
  6.5 2.1 %rim_rows.6 = bf16[2,16,64,128]{3,2,1,0:T(8,128)(2,1)} custom-call(f32[2,64,128,128]{3,2,1,0:T(8,128)} %own_ref.7), custom_call_target="tpu_custom_call" | custom-call | tf_op jit(solution)/shard_map/rim_rows/pallas_call | solution.py:77
  8.6 2.0 %collective-permute-start.2 = (bf16[2,16,64,128]{3,2,1,0:T(8,128)(2,1)}, bf16[2,16,64,128]{3,2,1,0:T(8,128)(2,1)S(1)}, u32[]{:S(2)}, u32[]{:S(2)}) collective-permute-start(bf16[2,16,64,128]{3,2,1,0:T(8,128)(2,1)} %rim_rows.6), channel_id=1, source_target_pairs={{1,0},{2,1},{3,2},{5,4},{6,5},{7,6},{9,8},{10,9},{11,10},{13,12},{... | collective-permute-start | bytes 1572872 | tf_op jit(solution)/shard_map/ppermute | solution.py:22
  10.6 2.1 %rim_rows.7 = bf16[2,16,64,128]{3,2,1,0:T(8,128)(2,1)} custom-call(f32[2,64,128,128]{3,2,1,0:T(8,128)} %own_ref.7), custom_call_target="tpu_custom_call" | custom-call | tf_op jit(solution)/shard_map/rim_rows/pallas_call | solution.py:77
  12.7 2.0 %collective-permute-start.3 = (bf16[2,16,64,128]{3,2,1,0:T(8,128)(2,1)}, bf16[2,16,64,128]{3,2,1,0:T(8,128)(2,1)}, u32[]{:S(2)}, u32[]{:S(2)}) collective-permute-start(bf16[2,16,64,128]{3,2,1,0:T(8,128)(2,1)} %rim_rows.7), channel_id=1, source_target_pairs={{1,0},{2,1},{3,2},{5,4},{6,5},{7,6},{9,8},{10,9},{11,10},{13,12},{... | collective-permute-start | bytes 1572872 | tf_op jit(solution)/shard_map/ppermute | solution.py:22
  15.5 0.6 gather_fusion.1
  17.2 3.6 %form_spectrum.4.refs_0_ = bf16[128,32,128]{2,1,0:T(8,128)(2,1)S(1)} custom-call(bf16[256,512]{1,0:T(8,128)(2,1)S(1)} %filter_rows.1.rows_ref, bf16[256,256]{1,0:T(8,128)(2,1)S(1)} %bitcast.23, f32[2,64,128,128]{3,2,1,0:T(8,128)} %own_ref.7, bf16[2,16,64,128]{3,2,1,0:T(8,128)(2,1)S(1)} %collective-permute-done.next_ref), custom_call_target="tpu_custom_call" | custom-call | flops 805306368 | bytes 2097152 | tf_op jit(solution)/shard_map/form_spectrum/pallas_call | solution.py:135
  20.9 3.6 %form_spectrum.5.refs_1_ = bf16[128,32,128]{2,1,0:T(8,128)(2,1)S(1)} custom-call(bf16[256,512]{1,0:T(8,128)(2,1)S(1)} %filter_rows.1.rows_ref, bf16[256,256]{1,0:T(8,128)(2,1)S(1)} %bitcast.24, f32[2,64,128,128]{3,2,1,0:T(8,128)} %own_ref.7, bf16[2,16,64,128]{3,2,1,0:T(8,128)(2,1)S(1)} %collective-permute-done.1.next_ref), custom_call_target="tpu_custom_call" | custom-call | flops 805306368 | bytes 2097152 | tf_op jit(solution)/shard_map/form_spectrum/pallas_call | solution.py:135
  24.5 0.8 copy-done.2
  25.3 1.0 copy-done.3
  26.4 3.6 %form_spectrum.6.refs_2_ = bf16[128,32,128]{2,1,0:T(8,128)(2,1)S(1)} custom-call(bf16[256,512]{1,0:T(8,128)(2,1)S(1)} %filter_rows.1.rows_ref, bf16[256,256]{1,0:T(8,128)(2,1)S(1)} %bitcast.25, f32[2,64,128,128]{3,2,1,0:T(8,128)} %own_ref.7, bf16[2,16,64,128]{3,2,1,0:T(8,128)(2,1)S(1)} %copy-done.3), custom_call_target="tpu_custom_call" | custom-call | flops 805306368 | bytes 2097152 | tf_op jit(solution)/shard_map/form_spectrum/pallas_call | solution.py:135
  30.0 3.7 %form_spectrum.7.refs_3_ = bf16[128,32,128]{2,1,0:T(8,128)(2,1)S(1)} custom-call(bf16[256,512]{1,0:T(8,128)(2,1)S(1)} %filter_rows.1.rows_ref, bf16[256,256]{1,0:T(8,128)(2,1)S(1)} %bitcast.26, f32[2,64,128,128]{3,2,1,0:T(8,128)} %own_ref.7, bf16[2,16,64,128]{3,2,1,0:T(8,128)(2,1)} %collective-permute-done.3.next_ref), custom_call_target="tpu_custom_call" | custom-call | flops 805306368 | bytes 2097152 | tf_op jit(solution)/shard_map/form_spectrum/pallas_call | solution.py:135
  33.6 5.4 %select_gates.2 = bf16[8,8,128,128]{3,2,1,0:T(8,128)(2,1)} custom-call(s32[128]{0:T(128)S(1)} %min.22.bins_ref, s32[64,128]{1,0:T(8,128)S(1)} %reshape.188.gates_ref, bf16[128,32,128]{2,1,0:T(8,128)(2,1)S(1)} %form_spectrum.4.refs_0_, bf16[128,32,128]{2,1,0:T(8,128)(2,1)S(1)} %form_spectrum.5.refs_1_, bf16[128,32,128]{2,1,0:T(8,128)(2,1)S(1)} %form_spectrum.6.refs_2_, ...), custom_call_target="tpu_custom_call" | custom-call | flops 536870912 | bytes 2097152 | tf_op jit(solution)/shard_map/select_gates/pallas_call | solution.py:189
  39.1 1.0 copy-done
  40.1 7.0 %all-to-all-start = ((bf16[8,8,128,128]{3,2,1,0:T(8,128)(2,1)}), bf16[8,8,128,128]{3,2,1,0:T(8,128)(2,1)}, u32[]{:S(2)}, u32[]{:S(2)}) async-start(bf16[8,8,128,128]{3,2,1,0:T(8,128)(2,1)} %select_gates.2), calls=%async_computation | async-start | bytes 4194304 | tf_op jit(solution)/shard_map/all_to_all | solution.py:518
  47.2 0.6 gather_fusion.3
  48.0 1.2 copy-done.1
  49.2 5.4 %select_gates.3 = bf16[8,8,128,128]{3,2,1,0:T(8,128)(2,1)} custom-call(s32[128]{0:T(128)S(1)} %min.25.bins_ref, s32[64,128]{1,0:T(8,128)S(1)} %reshape.189.gates_ref, bf16[128,32,128]{2,1,0:T(8,128)(2,1)S(1)} %form_spectrum.4.refs_0_, bf16[128,32,128]{2,1,0:T(8,128)(2,1)S(1)} %form_spectrum.5.refs_1_, bf16[128,32,128]{2,1,0:T(8,128)(2,1)S(1)} %form_spectrum.6.refs_2_, ...), custom_call_target="tpu_custom_call" | custom-call | flops 536870912 | bytes 2097152 | tf_op jit(solution)/shard_map/select_gates/pallas_call | solution.py:189
  54.7 39.7 %all-to-all-done.arrived_ref = bf16[8,8,128,128]{3,2,1,0:T(8,128)(2,1)} async-done(((bf16[8,8,128,128]{3,2,1,0:T(8,128)(2,1)}), bf16[8,8,128,128]{3,2,1,0:T(8,128)(2,1)}, u32[]{:S(2)}, u32[]{:S(2)}) %all-to-all-start) | async-done | bytes 2097184 | tf_op jit(solution)/shard_map/all_to_all | solution.py:518
  94.3 3.6 %all-to-all-start.1 = ((bf16[8,8,128,128]{3,2,1,0:T(8,128)(2,1)}), bf16[8,8,128,128]{3,2,1,0:T(8,128)(2,1)S(1)}, u32[]{:S(2)}, u32[]{:S(2)}) async-start(bf16[8,8,128,128]{3,2,1,0:T(8,128)(2,1)} %select_gates.3), calls=%async_computation.1 | async-start | bytes 4194304 | tf_op jit(solution)/shard_map/all_to_all | solution.py:518
  98.9 0.6 dynamic_slice.8
  101.4 2.6 %form_beams.2 = (bf16[2,384,128]{2,1,0:T(8,128)(2,1)S(1)}, bf16[2,384,128]{2,1,0:T(8,128)(2,1)S(1)}, bf16[2,384,128]{2,1,0:T(8,128)(2,1)S(1)}, bf16[2,384,128]{2,1,0:T(8,128)(2,1)S(1)}) custom-call(s32[1]{0:T(128)} %bitcast.me_ref, bf16[1024,384]{1,0:T(8,128)(2,1)S(1)} %bitcast.27, bf16[8,8,128,128]{3,2,1,0:T(8,128)(2,1)} %all-to-all-done.arrived_ref), custom_call_target="tpu_custom_call" | custom-call | flops 805306368 | bytes 2097152 | tf_op jit(solution)/shard_map/form_beams/pallas_call | solution.py:224
  104.0 4.9 %collective-permute-start.4 = (bf16[2,384,128]{2,1,0:T(8,128)(2,1)S(1)}, bf16[2,384,128]{2,1,0:T(8,128)(2,1)S(1)}, u32[]{:S(2)}, u32[]{:S(2)}) collective-permute-start(bf16[2,384,128]{2,1,0:T(8,128)(2,1)S(1)} %get-tuple-element.24), channel_id=1, source_target_pairs={{0,1},{1,2},{2,3},{3,0},{4,5},{5,6},{6,7},{7,4},{8,9},{9,10},{10,1... | collective-permute-start | bytes 589832 | tf_op jit(solution)/shard_map/ppermute | solution.py:249
  109.6 3.5 %collective-permute-done.4.refs_1_ = bf16[2,384,128]{2,1,0:T(8,128)(2,1)S(1)} collective-permute-done((bf16[2,384,128]{2,1,0:T(8,128)(2,1)S(1)}, bf16[2,384,128]{2,1,0:T(8,128)(2,1)S(1)}, u32[]{:S(2)}, u32[]{:S(2)}) %collective-permute-start.4) | collective-permute-done | bytes 196640 | tf_op jit(solution)/shard_map/ppermute | solution.py:249
  113.1 4.7 %collective-permute-done.5.refs_2_ = bf16[2,384,128]{2,1,0:T(8,128)(2,1)S(1)} collective-permute-done((bf16[2,384,128]{2,1,0:T(8,128)(2,1)S(1)}, bf16[2,384,128]{2,1,0:T(8,128)(2,1)S(1)}, u32[]{:S(2)}, u32[]{:S(2)}) %collective-permute-start.5) | collective-permute-done | bytes 196640 | tf_op jit(solution)/shard_map/ppermute | solution.py:249
  117.7 0.6 collective-permute-done.6.refs_3_
  118.4 21.7 %factor_slots.2 = (bf16[4,96,384]{2,1,0:T(8,128)(2,1)S(1)}, bf16[4,96,384]{2,1,0:T(8,128)(2,1)S(1)}, bf16[4,96,384]{2,1,0:T(8,128)(2,1)S(1)}, bf16[4,96,384]{2,1,0:T(8,128)(2,1)S(1)}) custom-call(s32[1]{0:T(128)} %bitcast.me_ref, s32[4,192]{1,0:T(4,128)S(1)} %broadcast_select_fusion.3.pivots_ref, bf16[2,384,128]{2,1,0:T(8,128)(2,1)S(1)} %get-tuple-element.23.refs_0_, ...), custom_call_target="tpu_custom_call" | custom-call | flops 23040000000 | bytes 786432 | tf_op jit(solution)/shard_map/factor_slots/pallas_call | solution.py:416
  140.1 0.7 copy-done.4
  140.8 0.7 copy-done.6
  141.5 4.4 %all-to-all-done.1.arrived_ref = bf16[8,8,128,128]{3,2,1,0:T(8,128)(2,1)S(1)} async-done(((bf16[8,8,128,128]{3,2,1,0:T(8,128)(2,1)}), bf16[8,8,128,128]{3,2,1,0:T(8,128)(2,1)S(1)}, u32[]{:S(2)}, u32[]{:S(2)}) %all-to-all-start.1) | async-done | bytes 2097184 | tf_op jit(solution)/shard_map/all_to_all | solution.py:518
  145.9 1.0 form_beams.3
  147.0 5.7 %collective-permute-start.10 = (bf16[2,384,128]{2,1,0:T(8,128)(2,1)S(1)}, bf16[2,384,128]{2,1,0:T(8,128)(2,1)S(1)}, u32[]{:S(2)}, u32[]{:S(2)}) collective-permute-start(bf16[2,384,128]{2,1,0:T(8,128)(2,1)S(1)} %get-tuple-element.32), channel_id=1, source_target_pairs={{0,1},{1,2},{2,3},{3,0},{4,5},{5,6},{6,7},{7,4},{8,9},{9,10},{10,1... | collective-permute-start | bytes 589832 | tf_op jit(solution)/shard_map/ppermute | solution.py:249
  153.2 1.3 collective-permute-start.7
  154.5 1.4 collective-permute-start.8
  155.9 0.8 collective-permute-done.10.refs_1_
  156.7 4.2 %collective-permute-done.11.refs_2_ = bf16[2,384,128]{2,1,0:T(8,128)(2,1)S(1)} collective-permute-done((bf16[2,384,128]{2,1,0:T(8,128)(2,1)S(1)}, bf16[2,384,128]{2,1,0:T(8,128)(2,1)S(1)}, u32[]{:S(2)}, u32[]{:S(2)}) %collective-permute-start.11) | collective-permute-done | bytes 196640 | tf_op jit(solution)/shard_map/ppermute | solution.py:249
  161.0 1.8 collective-permute-done.12.refs_3_
  162.7 21.7 %factor_slots.3 = (bf16[4,96,384]{2,1,0:T(8,128)(2,1)S(1)}, bf16[4,96,384]{2,1,0:T(8,128)(2,1)S(1)}, bf16[4,96,384]{2,1,0:T(8,128)(2,1)S(1)}, bf16[4,96,384]{2,1,0:T(8,128)(2,1)S(1)}) custom-call(s32[1]{0:T(128)} %bitcast.me_ref, s32[4,192]{1,0:T(4,128)S(1)} %broadcast_select_fusion.2.pivots_ref, bf16[2,384,128]{2,1,0:T(8,128)(2,1)S(1)} %get-tuple-element.31.refs_0_, ...), custom_call_target="tpu_custom_call" | custom-call | flops 23040000000 | bytes 786432 | tf_op jit(solution)/shard_map/factor_slots/pallas_call | solution.py:416
  184.5 1.7 collective-permute-start.14
  186.2 0.7 collective-permute-start.15
  186.9 0.6 dynamic_slice.7
  187.5 0.7 pad_add_fusion.place_ref
  188.7 10.2 %collective-permute-done.14.refs_6_ = bf16[4,96,384]{2,1,0:T(8,128)(2,1)S(1)} collective-permute-done((bf16[4,96,384]{2,1,0:T(8,128)(2,1)S(1)}, bf16[4,96,384]{2,1,0:T(8,128)(2,1)S(1)}, u32[]{:S(2)}, u32[]{:S(2)}) %collective-permute-start.14) | collective-permute-done | bytes 294944 | tf_op jit(solution)/shard_map/ppermute | solution.py:249
  198.9 0.8 collective-permute-done.15.refs_7_
  199.7 3.0 %place_rows.1 = f32[32,96,384]{2,1,0:T(8,128)} custom-call(s32[2]{0:T(128)S(1)} %pad_add_fusion.place_ref, bf16[4,96,384]{2,1,0:T(8,128)(2,1)S(1)} %get-tuple-element.27.refs_0_, bf16[4,96,384]{2,1,0:T(8,128)(2,1)S(1)} %collective-permute-done.7.refs_1_, bf16[4,96,384]{2,1,0:T(8,128)(2,1)S(1)} %collective-permute-done.8.refs_2_, ...), custom_call_target="tpu_custom_call" | custom-call | tf_op jit(solution)/shard_map/place_rows/pallas_call | solution.py:450
  (81 shorter events, 5.8 us)
Async XLA Ops:
  1.3 16.0 %collective-permute-start = (bf16[2,16,64,128]{3,2,1,0:T(8,128)(2,1)S(1)}, bf16[2,16,64,128]{3,2,1,0:T(8,128)(2,1)S(1)}, u32[]{:S(2)}, u32[]{:S(2)}) collective-permute-start(bf16[2,16,64,128]{3,2,1,0:T(8,128)(2,1)S(1)} %rim_rows.4), channel_id=1, source_target_pairs={{1,0},{2,1},{3,2},{5,4},{6,5},{7,6},{9,8},{10,9},{11,10},{13,12},{... | collective-permute-start | bytes 1572872 | tf_op jit(solution)/shard_map/ppermute | solution.py:22
  4.6 16.3 %collective-permute-start.1 = (bf16[2,16,64,128]{3,2,1,0:T(8,128)(2,1)S(1)}, bf16[2,16,64,128]{3,2,1,0:T(8,128)(2,1)S(1)}, u32[]{:S(2)}, u32[]{:S(2)}) collective-permute-start(bf16[2,16,64,128]{3,2,1,0:T(8,128)(2,1)S(1)} %rim_rows.5), channel_id=1, source_target_pairs={{1,0},{2,1},{3,2},{5,4},{6,5},{7,6},{9,8},{10,9},{11,10},{13,12},{... | collective-permute-start | bytes 1572872 | tf_op jit(solution)/shard_map/ppermute | solution.py:22
  8.6 6.4 %copy-start.12 = (s32[8]{0:T(128)S(1)}, s32[8]{0:T(128)}, u32[]{:S(2)}) copy-start(s32[8]{0:T(128)} %param.14) | copy-start | bytes 100
  8.6 6.8 %copy-start.10 = (s32[128,64]{0,1:T(8,128)S(1)}, s32[128,64]{0,1:T(8,128)}, u32[]{:S(2)}) copy-start(s32[128,64]{0,1:T(8,128)} %param.15) | copy-start | bytes 98308
  8.6 15.9 %collective-permute-start.2 = (bf16[2,16,64,128]{3,2,1,0:T(8,128)(2,1)}, bf16[2,16,64,128]{3,2,1,0:T(8,128)(2,1)S(1)}, u32[]{:S(2)}, u32[]{:S(2)}) collective-permute-start(bf16[2,16,64,128]{3,2,1,0:T(8,128)(2,1)} %rim_rows.6), channel_id=1, source_target_pairs={{1,0},{2,1},{3,2},{5,4},{6,5},{7,6},{9,8},{10,9},{11,10},{13,12},{... | collective-permute-start | bytes 1572872 | tf_op jit(solution)/shard_map/ppermute | solution.py:22
  12.7 4.4 %copy-start.11 = (f32[2,64]{1,0:T(2,128)S(1)}, f32[2,64]{1,0:T(2,128)}, u32[]{:S(2)}) copy-start(f32[2,64]{1,0:T(2,128)} %param.11) | copy-start | bytes 1540
  12.7 17.3 %collective-permute-start.3 = (bf16[2,16,64,128]{3,2,1,0:T(8,128)(2,1)}, bf16[2,16,64,128]{3,2,1,0:T(8,128)(2,1)}, u32[]{:S(2)}, u32[]{:S(2)}) collective-permute-start(bf16[2,16,64,128]{3,2,1,0:T(8,128)(2,1)} %rim_rows.7), channel_id=1, source_target_pairs={{1,0},{2,1},{3,2},{5,4},{6,5},{7,6},{9,8},{10,9},{11,10},{13,12},{... | collective-permute-start | bytes 1572872 | tf_op jit(solution)/shard_map/ppermute | solution.py:22
  24.5 0.8 copy-start.2
  25.3 1.0 copy-start.3
  39.1 1.0 copy-start
  40.1 54.3 %all-to-all-start = ((bf16[8,8,128,128]{3,2,1,0:T(8,128)(2,1)}), bf16[8,8,128,128]{3,2,1,0:T(8,128)(2,1)}, u32[]{:S(2)}, u32[]{:S(2)}) async-start(bf16[8,8,128,128]{3,2,1,0:T(8,128)(2,1)} %select_gates.2), calls=%async_computation | async-start | bytes 4194304 | tf_op jit(solution)/shard_map/all_to_all | solution.py:518
  48.0 1.2 copy-start.1
  54.7 43.3 %copy-start.8 = (bf16[2,512,192]{1,2,0:T(8,128)(2,1)S(1)}, bf16[2,512,192]{1,2,0:T(8,128)(2,1)}, u32[]{:S(2)}) copy-start(bf16[2,512,192]{1,2,0:T(8,128)(2,1)} %param.12) | copy-start | bytes 1179652
  94.3 51.6 %all-to-all-start.1 = ((bf16[8,8,128,128]{3,2,1,0:T(8,128)(2,1)}), bf16[8,8,128,128]{3,2,1,0:T(8,128)(2,1)S(1)}, u32[]{:S(2)}, u32[]{:S(2)}) async-start(bf16[8,8,128,128]{3,2,1,0:T(8,128)(2,1)} %select_gates.3), calls=%async_computation.1 | async-start | bytes 4194304 | tf_op jit(solution)/shard_map/all_to_all | solution.py:518
  98.3 1.1 copy-start.9
  104.0 9.0 %collective-permute-start.4 = (bf16[2,384,128]{2,1,0:T(8,128)(2,1)S(1)}, bf16[2,384,128]{2,1,0:T(8,128)(2,1)S(1)}, u32[]{:S(2)}, u32[]{:S(2)}) collective-permute-start(bf16[2,384,128]{2,1,0:T(8,128)(2,1)S(1)} %get-tuple-element.24), channel_id=1, source_target_pairs={{0,1},{1,2},{2,3},{3,0},{4,5},{5,6},{6,7},{7,4},{8,9},{9,10},{10,1... | collective-permute-start | bytes 589832 | tf_op jit(solution)/shard_map/ppermute | solution.py:249
  109.0 8.7 %collective-permute-start.5 = (bf16[2,384,128]{2,1,0:T(8,128)(2,1)S(1)}, bf16[2,384,128]{2,1,0:T(8,128)(2,1)S(1)}, u32[]{:S(2)}, u32[]{:S(2)}) collective-permute-start(bf16[2,384,128]{2,1,0:T(8,128)(2,1)S(1)} %get-tuple-element.25), channel_id=1, source_target_pairs={{0,2},{1,3},{2,0},{3,1},{4,6},{5,7},{6,4},{7,5},{8,10},{9,11},{10,... | collective-permute-start | bytes 589832 | tf_op jit(solution)/shard_map/ppermute | solution.py:249
  109.0 9.4 %collective-permute-start.6 = (bf16[2,384,128]{2,1,0:T(8,128)(2,1)S(1)}, bf16[2,384,128]{2,1,0:T(8,128)(2,1)S(1)}, u32[]{:S(2)}, u32[]{:S(2)}) collective-permute-start(bf16[2,384,128]{2,1,0:T(8,128)(2,1)S(1)} %get-tuple-element.26), channel_id=1, source_target_pairs={{0,3},{1,0},{2,1},{3,2},{4,7},{5,4},{6,5},{7,6},{8,11},{9,8},{10,9... | collective-permute-start | bytes 589832 | tf_op jit(solution)/shard_map/ppermute | solution.py:249
  140.1 0.7 copy-start.4
  140.8 0.7 copy-start.6
  145.9 7.2 %copy-start.7 = (bf16[4,96,384]{2,1,0:T(8,128)(2,1)S(1)}, bf16[4,96,384]{2,1,0:T(8,128)(2,1)}, u32[]{:S(2)}) copy-start(bf16[4,96,384]{2,1,0:T(8,128)(2,1)} %copy-done.6) | copy-start | bytes 884740
  145.9 8.5 %copy-start.5 = (bf16[4,96,384]{2,1,0:T(8,128)(2,1)S(1)}, bf16[4,96,384]{2,1,0:T(8,128)(2,1)}, u32[]{:S(2)}) copy-start(bf16[4,96,384]{2,1,0:T(8,128)(2,1)} %copy-done.4) | copy-start | bytes 884740
  147.0 9.8 %collective-permute-start.10 = (bf16[2,384,128]{2,1,0:T(8,128)(2,1)S(1)}, bf16[2,384,128]{2,1,0:T(8,128)(2,1)S(1)}, u32[]{:S(2)}, u32[]{:S(2)}) collective-permute-start(bf16[2,384,128]{2,1,0:T(8,128)(2,1)S(1)} %get-tuple-element.32), channel_id=1, source_target_pairs={{0,1},{1,2},{2,3},{3,0},{4,5},{5,6},{6,7},{7,4},{8,9},{9,10},{10,1... | collective-permute-start | bytes 589832 | tf_op jit(solution)/shard_map/ppermute | solution.py:249
  152.6 8.3 %collective-permute-start.11 = (bf16[2,384,128]{2,1,0:T(8,128)(2,1)S(1)}, bf16[2,384,128]{2,1,0:T(8,128)(2,1)S(1)}, u32[]{:S(2)}, u32[]{:S(2)}) collective-permute-start(bf16[2,384,128]{2,1,0:T(8,128)(2,1)S(1)} %get-tuple-element.33), channel_id=1, source_target_pairs={{0,2},{1,3},{2,0},{3,1},{4,6},{5,7},{6,4},{7,5},{8,10},{9,11},{10,... | collective-permute-start | bytes 589832 | tf_op jit(solution)/shard_map/ppermute | solution.py:249
  152.6 10.1 %collective-permute-start.12 = (bf16[2,384,128]{2,1,0:T(8,128)(2,1)S(1)}, bf16[2,384,128]{2,1,0:T(8,128)(2,1)S(1)}, u32[]{:S(2)}, u32[]{:S(2)}) collective-permute-start(bf16[2,384,128]{2,1,0:T(8,128)(2,1)S(1)} %get-tuple-element.34), channel_id=1, source_target_pairs={{0,3},{1,0},{2,1},{3,2},{4,7},{5,4},{6,5},{7,6},{8,11},{9,8},{10,9... | collective-permute-start | bytes 589832 | tf_op jit(solution)/shard_map/ppermute | solution.py:249
  153.2 33.0 %collective-permute-start.7 = (bf16[4,96,384]{2,1,0:T(8,128)(2,1)S(1)}, bf16[4,96,384]{2,1,0:T(8,128)(2,1)S(1)}, u32[]{:S(2)}, u32[]{:S(2)}) collective-permute-start(bf16[4,96,384]{2,1,0:T(8,128)(2,1)S(1)} %copy-done.7), channel_id=1, source_target_pairs={{0,1},{1,2},{2,3},{3,0},{4,5},{5,6},{6,7},{7,4},{8,9},{9,10},{10,1... | collective-permute-start | bytes 884744 | tf_op jit(solution)/shard_map/ppermute | solution.py:249
  154.5 33.7 %collective-permute-start.8 = (bf16[4,96,384]{2,1,0:T(8,128)(2,1)S(1)}, bf16[4,96,384]{2,1,0:T(8,128)(2,1)S(1)}, u32[]{:S(2)}, u32[]{:S(2)}) collective-permute-start(bf16[4,96,384]{2,1,0:T(8,128)(2,1)S(1)} %copy-done.5), channel_id=1, source_target_pairs={{0,2},{1,3},{2,0},{3,1},{4,6},{5,7},{6,4},{7,5},{8,10},{9,11},{10,... | collective-permute-start | bytes 884744 | tf_op jit(solution)/shard_map/ppermute | solution.py:249
  156.7 31.5 %collective-permute-start.9 = (bf16[4,96,384]{2,1,0:T(8,128)(2,1)S(1)}, bf16[4,96,384]{2,1,0:T(8,128)(2,1)S(1)}, u32[]{:S(2)}, u32[]{:S(2)}) collective-permute-start(bf16[4,96,384]{2,1,0:T(8,128)(2,1)S(1)} %get-tuple-element.30), channel_id=1, source_target_pairs={{0,3},{1,0},{2,1},{3,2},{4,7},{5,4},{6,5},{7,6},{8,11},{9,8},{10,9... | collective-permute-start | bytes 884744 | tf_op jit(solution)/shard_map/ppermute | solution.py:249
  184.4 4.2 %collective-permute-start.13 = (bf16[4,96,384]{2,1,0:T(8,128)(2,1)S(1)}, bf16[4,96,384]{2,1,0:T(8,128)(2,1)S(1)}, u32[]{:S(2)}, u32[]{:S(2)}) collective-permute-start(bf16[4,96,384]{2,1,0:T(8,128)(2,1)S(1)} %get-tuple-element.36), channel_id=1, source_target_pairs={{0,1},{1,2},{2,3},{3,0},{4,5},{5,6},{6,7},{7,4},{8,9},{9,10},{10,1... | collective-permute-start | bytes 884744 | tf_op jit(solution)/shard_map/ppermute | solution.py:249
  184.5 14.4 %collective-permute-start.14 = (bf16[4,96,384]{2,1,0:T(8,128)(2,1)S(1)}, bf16[4,96,384]{2,1,0:T(8,128)(2,1)S(1)}, u32[]{:S(2)}, u32[]{:S(2)}) collective-permute-start(bf16[4,96,384]{2,1,0:T(8,128)(2,1)S(1)} %get-tuple-element.37), channel_id=1, source_target_pairs={{0,2},{1,3},{2,0},{3,1},{4,6},{5,7},{6,4},{7,5},{8,10},{9,11},{10,... | collective-permute-start | bytes 884744 | tf_op jit(solution)/shard_map/ppermute | solution.py:249
  186.2 13.5 %collective-permute-start.15 = (bf16[4,96,384]{2,1,0:T(8,128)(2,1)S(1)}, bf16[4,96,384]{2,1,0:T(8,128)(2,1)S(1)}, u32[]{:S(2)}, u32[]{:S(2)}) collective-permute-start(bf16[4,96,384]{2,1,0:T(8,128)(2,1)S(1)} %get-tuple-element.38), channel_id=1, source_target_pairs={{0,3},{1,0},{2,1},{3,2},{4,7},{5,4},{6,5},{7,6},{8,11},{9,8},{10,9... | collective-permute-start | bytes 884744 | tf_op jit(solution)/shard_map/ppermute | solution.py:249

commit v6 on v5

--- a/solution.py
+++ b/solution.py
@@ -67,19 +67,23 @@
     )(jnp.pad(replica, ((0, 0), (0, span - tap_count))))
 
 
-def rim_kernel(echo_ref, out_ref):
-    out_ref[...] = echo_ref[...].astype(BF16)
-
-
-def rim_rows(raw_echo, rim, chunk, chunks):
+def rim_kernel(echo_ref, *out_refs):
+    for chunk, out_ref in enumerate(out_refs):
+
+        @pl.when(pl.program_id(0) == chunk)
+        def _(out_ref=out_ref):
+            out_ref[...] = echo_ref[...].astype(BF16)
+
+
+def rim_rows(raw_echo, rim, chunks):
     _, ch_local, _, pulses = raw_echo.shape
     shape = (2, ch_local // chunks, rim, pulses)
     return pl.pallas_call(
         rim_kernel,
-        out_shape=jax.ShapeDtypeStruct(shape, BF16),
-        grid=(1,),
-        in_specs=[pl.BlockSpec(shape, lambda i: (0, chunk, 0, 0))],
-        out_specs=pl.BlockSpec(shape, lambda i: (0, 0, 0, 0)),
+        out_shape=[jax.ShapeDtypeStruct(shape, BF16)] * chunks,
+        grid=(chunks,),
+        in_specs=[pl.BlockSpec(shape, lambda i: (0, i, 0, 0))],
+        out_specs=[pl.BlockSpec(shape, lambda i: (0, 0, 0, 0))] * chunks,
         compiler_params=PARAMS,
         name="rim_rows",
     )(raw_echo)
@@ -158,24 +162,21 @@
     *spectrum_refs, out_ref = refs
     gate_rows = spectrum_refs[0].shape[2]
     owners, groups, rows, width = out_ref.shape
-    gate_index = lax.broadcasted_iota(jnp.int32, (gate_rows, width), 0)
-    part_index = lax.broadcasted_iota(jnp.int32, (gate_rows, width), 1) // (width // pack)
+    gate_index = lax.broadcasted_iota(jnp.int32, (pack * gate_rows, width), 0)
     unroll = math.gcd(groups, 4)
-    masks = [part_index == part for part in range(pack)]
 
     def some_groups(step, carry):
         owner = step // (groups // unroll)
         lead = step % (groups // unroll) * unroll
         for inner in range(unroll):
             group = step * unroll + inner
-            hit = gate_index == gates_ref[pl.ds(group, 1), :]
-            total = jnp.zeros((rows, width), F32)
-            for part in range(pack):
-                bin_index = bins_ref[group * pack + part]
-                chooser = jnp.where(hit & masks[part], 1.0, 0.0).astype(BF16)
-                spectra = jnp.concatenate([ref[bin_index] for ref in spectrum_refs], axis=0)
-                total += jnp.dot(spectra, chooser, preferred_element_type=F32)
-            out_ref[owner, lead + inner] = total.astype(BF16)
+            chooser = jnp.where(gate_index == gates_ref[pl.ds(group, 1), :], 1.0, 0.0)
+            bins = [bins_ref[group * pack + part] for part in range(pack)]
+            spectra = jnp.concatenate(
+                [jnp.concatenate([ref[b] for b in bins], axis=1) for ref in spectrum_refs], axis=0
+            )
+            picked = jnp.dot(spectra, chooser.astype(BF16), preferred_element_type=F32)
+            out_ref[owner, lead + inner] = picked.astype(BF16)
         return carry
 
     lax.fori_loop(0, owners * groups // unroll, some_groups, 0)
@@ -332,8 +333,9 @@
 
 def factor_kernel(me_ref, pivots_ref, *refs, ranges, pack, count_rows):
     beams_refs, out_refs = refs[:ranges], refs[ranges : 2 * ranges]
-    panel_ref, *work = refs[2 * ranges :]
-    slots = len(work)
+    panel_ref, *scratch = refs[2 * ranges :]
+    slots = len(scratch) // 2
+    work, last = scratch[:slots], scratch[slots:]
     order = work[0].shape[0]
     height = panel_ref.shape[1] // PANEL
 
@@ -354,19 +356,28 @@
 
     lane = lax.broadcasted_iota(jnp.int32, (PANEL, LANES), 1)
     eights = range(0, PANEL, 8)
+
+    def spread_out(slot, rows, chunks):
+        for i in eights:
+            for w in range(chunks):
+                piece = rows[i : i + 8, w * LANES : (w + 1) * LANES]
+                panel_ref[w, pl.ds(i * height + slot, 8, stride=height), :] = piece
+
     for start in range(0, order, LANES):
         chunks = (order - start) // LANES
-
-        def one_panel(p, carry, start=start, chunks=chunks):
+        stop = start + LANES
+        for slot in range(slots):
+            spread_out(slot, work[slot][start : start + PANEL, start:], chunks)
+            last[slot][...] = jnp.zeros_like(last[slot])
+
+        def one_panel(p, carry, start=start, stop=stop, chunks=chunks):
             base = pl.multiple_of(start + p * PANEL, PANEL)
+            following = pl.multiple_of(jnp.minimum(base + PANEL, order - PANEL), PANEL)
             back = p * PANEL
             for slot in range(slots):
-                for i in eights:
-                    place = pl.ds(pl.multiple_of(base + i, 8), 8)
-                    for w in range(chunks):
-                        left = start + w * LANES
-                        piece = work[slot][place, left : left + LANES]
-                        panel_ref[w, pl.ds(i * height + slot, 8, stride=height), :] = piece
+                before = last[slot][:, start:]
+                below = jnp.where(lane >= back + PANEL, before[:, :LANES], 0.0)
+                work[slot][start:stop, start:] -= cross_product(below, before)
             rows = []
             for t in range(PANEL):
                 pieces = [panel_ref[w, t * height : (t + 1) * height, :] for w in range(chunks)]
@@ -385,9 +396,11 @@
                     ]
                     parts.append(jnp.concatenate(pieces, axis=0))
                 panel = jnp.concatenate(parts, axis=1)
+                ahead = pltpu.roll(parts[0], (2 * LANES - PANEL - back) % LANES, 1)[:, :PANEL]
+                ready = work[slot][pl.ds(following, PANEL), start:] - cross_product(ahead, panel)
+                spread_out(slot, ready, chunks)
                 work[slot][pl.ds(base, PANEL), start:] = panel
-                below = jnp.where(lane >= back + PANEL, parts[0], 0.0)
-                work[slot][start : start + LANES, start:] -= cross_product(below, panel)
+                last[slot][:, start:] = panel
             return carry
 
         lax.fori_loop(0, LANES // PANEL, one_panel, 0)
@@ -420,7 +433,8 @@
         + [pl.BlockSpec(memory_space=pltpu.VMEM)] * (1 + ranges),
         out_specs=[pl.BlockSpec(memory_space=pltpu.VMEM)] * ranges,
         scratch_shapes=[pltpu.VMEM((order // LANES, PANEL * height, LANES), F32)]
-        + [pltpu.VMEM((order, order), F32) for _ in range(slots)],
+        + [pltpu.VMEM((order, order), F32) for _ in range(slots)]
+        + [pltpu.VMEM((PANEL, order), F32) for _ in range(slots)],
         compiler_params=PARAMS,
         cost_estimate=pl.CostEstimate(
             flops=order * 60_000_000,
@@ -459,9 +473,8 @@
 
 
 def slot_parts(share_slots, pack):
-    halves = 2 if share_slots % (2 * pack) == 0 else 1
-    count = share_slots // halves
-    return [(i * count, count) for i in range(halves)]
+    head = share_slots - pack
+    return [(0, head), (head, pack)] if head > 0 else [(0, share_slots)]
 
 
 def local(raw_echo, replica, beam_weights, pivots, owner_counts, train_gates):
@@ -482,7 +495,7 @@
     filters = filter_rows(replica, gate_rows)
     table = doppler_table(pulse_count).transpose(0, 3, 1, 2)
     table = table.reshape(2 * pulse_count, -1).astype(BF16)
-    following = [shifted(rim_rows(raw_echo, rim, c, chunks), "rng", -1) for c in range(chunks)]
+    following = [shifted(rows, "rng", -1) for rows in rim_rows(raw_echo, rim, chunks)]
     spectra = [
         form_spectrum(filters, table, raw_echo, following[c], c, chunks) for c in range(chunks)
     ]
@@ -513,7 +526,10 @@
         some = first + jnp.arange(count, dtype=jnp.int32)
         slots = (lead_slots[:, None] + some[None, :]).reshape(-1)
         bins = jnp.minimum(starts[:, None] + slots[None, :], pulse_count - 1).reshape(-1)
-        gates = jnp.take(local_gates, bins, axis=0).reshape(-1, pack * train_local)
+        gates = jnp.take(local_gates, bins, axis=0).reshape(-1, pack, train_local)
+        gates = (gates + gate_rows * jnp.arange(pack, dtype=jnp.int32)[:, None]).reshape(
+            -1, pack * train_local
+        )
         outgoing = select_gates(spectra, bins, gates, owners, pack)
         sent.append(lax.all_to_all(outgoing, "dop", split_axis=0, concat_axis=0, tiled=True))
     done, earlier = [], []

time: 204 us -> 212 us (1.039)
  local copies, waits for them, and re-layouts: 10.3 us -> 23.9 us
  waiting for transfers between devices: 71.2 us -> 64.8 us
  starting transfers between devices: 35.3 us -> 30.8 us
  other arithmetic: 2.53 us -> 6.82 us
    ppermute x12, waiting for transfers between devices: 27.1 us -> 7.03 us  [exchange(): moved.append(lax.ppermute(arrays[shift], axis, pairs))]
    all_to_all x2, waiting for transfers between devices: 44.1 us -> 53.3 us  [local(): lax.all_to_all(outgoing, 'dop', split_axis=0, concat_axis=0, tiled=True)]
    unnamed x31 -> x41, local copies, waits for them, and re-layouts: 5.96 us -> 13.1 us
    ppermute x4, waiting for transfers between devices: 0.01 us -> 4.5 us  [shifted(): return lax.ppermute(array, axis, pairs)]
    ppermute x12, starting transfers between devices: 16.8 us -> 13.7 us  [exchange(): moved.append(lax.ppermute(arrays[shift], axis, pairs))]
    pallas_call x2, Pallas kernels: 43.4 us -> 46.3 us  [factor_slots(): pl.pallas_call(functools.partial(factor_kernel, ranges=ranges, pack=pack,...]
    pallas_call x4 -> x1, Pallas kernels: 6.72 us -> 4.17 us  [rim_rows(): pl.pallas_call(rim_kernel, out_shape=[jax.ShapeDtypeStruct(shape, BF16)]...]
  transfers between devices with their start and end apart: 18 -> 18, of which waited for: 11 -> 11; matrix products, arithmetic and copies ran while one was open for 4% -> 10% of each run, Pallas kernels for 33% -> 28%
where the time goes in v6:
time: 212 us; the launch traced here: 211 us
  Pallas kernels  83.3 us (39%)
  waiting for transfers between devices  64.8 us (31%)
  starting transfers between devices  30.8 us (15%)
  local copies, waits for them, and re-layouts  23.9 us (11%)
  other arithmetic  6.82 us (3%)
    all_to_all x2, waiting for transfers between devices, local(): lax.all_to_all(outgoing, 'dop', split_axis=0, concat_axis=0, tiled=True)  53.3 us
    pallas_call x2, Pallas kernels, factor_slots(): pl.pallas_call(functools.partial(factor_kernel, ranges=ranges, pack=pack,...  46.3 us
    pallas_call x4, Pallas kernels, form_spectrum(): pl.pallas_call(spectrum_kernel, out_shape=jax.ShapeDtypeStruct((bins, hei...  14.4 us
    ppermute x12, starting transfers between devices, exchange(): moved.append(lax.ppermute(arrays[shift], axis, pairs))  13.7 us
    unnamed x41, local copies, waits for them, and re-layouts  13.1 us
    pallas_call x2, Pallas kernels, select_gates(): pl.pallas_call(functools.partial(select_kernel, pack=pack), out_shape=jax...  9.78 us
    all_to_all x2, starting transfers between devices, local(): lax.all_to_all(outgoing, 'dop', split_axis=0, concat_axis=0, tiled=True)  9.42 us
    ppermute x4, starting transfers between devices, shifted(): return lax.ppermute(array, axis, pairs)  7.72 us
  transfers between devices with their start and end apart: 18, of which 11 were waited for; matrix products, arithmetic and copies ran while one was open for 10% of the time, Pallas kernels for 28%

profile of v6, /device:TPU:1, one launch (start us, length us, event | category | flops | bytes accessed | tf_op | source)
XLA Modules:
  0.0 210.7 jit_solution(9256132983106886841)
XLA Ops:
  0.0 4.2 %rim_rows.1 = (bf16[2,16,64,128]{3,2,1,0:T(8,128)(2,1)S(1)}, bf16[2,16,64,128]{3,2,1,0:T(8,128)(2,1)}, bf16[2,16,64,128]{3,2,1,0:T(8,128)(2,1)}, bf16[2,16,64,128]{3,2,1,0:T(8,128)(2,1)}) custom-call(f32[2,64,128,128]{3,2,1,0:T(8,128)} %own_ref.7), custom_call_target="tpu_custom_call" | custom-call | tf_op jit(solution)/shard_map/rim_rows/pallas_call | solution.py:81
  4.2 2.0 collective-permute-start
  6.1 1.9 collective-permute-start.1
  8.1 1.9 collective-permute-start.2
  10.0 1.9 collective-permute-start.3
  15.5 3.6 %form_spectrum.4.refs_0_ = bf16[128,32,128]{2,1,0:T(8,128)(2,1)S(1)} custom-call(bf16[256,512]{1,0:T(8,128)(2,1)S(1)} %filter_rows.1.rows_ref, bf16[256,256]{1,0:T(8,128)(2,1)S(1)} %bitcast.37, f32[2,64,128,128]{3,2,1,0:T(8,128)} %own_ref.7, bf16[2,16,64,128]{3,2,1,0:T(8,128)(2,1)S(1)} %collective-permute-done.next_ref), custom_call_target="tpu_custom_call" | custom-call | flops 805306368 | bytes 2097152 | tf_op jit(solution)/shard_map/form_spectrum/pallas_call | solution.py:139
  19.1 2.0 collective-permute-done.1.next_ref
  21.2 3.6 %form_spectrum.5.refs_1_ = bf16[128,32,128]{2,1,0:T(8,128)(2,1)S(1)} custom-call(bf16[256,512]{1,0:T(8,128)(2,1)S(1)} %filter_rows.1.rows_ref, bf16[256,256]{1,0:T(8,128)(2,1)S(1)} %bitcast.38, f32[2,64,128,128]{3,2,1,0:T(8,128)} %own_ref.7, bf16[2,16,64,128]{3,2,1,0:T(8,128)(2,1)S(1)} %collective-permute-done.1.next_ref), custom_call_target="tpu_custom_call" | custom-call | flops 805306368 | bytes 2097152 | tf_op jit(solution)/shard_map/form_spectrum/pallas_call | solution.py:139
  24.8 2.0 collective-permute-done.2.next_ref
  26.8 0.8 copy-done.5
  27.6 1.0 copy-done.6
  28.6 3.6 %form_spectrum.6.refs_2_ = bf16[128,32,128]{2,1,0:T(8,128)(2,1)S(1)} custom-call(bf16[256,512]{1,0:T(8,128)(2,1)S(1)} %filter_rows.1.rows_ref, bf16[256,256]{1,0:T(8,128)(2,1)S(1)} %bitcast.39, f32[2,64,128,128]{3,2,1,0:T(8,128)} %own_ref.7, bf16[2,16,64,128]{3,2,1,0:T(8,128)(2,1)S(1)} %copy-done.6), custom_call_target="tpu_custom_call" | custom-call | flops 805306368 | bytes 2097152 | tf_op jit(solution)/shard_map/form_spectrum/pallas_call | solution.py:139
  32.5 3.7 %form_spectrum.7.refs_3_ = bf16[128,32,128]{2,1,0:T(8,128)(2,1)S(1)} custom-call(bf16[256,512]{1,0:T(8,128)(2,1)S(1)} %filter_rows.1.rows_ref, bf16[256,256]{1,0:T(8,128)(2,1)S(1)} %bitcast.40, f32[2,64,128,128]{3,2,1,0:T(8,128)} %own_ref.7, bf16[2,16,64,128]{3,2,1,0:T(8,128)(2,1)} %collective-permute-done.3.next_ref), custom_call_target="tpu_custom_call" | custom-call | flops 805306368 | bytes 2097152 | tf_op jit(solution)/shard_map/form_spectrum/pallas_call | solution.py:139
  36.2 7.5 %select_gates.2 = bf16[8,12,128,128]{3,2,1,0:T(8,128)(2,1)} custom-call(s32[192]{0:T(256)S(1)} %min.86.bins_ref, s32[96,128]{1,0:T(8,128)S(1)} %select_add_fusion.gates_ref, bf16[128,32,128]{2,1,0:T(8,128)(2,1)S(1)} %form_spectrum.4.refs_0_, bf16[128,32,128]{2,1,0:T(8,128)(2,1)S(1)} %form_spectrum.5.refs_1_, bf16[128,32,128]{2,1,0:T(8,128)(2,1)S(1)} %form_spectrum.6.refs_2_, ...), custom_call_target="tpu_custom_call" | custom-call | flops 805306368 | bytes 3145728 | tf_op jit(solution)/shard_map/select_gates/pallas_call | solution.py:190
  43.6 1.0 copy-done
  44.6 5.7 %all-to-all-start = ((bf16[8,12,128,128]{3,2,1,0:T(8,128)(2,1)}), bf16[8,12,128,128]{3,2,1,0:T(8,128)(2,1)}, u32[]{:S(2)}, u32[]{:S(2)}) async-start(bf16[8,12,128,128]{3,2,1,0:T(8,128)(2,1)} %select_gates.2), calls=%async_computation | async-start | bytes 6291456 | tf_op jit(solution)/shard_map/all_to_all | solution.py:534
  52.4 1.8 fusion.11
  54.2 1.1 copy.44
  55.3 0.8 neg.13
  56.0 1.8 copy.43
  57.8 1.4 maximum_bitcast_fusion
  59.3 1.0 copy.33
  61.1 1.5 gather_fusion
  63.9 53.3 %all-to-all-done.arrived_ref = bf16[8,12,128,128]{3,2,1,0:T(8,128)(2,1)} async-done(((bf16[8,12,128,128]{3,2,1,0:T(8,128)(2,1)}), bf16[8,12,128,128]{3,2,1,0:T(8,128)(2,1)}, u32[]{:S(2)}, u32[]{:S(2)}) %all-to-all-start) | async-done | bytes 3145760 | tf_op jit(solution)/shard_map/all_to_all | solution.py:534
  117.2 1.1 copy-done.3
  118.3 4.4 %form_beams.2 = (bf16[3,384,128]{2,1,0:T(8,128)(2,1)S(1)}, bf16[3,384,128]{2,1,0:T(8,128)(2,1)}, bf16[3,384,128]{2,1,0:T(8,128)(2,1)}, bf16[3,384,128]{2,1,0:T(8,128)(2,1)}) custom-call(s32[1]{0:T(128)} %bitcast.me_ref, bf16[1024,384]{1,0:T(8,128)(2,1)S(1)} %bitcast.41, bf16[8,12,128,128]{3,2,1,0:T(8,128)(2,1)} %all-to-all-done.arrived_ref), custom_call_target="tpu_custom_call" | custom-call | flops 1207959552 | bytes 3145728 | tf_op jit(solution)/shard_map/form_beams/pallas_call | solution.py:225
  123.5 4.5 %collective-permute-start.4 = (bf16[3,384,128]{2,1,0:T(8,128)(2,1)}, bf16[3,384,128]{2,1,0:T(8,128)(2,1)S(1)}, u32[]{:S(2)}, u32[]{:S(2)}) collective-permute-start(bf16[3,384,128]{2,1,0:T(8,128)(2,1)} %get-tuple-element.30), channel_id=1, source_target_pairs={{0,1},{1,2},{2,3},{3,0},{4,5},{5,6},{6,7},{7,4},{8,9},{9,10},{10,1... | collective-permute-start | bytes 884744 | tf_op jit(solution)/shard_map/ppermute | solution.py:250
  130.1 1.6 gather_fusion.2
  132.4 1.2 copy-done.1
  133.6 2.3 %select_gates.3 = bf16[8,4,128,128]{3,2,1,0:T(8,128)(2,1)S(1)} custom-call(s32[64]{0:T(128)S(1)} %min.94.bins_ref, s32[32,128]{1,0:T(8,128)S(1)} %select_add_fusion.1.gates_ref, bf16[128,32,128]{2,1,0:T(8,128)(2,1)S(1)} %form_spectrum.4.refs_0_, bf16[128,32,128]{2,1,0:T(8,128)(2,1)S(1)} %form_spectrum.5.refs_1_, ...), custom_call_target="tpu_custom_call" | custom-call | flops 268435456 | bytes 1048576 | tf_op jit(solution)/shard_map/select_gates/pallas_call | solution.py:190
  135.9 1.0 copy-done.2
  136.9 3.7 %all-to-all-start.1 = ((bf16[8,4,128,128]{3,2,1,0:T(8,128)(2,1)}), bf16[8,4,128,128]{3,2,1,0:T(8,128)(2,1)S(1)}, u32[]{:S(2)}, u32[]{:S(2)}) async-start(bf16[8,4,128,128]{3,2,1,0:T(8,128)(2,1)} %copy-done.2), calls=%async_computation.1 | async-start | bytes 2097152 | tf_op jit(solution)/shard_map/all_to_all | solution.py:534
  140.9 1.0 copy-done.10
  141.8 25.8 %factor_slots.2 = (bf16[6,96,384]{2,1,0:T(8,128)(2,1)S(1)}, bf16[6,96,384]{2,1,0:T(8,128)(2,1)S(1)}, bf16[6,96,384]{2,1,0:T(8,128)(2,1)S(1)}, bf16[6,96,384]{2,1,0:T(8,128)(2,1)S(1)}) custom-call(s32[1]{0:T(128)} %bitcast.me_ref, s32[6,192]{1,0:T(8,128)S(1)} %broadcast_select_fusion.pivots_ref, bf16[3,384,128]{2,1,0:T(8,128)(2,1)S(1)} %copy-done.10, ...), custom_call_target="tpu_custom_call" | custom-call | flops 23040000000 | bytes 1179648 | tf_op jit(solution)/shard_map/factor_slots/pallas_call | solution.py:429
  169.1 1.0 form_beams.3
  170.2 1.2 collective-permute-start.10
  171.4 1.4 collective-permute-start.11
  173.6 1.1 collective-permute-start.7
  174.9 1.0 collective-permute-start.9
  175.9 1.4 collective-permute-done.11.refs_2_
  177.4 1.5 collective-permute-done.12.refs_3_
  178.9 20.5 %factor_slots.3 = (bf16[2,96,384]{2,1,0:T(8,128)(2,1)S(1)}, bf16[2,96,384]{2,1,0:T(8,128)(2,1)S(1)}, bf16[2,96,384]{2,1,0:T(8,128)(2,1)S(1)}, bf16[2,96,384]{2,1,0:T(8,128)(2,1)S(1)}) custom-call(s32[1]{0:T(128)} %bitcast.me_ref, s32[2,192]{1,0:T(2,128)S(1)} %broadcast_select_fusion.1.pivots_ref, bf16[1,384,128]{2,1,0:T(8,128)(2,1)S(1)} %get-tuple-element.37.refs_0_, ...), custom_call_target="tpu_custom_call" | custom-call | flops 23040000000 | bytes 393216 | tf_op jit(solution)/shard_map/factor_slots/pallas_call | solution.py:429
  199.5 1.0 collective-permute-start.14
  200.4 1.1 collective-permute-done.13.refs_5_
  201.6 2.0 collective-permute-start.15
  204.9 1.5 collective-permute-done.14.refs_6_
  206.3 1.3 collective-permute-done.15.refs_7_
  207.6 3.0 %place_rows.1 = f32[32,96,384]{2,1,0:T(8,128)} custom-call(s32[2]{0:T(128)S(1)} %pad_add_fusion.place_ref, bf16[6,96,384]{2,1,0:T(8,128)(2,1)S(1)} %get-tuple-element.33.refs_0_, bf16[6,96,384]{2,1,0:T(8,128)(2,1)S(1)} %collective-permute-done.7.refs_1_, bf16[6,96,384]{2,1,0:T(8,128)(2,1)S(1)} %collective-permute-done.8.refs_2_, ...), custom_call_target="tpu_custom_call" | custom-call | tf_op jit(solution)/shard_map/place_rows/pallas_call | solution.py:464
  (116 shorter events, 15.0 us)
Async XLA Ops:
  0.0 12.5 %copy-start.16 = (s32[8]{0:T(128)S(1)}, s32[8]{0:T(128)}, u32[]{:S(2)}) copy-start(s32[8]{0:T(128)} %param.10) | copy-start | bytes 100
  0.0 13.7 %copy-start.12 = (s32[128,64]{0,1:T(8,128)S(1)}, s32[128,64]{0,1:T(8,128)}, u32[]{:S(2)}) copy-start(s32[128,64]{0,1:T(8,128)} %param.11) | copy-start | bytes 98308
  0.0 15.2 %copy-start.14 = (f32[2,64]{1,0:T(2,128)S(1)}, f32[2,64]{1,0:T(2,128)}, u32[]{:S(2)}) copy-start(f32[2,64]{1,0:T(2,128)} %param.7) | copy-start | bytes 1540
  4.2 11.4 %collective-permute-start = (bf16[2,16,64,128]{3,2,1,0:T(8,128)(2,1)S(1)}, bf16[2,16,64,128]{3,2,1,0:T(8,128)(2,1)S(1)}, u32[]{:S(2)}, u32[]{:S(2)}) collective-permute-start(bf16[2,16,64,128]{3,2,1,0:T(8,128)(2,1)S(1)} %get-tuple-element.25), channel_id=1, source_target_pairs={{1,0},{2,1},{3,2},{5,4},{6,5},{7,6},{9,8},{10,9},{11,10},{13,12},{... | collective-permute-start | bytes 1572872 | tf_op jit(solution)/shard_map/ppermute | solution.py:22
  6.1 15.0 %collective-permute-start.1 = (bf16[2,16,64,128]{3,2,1,0:T(8,128)(2,1)}, bf16[2,16,64,128]{3,2,1,0:T(8,128)(2,1)S(1)}, u32[]{:S(2)}, u32[]{:S(2)}) collective-permute-start(bf16[2,16,64,128]{3,2,1,0:T(8,128)(2,1)} %get-tuple-element.26), channel_id=1, source_target_pairs={{1,0},{2,1},{3,2},{5,4},{6,5},{7,6},{9,8},{10,9},{11,10},{13,12},{... | collective-permute-start | bytes 1572872 | tf_op jit(solution)/shard_map/ppermute | solution.py:22
  8.1 18.7 %collective-permute-start.2 = (bf16[2,16,64,128]{3,2,1,0:T(8,128)(2,1)}, bf16[2,16,64,128]{3,2,1,0:T(8,128)(2,1)S(1)}, u32[]{:S(2)}, u32[]{:S(2)}) collective-permute-start(bf16[2,16,64,128]{3,2,1,0:T(8,128)(2,1)} %get-tuple-element.27), channel_id=1, source_target_pairs={{1,0},{2,1},{3,2},{5,4},{6,5},{7,6},{9,8},{10,9},{11,10},{13,12},{... | collective-permute-start | bytes 1572872 | tf_op jit(solution)/shard_map/ppermute | solution.py:22
  10.0 22.5 %collective-permute-start.3 = (bf16[2,16,64,128]{3,2,1,0:T(8,128)(2,1)}, bf16[2,16,64,128]{3,2,1,0:T(8,128)(2,1)}, u32[]{:S(2)}, u32[]{:S(2)}) collective-permute-start(bf16[2,16,64,128]{3,2,1,0:T(8,128)(2,1)} %get-tuple-element.28), channel_id=1, source_target_pairs={{1,0},{2,1},{3,2},{5,4},{6,5},{7,6},{9,8},{10,9},{11,10},{13,12},{... | collective-permute-start | bytes 1572872 | tf_op jit(solution)/shard_map/ppermute | solution.py:22
  14.1 5.0 %copy-start.13 = (s32[128]{0:T(128)}, s32[128]{0:T(128)S(1)}, u32[]{:S(2)}) copy-start(s32[128]{0:T(128)S(1)} %add.363) | copy-start | bytes 1540
  26.8 0.8 copy-start.5
  27.6 1.0 copy-start.6
  43.6 1.0 copy-start
  44.6 7.0 %copy-start.11 = (s32[128,192]{0,1:T(8,128)S(1)}, s32[128,192]{0,1:T(8,128)}, u32[]{:S(2)}) copy-start(s32[128,192]{0,1:T(8,128)} %param.9) | copy-start | bytes 294916
  44.6 72.5 %all-to-all-start = ((bf16[8,12,128,128]{3,2,1,0:T(8,128)(2,1)}), bf16[8,12,128,128]{3,2,1,0:T(8,128)(2,1)}, u32[]{:S(2)}, u32[]{:S(2)}) async-start(bf16[8,12,128,128]{3,2,1,0:T(8,128)(2,1)} %select_gates.2), calls=%async_computation | async-start | bytes 6291456 | tf_op jit(solution)/shard_map/all_to_all | solution.py:534
  117.2 1.1 copy-start.3
  122.7 0.7 copy-start.9
  123.5 17.1 %collective-permute-start.4 = (bf16[3,384,128]{2,1,0:T(8,128)(2,1)}, bf16[3,384,128]{2,1,0:T(8,128)(2,1)S(1)}, u32[]{:S(2)}, u32[]{:S(2)}) collective-permute-start(bf16[3,384,128]{2,1,0:T(8,128)(2,1)} %get-tuple-element.30), channel_id=1, source_target_pairs={{0,1},{1,2},{2,3},{3,0},{4,5},{5,6},{6,7},{7,4},{8,9},{9,10},{10,1... | collective-permute-start | bytes 884744 | tf_op jit(solution)/shard_map/ppermute | solution.py:250
  127.9 12.9 %collective-permute-start.5 = (bf16[3,384,128]{2,1,0:T(8,128)(2,1)}, bf16[3,384,128]{2,1,0:T(8,128)(2,1)}, u32[]{:S(2)}, u32[]{:S(2)}) collective-permute-start(bf16[3,384,128]{2,1,0:T(8,128)(2,1)} %get-tuple-element.31), channel_id=1, source_target_pairs={{0,2},{1,3},{2,0},{3,1},{4,6},{5,7},{6,4},{7,5},{8,10},{9,11},{10,... | collective-permute-start | bytes 884744 | tf_op jit(solution)/shard_map/ppermute | solution.py:250
  127.9 12.9 %collective-permute-start.6 = (bf16[3,384,128]{2,1,0:T(8,128)(2,1)}, bf16[3,384,128]{2,1,0:T(8,128)(2,1)}, u32[]{:S(2)}, u32[]{:S(2)}) collective-permute-start(bf16[3,384,128]{2,1,0:T(8,128)(2,1)} %get-tuple-element.32), channel_id=1, source_target_pairs={{0,3},{1,0},{2,1},{3,2},{4,7},{5,4},{6,5},{7,6},{8,11},{9,8},{10,9... | collective-permute-start | bytes 884744 | tf_op jit(solution)/shard_map/ppermute | solution.py:250
  132.4 1.2 copy-start.1
  135.9 1.0 copy-start.2
  136.9 32.3 %all-to-all-start.1 = ((bf16[8,4,128,128]{3,2,1,0:T(8,128)(2,1)}), bf16[8,4,128,128]{3,2,1,0:T(8,128)(2,1)S(1)}, u32[]{:S(2)}, u32[]{:S(2)}) async-start(bf16[8,4,128,128]{3,2,1,0:T(8,128)(2,1)} %copy-done.2), calls=%async_computation.1 | async-start | bytes 2097152 | tf_op jit(solution)/shard_map/all_to_all | solution.py:534
  140.9 1.0 copy-start.10
  141.8 27.3 %copy-start.4 = (bf16[8,4,2,16,384]{4,3,2,1,0:T(8,128)(2,1)S(1)}, bf16[8,4,2,16,384]{4,3,2,1,0:T(8,128)(2,1)}, u32[]{:S(2)}) copy-start(bf16[8,4,2,16,384]{4,3,2,1,0:T(8,128)(2,1)} %copy.33) | copy-start | bytes 2359300
  141.8 31.7 %copy-start.15 = (pred[2]{0:T(512)(128)(4,1)S(1)}, pred[2]{0:T(512)(128)(4,1)}, u32[]{:S(2)}) copy-start(pred[2]{0:T(512)(128)(4,1)} %compare_and_fusion.1) | copy-start | bytes 10
  167.6 0.8 copy-start.7
  168.4 0.8 copy-start.8
  170.2 4.7 %collective-permute-start.10 = (bf16[1,384,128]{2,1,0:T(8,128)(2,1)S(1)}, bf16[1,384,128]{2,1,0:T(8,128)(2,1)S(1)}, u32[]{:S(2)}, u32[]{:S(2)}) collective-permute-start(bf16[1,384,128]{2,1,0:T(8,128)(2,1)S(1)} %get-tuple-element.38), channel_id=1, source_target_pairs={{0,1},{1,2},{2,3},{3,0},{4,5},{5,6},{6,7},{7,4},{8,9},{9,10},{10,1... | collective-permute-start | bytes 294920 | tf_op jit(solution)/shard_map/ppermute | solution.py:250
  171.4 6.0 %collective-permute-start.11 = (bf16[1,384,128]{2,1,0:T(8,128)(2,1)S(1)}, bf16[1,384,128]{2,1,0:T(8,128)(2,1)S(1)}, u32[]{:S(2)}, u32[]{:S(2)}) collective-permute-start(bf16[1,384,128]{2,1,0:T(8,128)(2,1)S(1)} %get-tuple-element.39), channel_id=1, source_target_pairs={{0,2},{1,3},{2,0},{3,1},{4,6},{5,7},{6,4},{7,5},{8,10},{9,11},{10,... | collective-permute-start | bytes 294920 | tf_op jit(solution)/shard_map/ppermute | solution.py:250
  172.8 6.1 %collective-permute-start.12 = (bf16[1,384,128]{2,1,0:T(8,128)(2,1)S(1)}, bf16[1,384,128]{2,1,0:T(8,128)(2,1)S(1)}, u32[]{:S(2)}, u32[]{:S(2)}) collective-permute-start(bf16[1,384,128]{2,1,0:T(8,128)(2,1)S(1)} %get-tuple-element.40), channel_id=1, source_target_pairs={{0,3},{1,0},{2,1},{3,2},{4,7},{5,4},{6,5},{7,6},{8,11},{9,8},{10,9... | collective-permute-start | bytes 294920 | tf_op jit(solution)/shard_map/ppermute | solution.py:250
  173.6 34.1 %collective-permute-start.7 = (bf16[6,96,384]{2,1,0:T(8,128)(2,1)}, bf16[6,96,384]{2,1,0:T(8,128)(2,1)S(1)}, u32[]{:S(2)}, u32[]{:S(2)}) collective-permute-start(bf16[6,96,384]{2,1,0:T(8,128)(2,1)} %copy-done.8), channel_id=1, source_target_pairs={{0,1},{1,2},{2,3},{3,0},{4,5},{5,6},{6,7},{7,4},{8,9},{9,10},{10,1... | collective-permute-start | bytes 1327112 | tf_op jit(solution)/shard_map/ppermute | solution.py:250
  174.6 33.0 %collective-permute-start.8 = (bf16[6,96,384]{2,1,0:T(8,128)(2,1)}, bf16[6,96,384]{2,1,0:T(8,128)(2,1)S(1)}, u32[]{:S(2)}, u32[]{:S(2)}) collective-permute-start(bf16[6,96,384]{2,1,0:T(8,128)(2,1)} %copy-done.7), channel_id=1, source_target_pairs={{0,2},{1,3},{2,0},{3,1},{4,6},{5,7},{6,4},{7,5},{8,10},{9,11},{10,... | collective-permute-start | bytes 1327112 | tf_op jit(solution)/shard_map/ppermute | solution.py:250
  174.9 32.7 %collective-permute-start.9 = (bf16[6,96,384]{2,1,0:T(8,128)(2,1)S(1)}, bf16[6,96,384]{2,1,0:T(8,128)(2,1)S(1)}, u32[]{:S(2)}, u32[]{:S(2)}) collective-permute-start(bf16[6,96,384]{2,1,0:T(8,128)(2,1)S(1)} %get-tuple-element.36), channel_id=1, source_target_pairs={{0,3},{1,0},{2,1},{3,2},{4,7},{5,4},{6,5},{7,6},{8,11},{9,8},{10,9... | collective-permute-start | bytes 1327112 | tf_op jit(solution)/shard_map/ppermute | solution.py:250
  178.9 24.7 %copy-start.17 = (s32[8]{0:T(128)S(1)}, s32[8]{0:T(128)}, u32[]{:S(2)}) copy-start(s32[8]{0:T(128)} %param.10) | copy-start | bytes 100
  199.4 2.2 %collective-permute-start.13 = (bf16[2,96,384]{2,1,0:T(8,128)(2,1)S(1)}, bf16[2,96,384]{2,1,0:T(8,128)(2,1)S(1)}, u32[]{:S(2)}, u32[]{:S(2)}) collective-permute-start(bf16[2,96,384]{2,1,0:T(8,128)(2,1)S(1)} %get-tuple-element.42), channel_id=1, source_target_pairs={{0,1},{1,2},{2,3},{3,0},{4,5},{5,6},{6,7},{7,4},{8,9},{9,10},{10,1... | collective-permute-start | bytes 442376 | tf_op jit(solution)/shard_map/ppermute | solution.py:250
  199.5 6.9 %collective-permute-start.14 = (bf16[2,96,384]{2,1,0:T(8,128)(2,1)S(1)}, bf16[2,96,384]{2,1,0:T(8,128)(2,1)S(1)}, u32[]{:S(2)}, u32[]{:S(2)}) collective-permute-start(bf16[2,96,384]{2,1,0:T(8,128)(2,1)S(1)} %get-tuple-element.43), channel_id=1, source_target_pairs={{0,2},{1,3},{2,0},{3,1},{4,6},{5,7},{6,4},{7,5},{8,10},{9,11},{10,... | collective-permute-start | bytes 442376 | tf_op jit(solution)/shard_map/ppermute | solution.py:250
  201.6 6.1 %collective-permute-start.15 = (bf16[2,96,384]{2,1,0:T(8,128)(2,1)S(1)}, bf16[2,96,384]{2,1,0:T(8,128)(2,1)S(1)}, u32[]{:S(2)}, u32[]{:S(2)}) collective-permute-start(bf16[2,96,384]{2,1,0:T(8,128)(2,1)S(1)} %get-tuple-element.44), channel_id=1, source_target_pairs={{0,3},{1,0},{2,1},{3,2},{4,7},{5,4},{6,5},{7,6},{8,11},{9,8},{10,9... | collective-permute-start | bytes 442376 | tf_op jit(solution)/shard_map/ppermute | solution.py:250
